TPU v7x, 32 devices: a whole 2x2x4 slice. The times are simulated.
32 devices in a mesh: gx: 2 (over x), gy: 4 (over y, core), ga: 4 (over z).
Axes of the slice: x: 2, y: 2, z: 4, core: 2. Of those that a mesh axis runs over, the one named last changes fastest.
Arguments:
- density: float32 [64, 768, 768], P('ga', ('gx', 'gy')), may hold values from 0.5 to 1.5
- tensor: bfloat16 [6, 64, 768, 768], P(None, 'ga', ('gx', 'gy')), may hold values from -0.29882812 to 0.29882812
- grad_u: bfloat16 [3, 64, 768, 768], P(None, 'ga', ('gx', 'gy')), may hold values from -0.099609375 to 0.099609375
- plane_rate: float32 [64], P('ga'), may hold values from 2 to 800
- cotangent: float32 [64, 768, 768], P('ga', ('gx', 'gy')), may hold values from -6 to 6
Outputs:
- new_density: float32 [64, 768, 768], P('ga', ('gx', 'gy'))
- adjoint_density: float32 [64, 768, 768], P('ga', ('gx', 'gy'))
All inputs are finite; a program needn't handle non-finite values.
Results may differ from a plain program's by a relative error of at most 0.0003.
Values sent between devices are 32-bit elements; how exact they have to be, the bound alone decides.
A program may use at most 256 MiB of HBM per device.

v0:
```python
import jax
import jax.numpy as jnp
from jax import lax
from jax.sharding import PartitionSpec as P

ENTRY = ((0, 3, 4), (3, 1, 5), (4, 5, 2))


def with_halo(block, sides, width):
    for axis, dim in sides:
        count = lax.axis_size(axis)
        forward = [(i, i + 1) for i in range(count - 1)]
        forward.append((count - 1, 0))
        backward = [(target, source) for source, target in forward]
        low = lax.ppermute(
            lax.slice_in_dim(block, block.shape[dim] - width, None, axis=dim), axis, forward
        )
        high = lax.ppermute(lax.slice_in_dim(block, 0, width, axis=dim), axis, backward)
        block = jnp.concatenate([low, block, high], axis=dim)
    return block


def central_last(field):
    return 0.5 * (jnp.roll(field, -1, 2) - jnp.roll(field, 1, 2))


def second_last(field):
    return jnp.roll(field, -1, 2) + jnp.roll(field, 1, 2) - 2.0 * field


def second_across(rimmed_block, member):
    return (
        rimmed_block[member, 1:-1, 2:]
        + rimmed_block[member, 1:-1, :-2]
        - 2.0 * rimmed_block[member, 1:-1, 1:-1]
    )


def hartley_matrix(points):
    counter = lax.iota(jnp.int32, points)
    product = counter[:, None] * counter[None, :] % points
    angles = 2.0 * jnp.pi / points * product.astype(jnp.float32)
    return (jnp.cos(angles) + jnp.sin(angles)) / jnp.sqrt(jnp.float32(points))


def solve_last(field, hartley_table, eigen):
    spectrum = (
        jnp.einsum("prn,nk->prk", field, hartley_table, precision=lax.Precision.HIGHEST)
        / eigen[:, None, :]
    )
    return jnp.einsum("prk,kn->prn", spectrum, hartley_table, precision=lax.Precision.HIGHEST)


def solve_swapped(field, hartley_table, eigen):
    spectrum = (
        jnp.einsum("prn,nk->prk", field, hartley_table, precision=lax.Precision.HIGHEST)
        / eigen[:, None, :]
    )
    return jnp.einsum("prk,kn->pnr", spectrum, hartley_table, precision=lax.Precision.HIGHEST)


def rimmed(stacked):
    return with_halo(stacked, ((("gx", "gy"), 2), ("ga", 1)), 1)


def gradients(rimmed_block, member, centre):
    grad_x = central_last(centre)
    grad_y = 0.5 * (rimmed_block[member, 1:-1, 2:] - rimmed_block[member, 1:-1, :-2])
    grad_z = 0.5 * (rimmed_block[member, 2:, 1:-1] - rimmed_block[member, :-2, 1:-1])
    return [grad_x, grad_y, grad_z]


def apply_tensor(tensor, rate_root, vectors):
    scales = (rate_root, rate_root, 1.0)
    results = []
    for target in range(3):
        total = jnp.zeros_like(vectors[0])
        for source in range(3):
            entry = tensor[ENTRY[target][source]].astype(jnp.float32)
            if target == source:
                entry = entry + 1.0
            total = total + scales[target] * scales[source] * entry * vectors[source]
        results.append(total)
    return results


def divergence(fluxes):
    rim_flux = with_halo(jnp.stack([fluxes[1], fluxes[2]]), ((("gx", "gy"), 2), ("ga", 1)), 1)
    across = 0.5 * (rim_flux[0, 1:-1, 2:] - rim_flux[0, 1:-1, :-2])
    planar = 0.5 * (rim_flux[1, 2:, 1:-1] - rim_flux[1, :-2, 1:-1])
    return central_last(fluxes[0]) + across + planar


def to_lines(block):
    return lax.all_to_all(block, ("gx", "gy"), split_axis=1, concat_axis=2, tiled=True)


def local(density, tensor, grad_u, plane_rate, cotangent):
    points = density.shape[2]
    hartley_table = hartley_matrix(points)
    modes = lax.iota(jnp.int32, points).astype(jnp.float32)
    eigen = (
        1.0 + 2.0 * plane_rate[:, None] * (1.0 - jnp.cos(2.0 * jnp.pi / points * modes))[None, :]
    )
    weight = plane_rate[:, None, None]
    rate_root = jnp.sqrt(weight)
    drift = [grad_u[member].astype(jnp.float32) for member in range(3)]
    rim_one = rimmed(density[None])
    grads = gradients(rim_one, 0, density)
    pushed = [grads[source] + drift[source] * density for source in range(3)]
    change = divergence(apply_tensor(tensor, rate_root, pushed))
    first = solve_swapped(density + change - weight * second_last(density), hartley_table, eigen)
    across = jnp.swapaxes(second_across(rim_one, 0), 1, 2)
    moved = to_lines(first - weight * across)
    new_density = solve_last(moved, hartley_table, eigen)
    swept = solve_swapped(cotangent, hartley_table, eigen)
    returned = to_lines(swept)
    settled = solve_last(returned, hartley_table, eigen)
    rim_two = rimmed(jnp.stack([settled, returned]))
    grads_two = gradients(rim_two, 0, settled)
    pulled = [-term for term in apply_tensor(tensor, rate_root, grads_two)]
    back = -divergence(pulled)
    for target in range(3):
        back = back + drift[target] * pulled[target]
    adjoint_density = (
        settled + back - weight * second_last(settled) - weight * second_across(rim_two, 1)
    )
    return (new_density, adjoint_density)


def solution(mesh):
    placed = (
        P("ga", ("gx", "gy"), None),
        P(None, "ga", ("gx", "gy"), None),
        P(None, "ga", ("gx", "gy"), None),
        P("ga"),
        P("ga", ("gx", "gy"), None),
    )
    return jax.shard_map(
        local,
        mesh=mesh,
        in_specs=placed,
        out_specs=(P("ga", ("gx", "gy"), None), P("ga", ("gx", "gy"), None)),
        check_vma=False,
    )
```

profile of v0, /device:TPU:0, one launch (start us, length us, event | category | flops | bytes accessed | tf_op | source)
XLA Modules:
  0.0 540.6 jit_solution(222201697094236008)
XLA Ops:
  0.6 1.2 fusion.177
  1.8 3.4 collective-permute-start
  5.3 0.7 broadcast_multiply_fusion
  5.9 27.0 %fusion.109 = f32[768,16,96]{0,2,1:T(8,128)S(1)} fusion(f32[16,96,768]{2,1,0:T(8,128)} %param.9), kind=kOutput, calls=%fused_computation.185 | convolution fusion | flops 10878124032 | bytes 9437184 | tf_op jit(solution)/shard_map/prn,nk->prk/dot_general | solution.py:56
  33.0 22.7 %fusion.126 = f32[16,768,96]{1,2,0:T(8,128)} fusion(f32[768,16,96]{0,2,1:T(8,128)S(1)} %fusion.109, f32[16,768]{1,0:T(8,128)S(1)} %multiply_add_fusion), kind=kOutput, calls=%fused_computation.204 | convolution fusion | flops 10879303680 | bytes 9486336 | tf_op jit(solution)/shard_map/prk,kn->pnr/dot_general | solution.py:59
  55.6 6.3 %copy.22 = f32[16,768,96]{2,0,1:T(8,128)} copy(f32[16,768,96]{1,2,0:T(8,128)} %fusion.126) | data formatting | bytes 9437184 | tf_op jit(solution)/shard_map/prk,kn->pnr/transpose | solution.py:59
  62.0 4.8 all-to-all-start.1
  66.8 1.1 pad_maximum_fusion.74
  67.9 3.7 collective-permute-start.2
  71.5 9.0 %fusion.175 = (f32[16,96,767]{2,1,0:T(8,128)}, f32[16,96,767]{2,1,0:T(8,128)}) fusion(f32[16,96,768]{2,1,0:T(8,128)} %param.5), kind=kLoop, calls=%fused_computation.273 | loop fusion | bytes 18849792 | tf_op jit(solution)/shard_map/jit(_roll_static)/slice | solution.py:24
  80.9 5.7 %collective-permute-done.3 = f32[1,1,98,768]{3,2,1,0:T(8,128)S(1)} collective-permute-done((f32[1,1,98,768]{3,2,1,0:T(8,128)S(1)}, f32[1,1,98,768]{3,2,1,0:T(8,128)S(1)}, u32[]{:S(2)}, u32[]{:S(2)}) %collective-permute-start.3) | collective-permute-done | bytes 301088 | tf_op jit(solution)/shard_map/ppermute | solution.py:15
  86.6 0.7 copy-done.18
  87.3 21.4 %fusion.13 = (f32[16,96,768]{2,1,0:T(8,128)}, f32[16,96,768]{2,1,0:T(8,128)}, f32[16,96,768]{2,1,0:T(8,128)}, f32[16,96,768]{2,1,0:T(8,128)}) fusion(f32[16]{0:T(128)S(1)} %get-tuple-element.46, f32[16]{0:T(128)S(1)} %get-tuple-element.45, bf16[6,16,96,768]{3,2,1,0:T(8,128)(2,1)} %param.6, f32[16,96,768]{2,1,0:T(8,128)S(1)} %bitcast.294, ...), kind=kLoop, calls=%fused_computation.27 | loop fusion | flops 43646976 | bytes 52605056 | tf_op jit(solution)/shard_map/add | solution.py:82
  108.8 9.3 %fusion.16 = (f32[1,16,96,768]{3,2,1,0:T(8,128)}, f32[1,16,96,768]{3,2,1,0:T(8,128)}) fusion(f32[16,96,768]{2,1,0:T(8,128)} %get-tuple-element.5, f32[16,96,768]{2,1,0:T(8,128)} %get-tuple-element.3, f32[16,96,768]{2,1,0:T(8,128)} %get-tuple-element.4, f32[16]{0:T(128)S(1)} %get-tuple-element.46, f32[16]{0:T(128)S(1)} %get-tuple-element.45, ...), kind=kLoop, calls=%fused_computation.30 | loop fusion | flops 24772608 | bytes 35389568 | tf_op jit(solution)/shard_map/stack | solution.py:88
  118.1 1.6 pad_maximum_fusion.79
  119.7 1.6 collective-permute-start.4
  121.3 15.0 %collective-permute-done.4 = f32[2,16,1,768]{3,2,1,0:T(1,128)S(1)} collective-permute-done((f32[2,16,1,768]{3,2,1,0:T(1,128)S(1)}, f32[2,16,1,768]{3,2,1,0:T(1,128)S(1)}, u32[]{:S(2)}, u32[]{:S(2)}) %collective-permute-start.4) | collective-permute-done | bytes 98336 | tf_op jit(solution)/shard_map/ppermute | solution.py:18
  136.3 3.1 collective-permute-done.5
  139.5 1.1 copy.16
  140.6 3.6 collective-permute-start.6
  144.2 1.1 copy.18
  145.3 1.5 fusion.173
  146.8 5.2 fusion.174
  152.0 6.5 %collective-permute-done.6 = f32[2,1,98,768]{3,0,2,1:T(2,128)} collective-permute-done((f32[2,1,98,768]{3,0,2,1:T(2,128)}, f32[2,1,98,768]{3,0,2,1:T(2,128)}, u32[]{:S(2)}, u32[]{:S(2)}) %collective-permute-start.6) | collective-permute-done | bytes 602144 | tf_op jit(solution)/shard_map/ppermute | solution.py:18
  158.5 1.9 copy.17
  160.5 10.9 %collective-permute-done.7 = f32[2,1,98,768]{3,0,2,1:T(2,128)} collective-permute-done((f32[2,1,98,768]{3,0,2,1:T(2,128)}, f32[2,1,98,768]{3,0,2,1:T(2,128)}, u32[]{:S(2)}, u32[]{:S(2)}) %collective-permute-start.7) | collective-permute-done | bytes 602144 | tf_op jit(solution)/shard_map/ppermute | solution.py:15
  171.4 1.9 copy.19
  173.3 14.8 %fusion.193 = f32[16,96,768]{2,1,0:T(8,128)S(1)} fusion(f32[16,96,768]{2,1,0:T(8,128)S(1)} %bitcast.294, f32[2,1,98,768]{3,2,1,0:T(8,128)} %copy.19, f32[2,16,1,768]{3,2,1,0:T(1,128)S(1)} %collective-permute-done.4, f32[2,16,1,768]{3,2,1,0:T(1,128)S(1)} %collective-permute-done.5, f32[1,16,96,768]{3,2,1,0:T(8,128)S(1)} %copy-done.2, ...), kind=kLoop, calls=%fused_computation.111.clone.clone.2 | loop fusion | flops 33030144 | bytes 39149632 | tf_op jit(solution)/shard_map/prn,nk->prk/dot_general | solution.py:56
  188.1 25.6 %fusion.72 = f32[16,96,768]{2,1,0:T(8,128)S(1)} fusion(f32[16,96,768]{2,1,0:T(8,128)S(1)} %fusion.193), kind=kOutput, calls=%fused_computation.112 | convolution fusion | flops 10878124032 | bytes 9437184 | tf_op jit(solution)/shard_map/prn,nk->prk/dot_general | solution.py:56
  213.6 2.6 fusion.195
  216.3 9.0 %copy.36 = f32[16,8,96,96]{3,1,2,0:T(8,128)} copy(f32[16,8,96,96]{3,0,2,1:T(8,128)} %bitcast.24) | data formatting | bytes 9437184 | tf_op jit(solution)/shard_map/all_to_all | solution.py:95
  225.3 7.4 %all_to_all.33 = f32[16,96,768]{2,1,0:T(8,128)} reshape(f32[16,96,8,96]{3,2,1,0:T(8,128)} %bitcast.303) | data formatting | bytes 9437184 | tf_op jit(solution)/shard_map/all_to_all | solution.py:95
  232.7 7.4 %stack.27 = f32[1,16,96,768]{3,2,1,0:T(8,128)} reshape(f32[16,96,8,96]{3,2,1,0:T(8,128)} %bitcast.304) | data formatting | bytes 9437184 | tf_op jit(solution)/shard_map/stack | solution.py:119
  240.1 27.3 %fusion.106 = f32[16,96,768]{2,1,0:T(8,128)S(1)} fusion(f32[16,96,768]{2,1,0:T(8,128)} %all_to_all.33), kind=kOutput, calls=%fused_computation.182 | convolution fusion | flops 10878124032 | bytes 9437184 | tf_op jit(solution)/shard_map/prn,nk->prk/dot_general | solution.py:48
  267.4 27.0 %fusion.93 = f32[16,96,768]{2,1,0:T(8,128)S(1)} fusion(f32[16,96,768]{2,1,0:T(8,128)S(1)} %fusion.106, f32[16,768]{1,0:T(8,128)S(1)} %multiply_add_fusion), kind=kOutput, calls=%fused_computation.166 | convolution fusion | flops 10879303680 | bytes 9486336 | tf_op jit(solution)/shard_map/prk,kn->prn/dot_general | solution.py:51
  294.7 2.0 copy-done
  297.2 23.5 %bitcast_subtract_fusion = f32[16,768,96]{1,2,0:T(8,128)} fusion(f32[16,96,768]{2,1,0:T(8,128)S(1)} %bitcast.297, f32[1,16,1,768]{3,2,1,0:T(1,128)S(1)} %collective-permute-done, f32[1,16,96,768]{3,2,1,0:T(8,128)S(1)} %bitcast.298, f32[1,16,1,768]{3,2,1,0:T(1,128)S(1)} %collective-permute-done.1, f32[16]{0:T(128)S(1)} %copy-done.19, ...), kind=kOutput, calls=%fused_computation.159 | convolution fusion | flops 10886381568 | bytes 18972736 | tf_op jit(solution)/shard_map/prk,kn->pnr/dot_general | solution.py:59
  320.7 6.2 %copy.20 = f32[16,768,96]{2,0,1:T(8,128)} copy(f32[16,768,96]{1,2,0:T(8,128)} %bitcast_subtract_fusion) | data formatting | bytes 9437184 | tf_op jit(solution)/shard_map/sub | solution.py:114
  327.0 4.7 all-to-all-start
  331.8 1.4 pad_maximum_fusion.67
  333.5 2.9 collective-permute-start.10
  336.4 1.2 copy.26
  337.6 3.0 slice_bitcast_fusion.1
  340.6 12.7 %slice_bitcast_fusion.3 = (f32[1,16,96,767]{3,2,1,0:T(8,128)}, f32[1,16,96,767]{3,2,1,0:T(8,128)}, f32[16,96,767]{2,1,0:T(8,128)}, f32[16,96,767]{2,1,0:T(8,128)}) fusion(f32[16,96,768]{2,1,0:T(8,128)} %copy-done), kind=kLoop, calls=%fused_computation.268 | loop fusion | bytes 28274688 | tf_op jit(solution)/shard_map/jit(_roll_static)/concatenate | solution.py:24
  353.4 10.6 %collective-permute-done.11 = f32[2,1,98,768]{3,0,2,1:T(2,128)} collective-permute-done((f32[2,1,98,768]{3,0,2,1:T(2,128)}, f32[2,1,98,768]{3,0,2,1:T(2,128)}, u32[]{:S(2)}, u32[]{:S(2)}) %collective-permute-start.11) | collective-permute-done | bytes 602144 | tf_op jit(solution)/shard_map/ppermute | solution.py:15
  364.0 1.1 copy.27
  365.1 0.8 copy-done.6
  365.9 18.0 %fusion.3 = f32[1,16,96,768]{3,2,1,0:T(8,128)} fusion(f32[16]{0:T(128)S(1)} %get-tuple-element.46, f32[16]{0:T(128)S(1)} %get-tuple-element.45, bf16[6,16,96,768]{3,2,1,0:T(8,128)(2,1)} %param.6, f32[1,16,96,767]{3,2,1,0:T(8,128)} %get-tuple-element.27, f32[1,16,96,1]{3,2,1,0:T(8,128)S(1)} %get-tuple-element.31, f32[1,16,96,1]{3,2,1,0:T(8,128)S(1)} %get-tuple-element.30, ...), kind=kLoop, calls=%fused_computation.17 | loop fusion | flops 38928384 | bytes 32071808 | tf_op jit(solution)/shard_map/neg | solution.py:121
  384.0 14.9 %fusion.6 = f32[1,16,96,768]{3,2,1,0:T(8,128)} fusion(f32[16]{0:T(128)S(1)} %get-tuple-element.46, bf16[6,16,96,768]{3,2,1,0:T(8,128)(2,1)} %param.6, f32[1,16,96,767]{3,2,1,0:T(8,128)} %get-tuple-element.27, f32[1,16,96,1]{3,2,1,0:T(8,128)} %copy-done.13, f32[1,16,96,1]{3,2,1,0:T(8,128)} %copy-done.12, f32[1,16,96,767]{3,2,1,0:T(8,128)} %get-tuple-element.26, ...), kind=kLoop, calls=%fused_computation.20 | loop fusion | flops 37748736 | bytes 32071744 | tf_op jit(solution)/shard_map/neg | solution.py:121
  398.9 2.1 pad_maximum_fusion.75
  401.0 1.3 collective-permute-start.12
  402.3 10.5 %fusion.19 = f32[16,96,768]{2,1,0:T(8,128)} fusion(f32[16,96,767]{2,1,0:T(8,128)} %get-tuple-element.28, f32[16,96,1]{2,1,0:T(8,128)} %get-tuple-element.32, f32[16,96,1]{2,1,0:T(8,128)} %get-tuple-element.33, f32[16,96,767]{2,1,0:T(8,128)} %get-tuple-element.29, f32[16]{0:T(128)S(1)} %get-tuple-element.46, f32[16]{0:T(128)S(1)} %get-tuple-element.45, ...), kind=kLoop, calls=%fused_computation.33 | loop fusion | flops 38928384 | bytes 32071808 | tf_op jit(solution)/shard_map/neg | solution.py:121
  412.8 8.8 %fusion.172 = (f32[16,96,767]{2,1,0:T(8,128)}, f32[16,96,767]{2,1,0:T(8,128)}) fusion(f32[16,96,768]{2,1,0:T(8,128)} %fusion.19), kind=kLoop, calls=%fused_computation.270 | loop fusion | bytes 18849792 | tf_op jit(solution)/shard_map/jit(_roll_static)/slice | solution.py:24
  421.6 2.8 fusion.171
  424.4 1.3 pad_maximum_fusion.63
  426.0 3.6 collective-permute-start.14
  429.6 1.1 copy.32
  430.9 9.2 %copy.37 = f32[16,8,96,96]{3,1,2,0:T(8,128)} copy(f32[16,8,96,96]{3,0,2,1:T(8,128)} %bitcast.20) | data formatting | bytes 9437184 | tf_op jit(solution)/shard_map/all_to_all | solution.py:95
  440.1 7.4 %all_to_all.29 = f32[16,96,768]{2,1,0:T(8,128)} reshape(f32[16,96,8,96]{3,2,1,0:T(8,128)} %bitcast.307) | data formatting | bytes 9437184 | tf_op jit(solution)/shard_map/all_to_all | solution.py:95
  447.4 27.4 %fusion.112 = f32[16,96,768]{2,1,0:T(8,128)S(1)} fusion(f32[16,96,768]{2,1,0:T(8,128)} %all_to_all.29), kind=kOutput, calls=%fused_computation.188 | convolution fusion | flops 10878124032 | bytes 9437184 | tf_op jit(solution)/shard_map/prn,nk->prk/dot_general | solution.py:48
  474.9 22.9 %fusion.95 = f32[16,96,768]{2,1,0:T(8,128)} fusion(f32[16,96,768]{2,1,0:T(8,128)S(1)} %fusion.112, f32[16,768]{1,0:T(8,128)S(1)} %multiply_add_fusion), kind=kOutput, calls=%fused_computation.168 | convolution fusion | flops 10879303680 | bytes 9486336 | tf_op jit(solution)/shard_map/prk,kn->prn/dot_general | solution.py:51
  497.7 1.1 copy.31
  498.9 1.9 copy.33
  500.8 39.5 %fusion.48 = f32[16,96,768]{2,1,0:T(8,128)} fusion(f32[16,96,768]{2,1,0:T(8,128)} %copy-done, f32[16,96,768]{2,1,0:T(8,128)} %fusion.19, f32[2,16,1,768]{3,2,1,0:T(1,128)} %copy-done.15, f32[1,16,96,768]{3,2,1,0:T(8,128)} %stack.27, f32[1,16,96,768]{3,2,1,0:T(8,128)} %bitcast.282, f32[2,16,1,768]{3,2,1,0:T(1,128)} %copy-done.14, f32[2,1,98,768]{3,2,1,0:T(8,128)} %copy.33, ...), kind=kLoop, calls=%fused_computation.62 | loop fusion | flops 103809024 | bytes 78299328 | tf_op jit(solution)/shard_map/sub | solution.py:126
  (119 shorter events, 2.2 us)
Async XLA Ops:
  1.8 64.9 %collective-permute-start = (f32[1,16,1,768]{3,2,1,0:T(1,128)S(1)}, f32[1,16,1,768]{3,2,1,0:T(1,128)S(1)}, u32[]{:S(2)}, u32[]{:S(2)}) collective-permute-start(f32[1,16,1,768]{3,2,1,0:T(1,128)S(1)} %get-tuple-element.43), channel_id=1, source_target_pairs={{4,0},{8,4},{12,8},{16,12},{20,16},{24,20},{28,24},{0,28},{5,1},{9... | collective-permute-start | bytes 147464 | tf_op jit(solution)/shard_map/ppermute | solution.py:18
  5.2 61.5 %collective-permute-start.1 = (f32[1,16,1,768]{3,2,1,0:T(1,128)S(1)}, f32[1,16,1,768]{3,2,1,0:T(1,128)S(1)}, u32[]{:S(2)}, u32[]{:S(2)}) collective-permute-start(f32[1,16,1,768]{3,2,1,0:T(1,128)S(1)} %get-tuple-element.42), channel_id=1, source_target_pairs={{0,4},{4,8},{8,12},{12,16},{16,20},{20,24},{24,28},{28,0},{1,5},{5... | collective-permute-start | bytes 147464 | tf_op jit(solution)/shard_map/ppermute | solution.py:15
  62.0 154.3 %all-to-all-start.1 = ((f32[16,768,96]{2,0,1:T(8,128)}), f32[16,768,96]{2,0,1:T(8,128)}, u32[]{:S(2)}, u32[]{:S(2)}) async-start(f32[16,768,96]{2,0,1:T(8,128)} %copy.22), calls=%async_computation.1 | async-start | bytes 12582912 | tf_op jit(solution)/shard_map/all_to_all | solution.py:95
  67.9 13.0 %collective-permute-start.2 = (f32[1,1,98,768]{3,2,1,0:T(8,128)S(1)}, f32[1,1,98,768]{3,2,1,0:T(8,128)S(1)}, u32[]{:S(2)}, u32[]{:S(2)}) collective-permute-start(f32[1,1,98,768]{3,2,1,0:T(8,128)S(1)} %get-tuple-element.20), channel_id=1, source_target_pairs={{1,0},{2,1},{3,2},{0,3},{5,4},{6,5},{7,6},{4,7},{9,8},{10,9},{11,1... | collective-permute-start | bytes 903176 | tf_op jit(solution)/shard_map/ppermute | solution.py:18
  71.5 9.0 %slice-start.6 = ((s8[4718592]{0:T(1024)(128)(4,1)}), s8[4194304]{0:T(1024)(128)(4,1)S(1)}, s32[]{:S(2)}) async-start(s8[4718592]{0:T(1024)(128)(4,1)} %bitcast.293), calls=%async_computation.8 | async-start | bytes 8388608
  71.5 9.0 %slice-start.7 = ((s8[4718592]{0:T(1024)(128)(4,1)}), s8[524288]{0:T(1024)(128)(4,1)S(1)}, s32[]{:S(2)}) async-start(s8[4718592]{0:T(1024)(128)(4,1)} %bitcast.293), calls=%async_computation.9 | async-start | bytes 1048576
  71.5 15.1 %collective-permute-start.3 = (f32[1,1,98,768]{3,2,1,0:T(8,128)S(1)}, f32[1,1,98,768]{3,2,1,0:T(8,128)S(1)}, u32[]{:S(2)}, u32[]{:S(2)}) collective-permute-start(f32[1,1,98,768]{3,2,1,0:T(8,128)S(1)} %get-tuple-element.21), channel_id=1, source_target_pairs={{0,1},{1,2},{2,3},{3,0},{4,5},{5,6},{6,7},{7,4},{8,9},{9,10},{10,1... | collective-permute-start | bytes 903176 | tf_op jit(solution)/shard_map/ppermute | solution.py:15
  80.8 27.9 %copy-start.10 = (f32[16,96,1]{2,1,0:T(8,128)}, f32[16,96,1]{2,1,0:T(8,128)S(1)}, u32[]{:S(2)}) copy-start(f32[16,96,1]{2,1,0:T(8,128)S(1)} %get-tuple-element.40) | copy-start | bytes 18436
  80.8 27.8 %copy-start.11 = (f32[16,96,1]{2,1,0:T(8,128)}, f32[16,96,1]{2,1,0:T(8,128)S(1)}, u32[]{:S(2)}) copy-start(f32[16,96,1]{2,1,0:T(8,128)S(1)} %get-tuple-element.41) | copy-start | bytes 18436
  86.6 0.7 copy-start.18
  87.3 21.4 %slice-start.10 = ((s8[14155776]{0:T(1024)(128)(4,1)}), s8[4194304]{0:T(1024)(128)(4,1)S(1)}, s32[]{:S(2)}) async-start(s8[14155776]{0:T(1024)(128)(4,1)} %bitcast.299), calls=%async_computation.12 | async-start | bytes 8388608
  87.3 21.4 %slice-start.11 = ((s8[14155776]{0:T(1024)(128)(4,1)}), s8[4194304]{0:T(1024)(128)(4,1)S(1)}, s32[]{:S(2)}) async-start(s8[14155776]{0:T(1024)(128)(4,1)} %bitcast.299), calls=%async_computation.13 | async-start | bytes 8388608
  87.3 21.4 %slice-start.12 = ((s8[14155776]{0:T(1024)(128)(4,1)}), s8[4194304]{0:T(1024)(128)(4,1)S(1)}, s32[]{:S(2)}) async-start(s8[14155776]{0:T(1024)(128)(4,1)} %bitcast.299), calls=%async_computation.14 | async-start | bytes 8388608
  87.3 21.4 %slice-start.13 = ((s8[14155776]{0:T(1024)(128)(4,1)}), s8[1572864]{0:T(1024)(128)(4,1)S(1)}, s32[]{:S(2)}) async-start(s8[14155776]{0:T(1024)(128)(4,1)} %bitcast.299), calls=%async_computation.15 | async-start | bytes 3145728
  118.0 21.3 %copy-start.1 = (f32[1,16,96,768]{3,2,1,0:T(8,128)S(1)}, f32[1,16,96,768]{3,2,1,0:T(8,128)}, u32[]{:S(2)}) copy-start(f32[1,16,96,768]{3,2,1,0:T(8,128)} %get-tuple-element.6) | copy-start | bytes 14155780
  118.0 21.3 %copy-start.2 = (f32[1,16,96,768]{3,2,1,0:T(8,128)S(1)}, f32[1,16,96,768]{3,2,1,0:T(8,128)}, u32[]{:S(2)}) copy-start(f32[1,16,96,768]{3,2,1,0:T(8,128)} %get-tuple-element.7) | copy-start | bytes 14155780
  119.7 16.6 %collective-permute-start.4 = (f32[2,16,1,768]{3,2,1,0:T(1,128)S(1)}, f32[2,16,1,768]{3,2,1,0:T(1,128)S(1)}, u32[]{:S(2)}, u32[]{:S(2)}) collective-permute-start(f32[2,16,1,768]{3,2,1,0:T(1,128)S(1)} %get-tuple-element.19), channel_id=1, source_target_pairs={{4,0},{8,4},{12,8},{16,12},{20,16},{24,20},{28,24},{0,28},{5,1},{9... | collective-permute-start | bytes 294920 | tf_op jit(solution)/shard_map/ppermute | solution.py:18
  121.3 24.0 %slice-start.18 = ((s8[4718592]{0:T(1024)(128)(4,1)}), s8[4194304]{0:T(1024)(128)(4,1)S(1)}, s32[]{:S(2)}) async-start(s8[4718592]{0:T(1024)(128)(4,1)} %bitcast.305), calls=%async_computation.20 | async-start | bytes 8388608
  121.3 24.0 %slice-start.19 = ((s8[4718592]{0:T(1024)(128)(4,1)}), s8[524288]{0:T(1024)(128)(4,1)S(1)}, s32[]{:S(2)}) async-start(s8[4718592]{0:T(1024)(128)(4,1)} %bitcast.305), calls=%async_computation.21 | async-start | bytes 1048576
  121.3 18.0 %collective-permute-start.5 = (f32[2,16,1,768]{3,2,1,0:T(1,128)S(1)}, f32[2,16,1,768]{3,2,1,0:T(1,128)S(1)}, u32[]{:S(2)}, u32[]{:S(2)}) collective-permute-start(f32[2,16,1,768]{3,2,1,0:T(1,128)S(1)} %get-tuple-element.18), channel_id=1, source_target_pairs={{0,4},{4,8},{8,12},{12,16},{16,20},{20,24},{24,28},{28,0},{1,5},{5... | collective-permute-start | bytes 294920 | tf_op jit(solution)/shard_map/ppermute | solution.py:15
  140.6 17.9 %collective-permute-start.6 = (f32[2,1,98,768]{3,0,2,1:T(2,128)}, f32[2,1,98,768]{3,0,2,1:T(2,128)}, u32[]{:S(2)}, u32[]{:S(2)}) collective-permute-start(f32[2,1,98,768]{3,0,2,1:T(2,128)} %copy.16), channel_id=1, source_target_pairs={{1,0},{2,1},{3,2},{0,3},{5,4},{6,5},{7,6},{4,7},{9,8},{10,9},{11,1... | collective-permute-start | bytes 1806344 | tf_op jit(solution)/shard_map/ppermute | solution.py:18
  145.3 26.0 %collective-permute-start.7 = (f32[2,1,98,768]{3,0,2,1:T(2,128)}, f32[2,1,98,768]{3,0,2,1:T(2,128)}, u32[]{:S(2)}, u32[]{:S(2)}) collective-permute-start(f32[2,1,98,768]{3,0,2,1:T(2,128)} %copy.18), channel_id=1, source_target_pairs={{0,1},{1,2},{2,3},{3,0},{4,5},{5,6},{6,7},{7,4},{8,9},{9,10},{10,1... | collective-permute-start | bytes 1806344 | tf_op jit(solution)/shard_map/ppermute | solution.py:15
  146.8 26.5 %copy-start.19 = (f32[16]{0:T(128)S(1)}, f32[16]{0:T(128)}, u32[]{:S(2)}) copy-start(f32[16]{0:T(128)} %param.8) | copy-start | bytes 196
  240.1 54.4 %slice-start.2 = ((s8[4718592]{0:T(1024)(128)(4,1)}), s8[4194304]{0:T(1024)(128)(4,1)S(1)}, s32[]{:S(2)}) async-start(s8[4718592]{0:T(1024)(128)(4,1)} %bitcast.287), calls=%async_computation.4 | async-start | bytes 8388608
  240.1 57.1 %slice-start.8 = ((s8[4718592]{0:T(1024)(128)(4,1)}), s8[4194304]{0:T(1024)(128)(4,1)S(1)}, s32[]{:S(2)}) async-start(s8[4718592]{0:T(1024)(128)(4,1)} %bitcast.296), calls=%async_computation.10 | async-start | bytes 8388608
  240.1 57.1 %slice-start.20 = ((s8[4718592]{0:T(1024)(128)(4,1)}), s8[4194304]{0:T(1024)(128)(4,1)S(1)}, s32[]{:S(2)}) async-start(s8[4718592]{0:T(1024)(128)(4,1)} %bitcast.308), calls=%async_computation.22 | async-start | bytes 8388608
  267.4 27.1 %slice-start.3 = ((s8[4718592]{0:T(1024)(128)(4,1)}), s8[524288]{0:T(1024)(128)(4,1)S(1)}, s32[]{:S(2)}) async-start(s8[4718592]{0:T(1024)(128)(4,1)} %bitcast.287), calls=%async_computation.5 | async-start | bytes 1048576
  267.4 29.8 %slice-start.9 = ((s8[4718592]{0:T(1024)(128)(4,1)}), s8[524288]{0:T(1024)(128)(4,1)S(1)}, s32[]{:S(2)}) async-start(s8[4718592]{0:T(1024)(128)(4,1)} %bitcast.296), calls=%async_computation.11 | async-start | bytes 1048576
  267.4 29.8 %slice-start.21 = ((s8[4718592]{0:T(1024)(128)(4,1)}), s8[524288]{0:T(1024)(128)(4,1)S(1)}, s32[]{:S(2)}) async-start(s8[4718592]{0:T(1024)(128)(4,1)} %bitcast.308), calls=%async_computation.23 | async-start | bytes 1048576
  294.5 2.2 copy-start
  296.7 35.0 %collective-permute-start.8 = (f32[2,16,1,768]{3,2,1,0:T(1,128)S(1)}, f32[2,16,1,768]{3,2,1,0:T(1,128)S(1)}, u32[]{:S(2)}, u32[]{:S(2)}) collective-permute-start(f32[2,16,1,768]{3,2,1,0:T(1,128)S(1)} %get-tuple-element.16), channel_id=1, source_target_pairs={{4,0},{8,4},{12,8},{16,12},{20,16},{24,20},{28,24},{0,28},{5,1},{9... | collective-permute-start | bytes 294920 | tf_op jit(solution)/shard_map/ppermute | solution.py:18
  296.7 35.1 %collective-permute-start.9 = (f32[2,16,1,768]{3,2,1,0:T(1,128)S(1)}, f32[2,16,1,768]{3,2,1,0:T(1,128)S(1)}, u32[]{:S(2)}, u32[]{:S(2)}) collective-permute-start(f32[2,16,1,768]{3,2,1,0:T(1,128)S(1)} %get-tuple-element.17), channel_id=1, source_target_pairs={{0,4},{4,8},{8,12},{12,16},{16,20},{20,24},{24,28},{28,0},{1,5},{5... | collective-permute-start | bytes 294920 | tf_op jit(solution)/shard_map/ppermute | solution.py:15
  327.0 104.0 %all-to-all-start = ((f32[16,768,96]{2,0,1:T(8,128)}), f32[16,768,96]{2,0,1:T(8,128)}, u32[]{:S(2)}, u32[]{:S(2)}) async-start(f32[16,768,96]{2,0,1:T(8,128)} %copy.20), calls=%async_computation | async-start | bytes 12582912 | tf_op jit(solution)/shard_map/all_to_all | solution.py:95
  331.7 70.5 %copy-start.14 = (f32[2,16,1,768]{3,2,1,0:T(1,128)}, f32[2,16,1,768]{3,2,1,0:T(1,128)S(1)}, u32[]{:S(2)}) copy-start(f32[2,16,1,768]{3,2,1,0:T(1,128)S(1)} %collective-permute-done.8) | copy-start | bytes 294916
  331.7 70.5 %copy-start.15 = (f32[2,16,1,768]{3,2,1,0:T(1,128)}, f32[2,16,1,768]{3,2,1,0:T(1,128)S(1)}, u32[]{:S(2)}) copy-start(f32[2,16,1,768]{3,2,1,0:T(1,128)S(1)} %collective-permute-done.9) | copy-start | bytes 294916
  333.5 19.8 %collective-permute-start.10 = (f32[2,1,98,768]{3,0,2,1:T(2,128)S(1)}, f32[2,1,98,768]{3,0,2,1:T(2,128)S(1)}, u32[]{:S(2)}, u32[]{:S(2)}) collective-permute-start(f32[2,1,98,768]{3,0,2,1:T(2,128)S(1)} %copy.24), channel_id=1, source_target_pairs={{1,0},{2,1},{3,2},{0,3},{5,4},{6,5},{7,6},{4,7},{9,8},{10,9},{11,1... | collective-permute-start | bytes 1806344 | tf_op jit(solution)/shard_map/ppermute | solution.py:18
  337.6 26.4 %collective-permute-start.11 = (f32[2,1,98,768]{3,0,2,1:T(2,128)}, f32[2,1,98,768]{3,0,2,1:T(2,128)}, u32[]{:S(2)}, u32[]{:S(2)}) collective-permute-start(f32[2,1,98,768]{3,0,2,1:T(2,128)} %copy.26), channel_id=1, source_target_pairs={{0,1},{1,2},{2,3},{3,0},{4,5},{5,6},{6,7},{7,4},{8,9},{9,10},{10,1... | collective-permute-start | bytes 1806344 | tf_op jit(solution)/shard_map/ppermute | solution.py:15
  340.6 24.5 %copy-start.12 = (f32[1,16,96,1]{3,2,1,0:T(8,128)}, f32[1,16,96,1]{3,2,1,0:T(8,128)S(1)}, u32[]{:S(2)}) copy-start(f32[1,16,96,1]{3,2,1,0:T(8,128)S(1)} %get-tuple-element.30) | copy-start | bytes 18436
  340.6 24.5 %copy-start.13 = (f32[1,16,96,1]{3,2,1,0:T(8,128)}, f32[1,16,96,1]{3,2,1,0:T(8,128)S(1)}, u32[]{:S(2)}) copy-start(f32[1,16,96,1]{3,2,1,0:T(8,128)S(1)} %get-tuple-element.31) | copy-start | bytes 18436
  353.3 30.6 %slice-start = ((s8[4718592]{0:T(1024)(128)(4,1)}), s8[4194304]{0:T(1024)(128)(4,1)S(1)}, s32[]{:S(2)}) async-start(s8[4718592]{0:T(1024)(128)(4,1)} %bitcast.283), calls=%async_computation.2 | async-start | bytes 8388608
  353.3 30.6 %slice-start.4 = ((s8[4718592]{0:T(1024)(128)(4,1)}), s8[4194304]{0:T(1024)(128)(4,1)S(1)}, s32[]{:S(2)}) async-start(s8[4718592]{0:T(1024)(128)(4,1)} %bitcast.289), calls=%async_computation.6 | async-start | bytes 8388608
  353.3 11.8 %copy-start.4 = (f32[2,1,98,768]{3,2,1,0:T(8,128)}, f32[2,1,98,768]{3,2,1,0:T(8,128)S(1)}, u32[]{:S(2)}) copy-start(f32[2,1,98,768]{3,2,1,0:T(8,128)S(1)} %copy.25) | copy-start | bytes 1806340
  365.1 0.8 copy-start.6
  365.9 18.0 %slice-start.1 = ((s8[4718592]{0:T(1024)(128)(4,1)}), s8[524288]{0:T(1024)(128)(4,1)S(1)}, s32[]{:S(2)}) async-start(s8[4718592]{0:T(1024)(128)(4,1)} %bitcast.283), calls=%async_computation.3 | async-start | bytes 1048576
  365.9 18.0 %slice-start.5 = ((s8[4718592]{0:T(1024)(128)(4,1)}), s8[524288]{0:T(1024)(128)(4,1)S(1)}, s32[]{:S(2)}) async-start(s8[4718592]{0:T(1024)(128)(4,1)} %bitcast.289), calls=%async_computation.7 | async-start | bytes 1048576
  365.9 36.4 %slice-start.14 = ((s8[14155776]{0:T(1024)(128)(4,1)}), s8[4194304]{0:T(1024)(128)(4,1)S(1)}, s32[]{:S(2)}) async-start(s8[14155776]{0:T(1024)(128)(4,1)} %bitcast.301), calls=%async_computation.16 | async-start | bytes 8388608
  365.9 36.4 %slice-start.15 = ((s8[14155776]{0:T(1024)(128)(4,1)}), s8[4194304]{0:T(1024)(128)(4,1)S(1)}, s32[]{:S(2)}) async-start(s8[14155776]{0:T(1024)(128)(4,1)} %bitcast.301), calls=%async_computation.17 | async-start | bytes 8388608
  384.0 18.3 %slice-start.16 = ((s8[14155776]{0:T(1024)(128)(4,1)}), s8[4194304]{0:T(1024)(128)(4,1)S(1)}, s32[]{:S(2)}) async-start(s8[14155776]{0:T(1024)(128)(4,1)} %bitcast.301), calls=%async_computation.18 | async-start | bytes 8388608
  384.0 18.3 %slice-start.17 = ((s8[14155776]{0:T(1024)(128)(4,1)}), s8[1572864]{0:T(1024)(128)(4,1)S(1)}, s32[]{:S(2)}) async-start(s8[14155776]{0:T(1024)(128)(4,1)} %bitcast.301), calls=%async_computation.19 | async-start | bytes 3145728
  401.0 23.4 %collective-permute-start.12 = (f32[2,16,1,768]{3,2,1,0:T(1,128)}, f32[2,16,1,768]{3,2,1,0:T(1,128)S(1)}, u32[]{:S(2)}, u32[]{:S(2)}) collective-permute-start(f32[2,16,1,768]{3,2,1,0:T(1,128)} %get-tuple-element.15), channel_id=1, source_target_pairs={{4,0},{8,4},{12,8},{16,12},{20,16},{24,20},{28,24},{0,28},{5,1},{9... | collective-permute-start | bytes 294920 | tf_op jit(solution)/shard_map/ppermute | solution.py:18
  402.3 22.1 %collective-permute-start.13 = (f32[2,16,1,768]{3,2,1,0:T(1,128)S(1)}, f32[2,16,1,768]{3,2,1,0:T(1,128)S(1)}, u32[]{:S(2)}, u32[]{:S(2)}) collective-permute-start(f32[2,16,1,768]{3,2,1,0:T(1,128)S(1)} %get-tuple-element.14), channel_id=1, source_target_pairs={{0,4},{4,8},{8,12},{12,16},{16,20},{20,24},{24,28},{28,0},{1,5},{5... | collective-permute-start | bytes 294920 | tf_op jit(solution)/shard_map/ppermute | solution.py:15
  412.8 11.6 %copy-start.3 = (f32[1,16,96,768]{3,2,1,0:T(8,128)S(1)}, f32[1,16,96,768]{3,2,1,0:T(8,128)}, u32[]{:S(2)}) copy-start(f32[1,16,96,768]{3,2,1,0:T(8,128)} %fusion.6) | copy-start | bytes 14155780
  424.4 1.3 copy-start.16
  424.4 1.3 copy-start.17
  426.0 71.7 %collective-permute-start.14 = (f32[2,1,98,768]{3,0,2,1:T(2,128)S(1)}, f32[2,1,98,768]{3,0,2,1:T(2,128)}, u32[]{:S(2)}, u32[]{:S(2)}) collective-permute-start(f32[2,1,98,768]{3,0,2,1:T(2,128)S(1)} %copy.30), channel_id=1, source_target_pairs={{1,0},{2,1},{3,2},{0,3},{5,4},{6,5},{7,6},{4,7},{9,8},{10,9},{11,1... | collective-permute-start | bytes 1806344 | tf_op jit(solution)/shard_map/ppermute | solution.py:18
  430.8 68.1 %collective-permute-start.15 = (f32[2,1,98,768]{3,0,2,1:T(2,128)}, f32[2,1,98,768]{3,0,2,1:T(2,128)}, u32[]{:S(2)}, u32[]{:S(2)}) collective-permute-start(f32[2,1,98,768]{3,0,2,1:T(2,128)} %copy.32), channel_id=1, source_target_pairs={{0,1},{1,2},{2,3},{3,0},{4,5},{5,6},{6,7},{7,4},{8,9},{9,10},{10,1... | collective-permute-start | bytes 1806344 | tf_op jit(solution)/shard_map/ppermute | solution.py:15
  474.8 26.0 %copy-start.5 = (f32[2,1,98,768]{3,2,1,0:T(8,128)S(1)}, f32[2,1,98,768]{3,2,1,0:T(8,128)}, u32[]{:S(2)}) copy-start(f32[2,1,98,768]{3,2,1,0:T(8,128)} %copy-done.4) | copy-start | bytes 1806340
  474.9 26.0 %copy-start.7 = (f32[2,1,98,768]{3,2,1,0:T(8,128)S(1)}, f32[2,1,98,768]{3,2,1,0:T(8,128)}, u32[]{:S(2)}) copy-start(f32[2,1,98,768]{3,2,1,0:T(8,128)} %copy-done.6) | copy-start | bytes 1806340
  474.9 26.0 %copy-start.8 = (f32[16,96,1]{2,1,0:T(8,128)S(1)}, f32[16,96,1]{2,1,0:T(8,128)}, u32[]{:S(2)}) copy-start(f32[16,96,1]{2,1,0:T(8,128)} %get-tuple-element.32) | copy-start | bytes 18436
  474.9 26.0 %copy-start.9 = (f32[16,96,1]{2,1,0:T(8,128)S(1)}, f32[16,96,1]{2,1,0:T(8,128)}, u32[]{:S(2)}) copy-start(f32[16,96,1]{2,1,0:T(8,128)} %get-tuple-element.33) | copy-start | bytes 18436
where the time goes:
time: 548 us; the launch traced here: 541 us
  matrix products  203 us (37%)
  other arithmetic  140 us (26%)
  local copies, waits for them, and re-layouts  114 us (21%)
  waiting for transfers between devices  51.8 us (9%)
  starting transfers between devices  30.2 us (6%)
    dot_general x2, matrix products, solve_last(): jnp.einsum('prn,nk->prk', field, hartley_table, precision=lax.Precision.H...  54.7 us
    dot_general x2, matrix products, solve_swapped(): jnp.einsum('prn,nk->prk', field, hartley_table, precision=lax.Precision.H...  52.5 us
    dot_general x2, matrix products, solve_last(): jnp.einsum('prk,kn->prn', spectrum, hartley_table, precision=lax.Precisio...  49.9 us
    dot_general x2, matrix products, solve_swapped(): jnp.einsum('prk,kn->pnr', spectrum, hartley_table, precision=lax.Precisio...  46.2 us
    neg x3, other arithmetic, local(): pulled = [-term for term in apply_tensor(tensor, rate_root, grads_two)]  43.3 us
    sub x1, other arithmetic, local(): settled + back - weight * second_last(settled)  39.5 us
    all_to_all x4, local copies, waits for them, and re-layouts, to_lines(): lax.all_to_all(block, ('gx', 'gy'), split_axis=1, concat_axis=2, tiled=True)  32.9 us
    ppermute x8, waiting for transfers between devices, with_halo(): lax.ppermute(lax.slice_in_dim(block, block.shape[dim] - width, None, axis...  30.3 us
  transfers between devices with their start and end apart: 18, of which 6 were waited for; matrix products, arithmetic and copies ran while one was open for 60% of the time, Pallas kernels for 0%

commit v1 on v0

--- a/solution.py
+++ b/solution.py
@@ -1,6 +1,10 @@
+import functools
+import math
 import jax
 import jax.numpy as jnp
 from jax import lax
+from jax.experimental import pallas as pl
+from jax.experimental.pallas import tpu as pltpu
 from jax.sharding import PartitionSpec as P
 
 ENTRY = ((0, 3, 4), (3, 1, 5), (4, 5, 2))
@@ -95,7 +99,7 @@
     return lax.all_to_all(block, ("gx", "gy"), split_axis=1, concat_axis=2, tiled=True)
 
 
-def local(density, tensor, grad_u, plane_rate, cotangent):
+def local_general(density, tensor, grad_u, plane_rate, cotangent):
     points = density.shape[2]
     hartley_table = hartley_matrix(points)
     modes = lax.iota(jnp.int32, points).astype(jnp.float32)
@@ -128,6 +132,376 @@
     return (new_density, adjoint_density)
 
 
+CHUNK = 256
+STRIP = 16
+LIMIT = 60 * 1024 * 1024
+
+
+def decay_matrix(theta, kappa):
+    row = lax.broadcasted_iota(jnp.int32, (CHUNK, CHUNK), 0)
+    column = lax.broadcasted_iota(jnp.int32, (CHUNK, CHUNK), 1)
+    distance = jnp.abs(row - column).astype(jnp.float32)
+    return kappa * jnp.exp(-theta * distance)
+
+
+def solve_lanes(field, par, plane):
+    theta, kappa, wrap = par[plane, 2], par[plane, 3], par[plane, 4]
+    matrix = decay_matrix(theta, kappa)
+    count = field.shape[1] // CHUNK
+    parts = [
+        jnp.dot(
+            field[:, CHUNK * a : CHUNK * (a + 1)],
+            matrix,
+            precision=lax.Precision.HIGHEST,
+            preferred_element_type=jnp.float32,
+        )
+        for a in range(count)
+    ]
+    place = lax.broadcasted_iota(jnp.int32, (1, CHUNK), 1).astype(jnp.float32)
+    rising = jnp.exp(-theta * (place + 1.0))
+    falling = jnp.exp(-theta * (CHUNK - place))
+    step = par[plane, 5]
+    firsts = [part[:, :1] for part in parts]
+    lasts = [part[:, CHUNK - 1 :] for part in parts]
+    results = []
+    for a in range(count):
+        left = lasts[(a - count) % count]
+        right = firsts[(a + count) % count]
+        for m in range(count - 1, 0, -1):
+            left = lasts[(a - m) % count] + step * left
+            right = firsts[(a + m) % count] + step * right
+        results.append(parts[a] + (wrap * left) * rising + (wrap * right) * falling)
+    return results
+
+
+def pack_plane(results, out_ref, slot, members, rows):
+    whole = jnp.concatenate(results, axis=1)
+    group = out_ref.shape[3] // rows
+    for j in range(group):
+
+        @pl.when(slot == j)
+        def _():
+            for d in range(members):
+                out_ref[d, 0, :, rows * j : rows * (j + 1)] = whole[:, rows * d : rows * (d + 1)]
+
+
+def lines_kernel(members, par, in_ref, out_ref):
+    plane = pl.program_id(0)
+    rows = in_ref.shape[1]
+    group = out_ref.shape[3] // rows
+    results = solve_lanes(in_ref[0], par, plane)
+    pack_plane(results, out_ref, lax.rem(plane, group), members, rows)
+
+
+def received_kernel(keep, par, in_ref, *outs):
+    members, _, rows, lanes = in_ref.shape
+    group = lanes // rows
+    block = in_ref[:, 0].reshape(members * rows, lanes)
+    turned = block.T
+    for j in range(group):
+        plane = pl.program_id(0) * group + j
+        lines = turned[rows * j : rows * (j + 1)]
+        results = solve_lanes(lines, par, plane)
+        for a, part in enumerate(results):
+            outs[0][j, :, CHUNK * a : CHUNK * (a + 1)] = part
+        if keep:
+            outs[1][j] = lines
+
+
+def stencil_kernel(adjoint, members, par, rho, rho_z, rho_y, tensor, grad, rim_z, rim_y, *rest):
+    if adjoint:
+        other, other_y, out_ref, cell, flux_y, flux_z, partial = rest
+    else:
+        out_ref, cell, flux_y, flux_z, partial = rest
+    planes, rows, lanes = rho.shape
+    k = pl.program_id(0)
+    now = lax.rem(k, 3)
+    ring = lax.rem(k, 2)
+
+    @pl.when(k == 0)
+    def _():
+        flux_z[2] = rim_z[0]
+
+    @pl.when(k == planes)
+    def _():
+        flux_z[now] = rim_z[1]
+
+    @pl.when(k < planes)
+    def _():
+        root = par[k, 1]
+        scales = (root, root, 1.0)
+        cell[8 : 8 + rows] = rho[k]
+        cell[7:8] = rho_y[k, 0:1]
+        cell[8 + rows : 9 + rows] = rho_y[k, 1:2]
+        flux_y[7:8] = rim_y[k, 0:1]
+        flux_y[8 + rows : 9 + rows] = rim_y[k, 1:2]
+        before = jnp.maximum(k - 1, 0)
+        after = jnp.minimum(k + 1, planes - 1)
+        for s in range(rows // STRIP):
+            top = STRIP * s
+            span = slice(top, top + STRIP)
+            centre = cell[8 + top : 8 + top + STRIP]
+            low = jnp.where(k == 0, rho_z[0, span], rho[before, span])
+            high = jnp.where(k == planes - 1, rho_z[1, span], rho[after, span])
+            vectors = [
+                0.5 * (pltpu.roll(centre, lanes - 1, 1) - pltpu.roll(centre, 1, 1)),
+                0.5 * (cell[9 + top : 9 + top + STRIP] - cell[7 + top : 7 + top + STRIP]),
+                0.5 * (high - low),
+            ]
+            drift = [grad[m, 0, span].astype(jnp.float32) for m in range(3)]
+            if not adjoint:
+                vectors = [vectors[m] + drift[m] * centre for m in range(3)]
+            scaled = [scales[m] * vectors[m] for m in range(3)]
+            entry = [tensor[m, 0, span].astype(jnp.float32) for m in range(6)]
+            fluxes = []
+            for target in range(3):
+                total = scaled[target]
+                for source in range(3):
+                    total = total + entry[ENTRY[target][source]] * scaled[source]
+                fluxes.append(total if target == 2 else root * total)
+            change = 0.5 * (pltpu.roll(fluxes[0], lanes - 1, 1) - pltpu.roll(fluxes[0], 1, 1))
+            if adjoint:
+                for m in range(3):
+                    change = change - drift[m] * fluxes[m]
+            flux_y[8 + top : 8 + top + STRIP] = fluxes[1]
+            flux_z[now, span] = fluxes[2]
+            partial[ring, span] = change
+        for s in range(rows // STRIP):
+            top = STRIP * s
+            span = slice(top, top + STRIP)
+            partial[ring, span] = partial[ring, span] + 0.5 * (
+                flux_y[9 + top : 9 + top + STRIP] - flux_y[7 + top : 7 + top + STRIP]
+            )
+
+    @pl.when(k > 0)
+    def _():
+        q = k - 1
+        rate = par[q, 0]
+        field, field_y = (other, other_y) if adjoint else (rho, rho_y)
+        change = partial[1 - ring] + 0.5 * (flux_z[now] - flux_z[lax.rem(k + 1, 3)])
+        pick = (q, slice(None), slice(None))
+        if adjoint:
+            centre = other[0]
+            edge = other_y[q]
+        else:
+            centre = rho[pick]
+            edge = rho_y[q]
+        index = lax.broadcasted_iota(jnp.int32, (rows, lanes), 0)
+        above = jnp.where(index == 0, edge[0:1], pltpu.roll(centre, 1, 0))
+        below = jnp.where(index == rows - 1, edge[1:2], pltpu.roll(centre, rows - 1, 0))
+        level = centre - rate * (above + below - 2.0 * centre)
+        if adjoint:
+            out_ref[0] = level + change
+        else:
+            parts = solve_lanes(change, par, q)
+            parts = [
+                part + level[:, CHUNK * a : CHUNK * (a + 1)] for a, part in enumerate(parts)
+            ]
+            group = out_ref.shape[3] // rows
+            pack_plane(parts, out_ref, lax.rem(q, group), members, rows)
+
+
+def exchange(low_edge, high_edge, axis):
+    count = lax.axis_size(axis)
+    forward = [(i, (i + 1) % count) for i in range(count)]
+    backward = [(target, source) for source, target in forward]
+    return lax.ppermute(high_edge, axis, forward), lax.ppermute(low_edge, axis, backward)
+
+
+def rims(field):
+    z_low, z_high = exchange(field[:1], field[-1:], "ga")
+    y_low, y_high = exchange(field[:, :1], field[:, -1:], ("gx", "gy"))
+    return jnp.concatenate([z_low, z_high], 0), jnp.concatenate([y_low, y_high], 1)
+
+
+def rim_flux(target, centre, differences, tensor, grad, root, adjoint):
+    scales = (root, root, 1.0)
+    total = 0.0
+    for source in range(3):
+        vector = 0.5 * differences[source]
+        if not adjoint:
+            vector = vector + grad[source].astype(jnp.float32) * centre
+        entry = tensor[ENTRY[target][source]].astype(jnp.float32)
+        if target == source:
+            entry = entry + 1.0
+        total = total + scales[target] * scales[source] * entry * vector
+    return total
+
+
+def ends(array, axis):
+    size = array.shape[axis]
+    return jnp.concatenate(
+        [lax.slice_in_dim(array, 0, 1, axis=axis), lax.slice_in_dim(array, size - 1, size, axis=axis)],
+        axis,
+    )
+
+
+def flux_rims(field, field_z, field_y, tensor, grad, root, adjoint):
+    def across_lanes(part):
+        return jnp.roll(part, -1, 2) - jnp.roll(part, 1, 2)
+
+    plane = ends(field, 0)
+    above = jnp.concatenate([field_y[:, :1], field[:, :-1]], 1)[:: field.shape[0] - 1]
+    below = jnp.concatenate([field[:, 1:], field_y[:, 1:]], 1)[:: field.shape[0] - 1]
+    before = jnp.concatenate([field_z[:1], field[-2:-1]], 0)
+    after = jnp.concatenate([field[1:2], field_z[1:]], 0)
+    flux_z = rim_flux(
+        2,
+        plane,
+        (across_lanes(plane), below - above, after - before),
+        ends(tensor, 1),
+        ends(grad, 1),
+        ends(root, 0),
+        adjoint,
+    )
+    row = ends(field, 1)
+    outer = ends(field_z, 1)
+    above = jnp.concatenate([field_y[:, :1], field[:, -2:-1]], 1)
+    below = jnp.concatenate([field[:, 1:2], field_y[:, 1:]], 1)
+    before = jnp.concatenate([outer[:1], row[:-1]], 0)
+    after = jnp.concatenate([row[1:], outer[1:]], 0)
+    flux_y = rim_flux(
+        1,
+        row,
+        (across_lanes(row), below - above, after - before),
+        ends(tensor, 2),
+        ends(grad, 2),
+        root,
+        adjoint,
+    )
+    z_low, z_high = exchange(flux_z[:1], flux_z[1:], "ga")
+    y_low, y_high = exchange(flux_y[:, :1], flux_y[:, 1:], ("gx", "gy"))
+    return jnp.concatenate([z_low, z_high], 0), jnp.concatenate([y_low, y_high], 1)
+
+
+def whole_block(array):
+    zeros = (0,) * array.ndim
+    return pl.BlockSpec(array.shape, lambda k: zeros)
+
+
+def stencil(adjoint, members, group, par, root, field, tensor, grad, extra=()):
+    planes, rows, lanes = field.shape
+    field_z, field_y = rims(field)
+    rim_z, rim_y = flux_rims(field, field_z, field_y, tensor, grad, root, adjoint)
+    stream = lambda k: (0, jnp.minimum(k, planes - 1), 0, 0)
+    specs = [
+        pl.BlockSpec(memory_space=pltpu.SMEM),
+        whole_block(field),
+        whole_block(field_z),
+        whole_block(field_y),
+        pl.BlockSpec((6, 1, rows, lanes), stream),
+        pl.BlockSpec((3, 1, rows, lanes), stream),
+        whole_block(rim_z),
+        whole_block(rim_y),
+    ]
+    args = [par, field, field_z, field_y, tensor, grad, rim_z, rim_y]
+    if adjoint:
+        other, other_y = extra
+        specs += [
+            pl.BlockSpec((1, rows, lanes), lambda k: (jnp.maximum(k - 1, 0), 0, 0)),
+            whole_block(other_y),
+        ]
+        args += [other, other_y]
+        out_shape = jax.ShapeDtypeStruct(field.shape, jnp.float32)
+        out_spec = pl.BlockSpec((1, rows, lanes), lambda k: (jnp.maximum(k - 1, 0), 0, 0))
+    else:
+        out_shape = jax.ShapeDtypeStruct((members, planes // group, rows, group * rows), jnp.float32)
+        out_spec = pl.BlockSpec(
+            (members, 1, rows, group * rows), lambda k: (0, jnp.maximum(k - 1, 0) // group, 0, 0)
+        )
+    return pl.pallas_call(
+        functools.partial(stencil_kernel, adjoint, members),
+        grid=(planes + 1,),
+        out_shape=out_shape,
+        in_specs=specs,
+        out_specs=out_spec,
+        scratch_shapes=[
+            pltpu.VMEM((rows + 16, lanes), jnp.float32),
+            pltpu.VMEM((rows + 16, lanes), jnp.float32),
+            pltpu.VMEM((3, rows, lanes), jnp.float32),
+            pltpu.VMEM((2, rows, lanes), jnp.float32),
+        ],
+        compiler_params=pltpu.CompilerParams(vmem_limit_bytes=LIMIT),
+        cost_estimate=pl.CostEstimate(
+            flops=80 * field.size, bytes_accessed=32 * field.size, transcendentals=0
+        ),
+    )(*args)
+
+
+def lines_solved(members, group, par, field):
+    planes, rows, lanes = field.shape
+    return pl.pallas_call(
+        functools.partial(lines_kernel, members),
+        grid=(planes,),
+        out_shape=jax.ShapeDtypeStruct(
+            (members, planes // group, rows, group * rows), jnp.float32
+        ),
+        in_specs=[
+            pl.BlockSpec(memory_space=pltpu.SMEM),
+            pl.BlockSpec((1, rows, lanes), lambda k: (k, 0, 0)),
+        ],
+        out_specs=pl.BlockSpec((members, 1, rows, group * rows), lambda k: (0, k // group, 0, 0)),
+        compiler_params=pltpu.CompilerParams(vmem_limit_bytes=LIMIT),
+        cost_estimate=pl.CostEstimate(
+            flops=3072 * field.size, bytes_accessed=8 * field.size, transcendentals=0
+        ),
+    )(par, field)
+
+
+def received_solved(keep, par, block):
+    members, groups, rows, packed = block.shape
+    group = packed // rows
+    shape = jax.ShapeDtypeStruct((groups * group, rows, members * rows), jnp.float32)
+    spec = pl.BlockSpec((group, rows, members * rows), lambda k: (k, 0, 0))
+    return pl.pallas_call(
+        functools.partial(received_kernel, keep),
+        grid=(groups,),
+        out_shape=[shape, shape] if keep else [shape],
+        in_specs=[
+            pl.BlockSpec(memory_space=pltpu.SMEM),
+            pl.BlockSpec((members, 1, rows, packed), lambda k: (0, k, 0, 0)),
+        ],
+        out_specs=[spec, spec] if keep else [spec],
+        compiler_params=pltpu.CompilerParams(vmem_limit_bytes=LIMIT),
+        cost_estimate=pl.CostEstimate(
+            flops=3072 * block.size, bytes_accessed=8 * block.size, transcendentals=0
+        ),
+    )(par, block)
+
+
+def traded(block):
+    return lax.all_to_all(block, ("gx", "gy"), split_axis=0, concat_axis=0, tiled=True)
+
+
+def local(density, tensor, grad_u, plane_rate, cotangent):
+    planes, rows, lanes = density.shape
+    members = lanes // rows
+    group = 128 // math.gcd(rows, 128)
+    if rows % STRIP or planes % group or lanes % CHUNK:
+        return local_general(density, tensor, grad_u, plane_rate, cotangent)
+    root = jnp.sqrt(plane_rate)
+    half = 0.5 / root
+    theta = 2.0 * jnp.log1p(half + half * half / (1.0 + jnp.sqrt(1.0 + half * half)))
+    kappa = 1.0 / jnp.sqrt(1.0 + 4.0 * plane_rate)
+    wrap = 1.0 / (1.0 - jnp.exp(-theta * lanes))
+    step = jnp.exp(-theta * CHUNK)
+    par = jnp.stack([plane_rate, root, theta, kappa, wrap, step], 1)
+    root = root[:, None, None]
+    swept = traded(lines_solved(members, group, par, cotangent))
+    packed = stencil(False, members, group, par, root, density, tensor, grad_u)
+    packed, swept = lax.optimization_barrier((packed, swept))
+    moved = traded(packed)
+    settled, returned = received_solved(True, par, swept)
+    low, high = exchange(returned[:, :1], returned[:, -1:], ("gx", "gy"))
+    returned_y = jnp.concatenate([low, high], 1)
+    adjoint_density = stencil(
+        True, members, group, par, root, settled, tensor, grad_u, (returned, returned_y)
+    )
+    moved, adjoint_density = lax.optimization_barrier((moved, adjoint_density))
+    (new_density,) = received_solved(False, par, moved)
+    return (new_density, adjoint_density)
+
+
 def solution(mesh):
     placed = (
         P("ga", ("gx", "gy"), None),

time: 548 us -> 260 us (0.47); the launches traced: 541 us -> 259 us
  matrix products: 203 us -> 0 us
  other arithmetic: 140 us -> 18.1 us
  Pallas kernels: 0 us -> 98.9 us
  local copies, waits for them, and re-layouts: 114 us -> 27 us
  waiting for transfers between devices: 51.8 us -> 73.5 us
  starting transfers between devices: 30.2 us -> 39.9 us
    dot_general x8 -> x0, matrix products: 203 us -> none  [the longest x2 54.7 us: solve_last(): jnp.einsum('prn,nk->prk', field, hartley_table, precision=lax.Precision.H...]
    pallas_call x0 -> x5, Pallas kernels: none -> 98.9 us  [the longest x2 60 us: stencil(): pl.pallas_call(functools.partial(stencil_kernel, adjoint, members), grid=...]
    neg x3 -> x0, other arithmetic: 43.3 us -> none  [local(): pulled = [-term for term in apply_tensor(tensor, rate_root, grads_two)]]
    sub x2 -> x0, other arithmetic: 39.6 us -> none  [the longest x1 39.5 us: local(): settled + back - weight * second_last(settled)]
    all_to_all x4 -> x0, local copies, waits for them, and re-layouts: 32.9 us -> none  [to_lines(): lax.all_to_all(block, ('gx', 'gy'), split_axis=1, concat_axis=2, tiled=True)]
    ppermute x16 -> x18, waiting for transfers between devices: 51.8 us -> 73.5 us  [the longest x9 44 us: exchange(): lax.ppermute(low_edge, axis, backward)]
    dot_general x2 -> x0, other arithmetic: 17.4 us -> none  [the longest x1 14.8 us: solve_swapped(): jnp.einsum('prn,nk->prk', field, hartley_table, precision=lax.Precision.H...]
    add x2 -> x4, other arithmetic: 21.4 us -> 5.01 us  [rim_flux(): total = total + scales[target] * scales[source] * entry * vector]
  transfers between devices with their start and end apart: 18 -> 20, of which waited for: 6 -> 5; matrix products, arithmetic and copies ran while one was open for 60% -> 16% of each run, Pallas kernels for 0% -> 30%
where the time goes in v1:
time: 260 us; the launch traced here: 259 us
  Pallas kernels  98.9 us (38%)
  waiting for transfers between devices  73.5 us (28%)
  starting transfers between devices  39.9 us (15%)
  local copies, waits for them, and re-layouts  27 us (10%)
  other arithmetic  18.1 us (7%)
    pallas_call x2, Pallas kernels, stencil(): pl.pallas_call(functools.partial(stencil_kernel, adjoint, members), grid=...  60 us
    ppermute x9, waiting for transfers between devices, exchange(): lax.ppermute(low_edge, axis, backward)  44 us
    ppermute x9, waiting for transfers between devices, exchange(): lax.ppermute(high_edge, axis, forward)  29.5 us
    ppermute x9, starting transfers between devices, exchange(): lax.ppermute(low_edge, axis, backward)  26.6 us
    pallas_call x2, Pallas kernels, received_solved(): pl.pallas_call(functools.partial(received_kernel, keep), grid=(groups,),...  21 us
    pallas_call x1, Pallas kernels, lines_solved(): pl.pallas_call(functools.partial(lines_kernel, members), grid=(planes,),...  17.9 us
    all_to_all x2, starting transfers between devices, traded(): lax.all_to_all(block, ('gx', 'gy'), split_axis=0, concat_axis=0, tiled=True)  9.38 us
    slice x6, local copies, waits for them, and re-layouts, ends(): lax.slice_in_dim(array, 0, 1, axis=axis)  7.43 us
  transfers between devices with their start and end apart: 20, of which 5 were waited for; matrix products, arithmetic and copies ran while one was open for 16% of the time, Pallas kernels for 30%

profile of v1, /device:TPU:0, one launch (start us, length us, event | category | flops | bytes accessed | tf_op | source)
XLA Modules:
  0.0 258.6 jit_solution(6199055536758085515)
XLA Ops:
  0.6 1.3 fusion.84
  2.0 3.1 %collective-permute-start = (f32[1,96,768]{2,1,0:T(8,128)S(1)}, f32[1,96,768]{2,1,0:T(8,128)}, u32[]{:S(2)}, u32[]{:S(2)}) collective-permute-start(f32[1,96,768]{2,1,0:T(8,128)S(1)} %get-tuple-element.53), channel_id=1, source_target_pairs={{0,1},{1,2},{2,3},{3,0},{4,5},{5,6},{6,7},{7,4},{8,9},{9,10},{10,1... | collective-permute-start | bytes 884744 | tf_op jit(solution)/shard_map/ppermute | solution.py:308
  5.0 2.1 collective-permute-start.1
  7.1 2.1 fusion.82
  9.3 2.6 %collective-permute-start.3 = (f32[16,1,768]{2,1,0:T(1,128)S(1)}, f32[16,1,768]{2,1,0:T(1,128)S(1)}, u32[]{:S(2)}, u32[]{:S(2)}) collective-permute-start(f32[16,1,768]{2,1,0:T(1,128)S(1)} %get-tuple-element.45), channel_id=1, source_target_pairs={{4,0},{8,4},{12,8},{16,12},{20,16},{24,20},{28,24},{0,28},{5,1},{9... | collective-permute-start | bytes 147464 | tf_op jit(solution)/shard_map/ppermute | solution.py:308
  11.9 1.2 sqrt_multiply_fusion
  13.5 0.7 copy.7
  14.3 0.7 stack.27.par
  15.0 17.9 %shard_map.69 = f32[8,4,96,384]{3,2,1,0:T(8,128)} custom-call(f32[16,6]{1,0:T(8,128)} %stack.27.par, f32[16,96,768]{2,1,0:T(8,128)} %in_ref.1), custom_call_target="tpu_custom_call" | custom-call | flops 3623878656 | bytes 9437184 | tf_op jit(solution)/shard_map/pallas_call | solution.py:433
  32.9 4.8 %all-to-all-start = ((f32[8,4,96,384]{3,2,1,0:T(8,128)}), f32[8,4,96,384]{3,2,1,0:T(8,128)}, u32[]{:S(2)}, u32[]{:S(2)}) async-start(f32[8,4,96,384]{3,2,1,0:T(8,128)} %shard_map.69), calls=%async_computation | async-start | bytes 9437184 | tf_op jit(solution)/shard_map/all_to_all | solution.py:473
  37.7 1.0 fusion.39
  38.6 0.8 fusion.61
  39.5 0.2 fusion.2
  39.7 0.7 fusion.44
  40.5 2.2 fusion.76
  42.7 0.7 fusion.91
  43.3 1.2 fusion.77
  44.5 1.6 fusion.75
  46.1 3.0 %fusion.74 = (bf16[6,16,1,768]{3,2,1,0:T(2,128)(2,1)}, bf16[6,16,1,768]{3,2,1,0:T(2,128)(2,1)}) fusion(bf16[6,16,96,768]{3,2,1,0:T(8,128)(2,1)} %tensor.3), kind=kLoop, calls=%fused_computation.179 | loop fusion | bytes 589824 | tf_op jit(solution)/shard_map/slice | solution.py:334
  49.1 0.9 fusion.83
  50.0 1.3 maximum_bitcast_fusion.3
  51.3 0.4 pad_maximum_fusion
  51.8 0.4 pad_maximum_fusion.1
  52.2 0.4 copy-done.9
  52.8 2.8 %fusion.13 = (f32[2,96,768]{2,1,0:T(8,128)S(1)}, bf16[1,2,96,768]{3,2,1,0:T(8,128)(2,1)}, bf16[2,96,768]{2,1,0:T(8,128)(2,1)}, bf16[2,96,768]{2,1,0:T(8,128)(2,1)}) fusion(f32[2,96,1]{2,1,0:T(8,128)S(1)} %copy-done.10, f32[2,96,767]{2,1,0:T(8,128)S(1)} %get-tuple-element.67, f32[2,96,767]{2,1,0:T(8,128)S(1)} %get-tuple-element.66, ...), kind=kLoop, calls=%fused_computation.38 | loop fusion | flops 5455872 | bytes 8257544 | tf_op jit(solution)/shard_map/add | solution.py:327
  55.7 3.8 %collective-permute-start.5 = (f32[1,96,768]{2,1,0:T(8,128)S(1)}, f32[1,96,768]{2,1,0:T(8,128)S(1)}, u32[]{:S(2)}, u32[]{:S(2)}) collective-permute-start(f32[1,96,768]{2,1,0:T(8,128)S(1)} %get-tuple-element.63), channel_id=1, source_target_pairs={{1,0},{2,1},{3,2},{0,3},{5,4},{6,5},{7,6},{4,7},{9,8},{10,9},{11,1... | collective-permute-start | bytes 884744 | tf_op jit(solution)/shard_map/ppermute | solution.py:308
  59.5 1.0 constant_dynamic-update-slice_fusion.1
  60.5 1.0 constant_dynamic-update-slice_fusion.rho_z
  61.6 1.2 fusion.59
  63.0 2.6 %collective-permute-start.7 = (f32[16,1,768]{2,1,0:T(1,128)S(1)}, f32[16,1,768]{2,1,0:T(1,128)S(1)}, u32[]{:S(2)}, u32[]{:S(2)}) collective-permute-start(f32[16,1,768]{2,1,0:T(1,128)S(1)} %get-tuple-element.75), channel_id=1, source_target_pairs={{4,0},{8,4},{12,8},{16,12},{20,16},{24,20},{28,24},{0,28},{5,1},{9... | collective-permute-start | bytes 147464 | tf_op jit(solution)/shard_map/ppermute | solution.py:308
  65.6 0.7 pad_maximum_fusion.12.rho_y
  66.3 26.4 %collective-permute-done.6 = f32[16,1,768]{2,1,0:T(1,128)S(1)} collective-permute-done((f32[16,1,768]{2,1,0:T(1,128)S(1)}, f32[16,1,768]{2,1,0:T(1,128)S(1)}, u32[]{:S(2)}, u32[]{:S(2)}) %collective-permute-start.6) | collective-permute-done | bytes 49184 | tf_op jit(solution)/shard_map/ppermute | solution.py:308
  92.8 0.7 pad_maximum_fusion.18.rim_y
  93.5 0.9 pad_maximum_fusion.6.rim_z
  94.4 35.5 %shard_map.68 = f32[8,4,96,384]{3,2,1,0:T(8,128)} custom-call(f32[16,6]{1,0:T(8,128)} %stack.27.par, f32[16,96,768]{2,1,0:T(8,128)} %rho.1, f32[2,96,768]{2,1,0:T(8,128)} %copy-done, f32[16,2,768]{2,1,0:T(2,128)} %pad_maximum_fusion.12.rho_y, bf16[6,16,96,768]{3,2,1,0:T(8,128)(2,1)} %tensor.3, bf16[3,16,96,768]{3,2,1,0:T(8,128)(2,1)} %grad.3, ...), custom_call_target="tpu_custom_call" | custom-call | flops 94371840 | bytes 37748736 | tf_op jit(solution)/shard_map/pallas_call | solution.py:412
  129.9 10.5 %shard_map.70 = (f32[16,96,768]{2,1,0:T(8,128)}, f32[16,96,768]{2,1,0:T(8,128)}) custom-call(f32[16,6]{1,0:T(8,128)} %stack.27.par, f32[8,4,96,384]{3,2,1,0:T(8,128)} %all-to-all-done.in_ref), custom_call_target="tpu_custom_call" | custom-call | flops 3623878656 | bytes 9437184 | tf_op jit(solution)/shard_map/pallas_call | solution.py:456
  140.4 1.3 fusion.81
  141.7 3.8 %collective-permute-start.9 = (f32[1,96,768]{2,1,0:T(8,128)S(1)}, f32[1,96,768]{2,1,0:T(8,128)S(1)}, u32[]{:S(2)}, u32[]{:S(2)}) collective-permute-start(f32[1,96,768]{2,1,0:T(8,128)S(1)} %get-tuple-element.42), channel_id=1, source_target_pairs={{1,0},{2,1},{3,2},{0,3},{5,4},{6,5},{7,6},{4,7},{9,8},{10,9},{11,1... | collective-permute-start | bytes 884744 | tf_op jit(solution)/shard_map/ppermute | solution.py:308
  145.5 4.6 %all-to-all-start.1 = ((f32[8,4,96,384]{3,2,1,0:T(8,128)}), f32[8,4,96,384]{3,2,1,0:T(8,128)}, u32[]{:S(2)}, u32[]{:S(2)}) async-start(f32[8,4,96,384]{3,2,1,0:T(8,128)} %shard_map.68), calls=%async_computation.1 | async-start | bytes 9437184 | tf_op jit(solution)/shard_map/all_to_all | solution.py:473
  150.2 1.6 fusion.79
  151.7 0.4 collective-permute-start.10
  152.2 2.3 collective-permute-start.11
  154.6 0.3 fusion.38
  155.0 0.2 fusion
  155.3 4.7 %fusion.80 = (f32[16,95,768]{2,1,0:T(8,128)S(1)}, f32[16,95,768]{2,1,0:T(8,128)S(1)}) fusion(f32[16,96,768]{2,1,0:T(8,128)} %get-tuple-element.10.rho), kind=kLoop, calls=%fused_computation.185 | loop fusion | bytes 18677760 | tf_op jit(solution)/shard_map/slice | solution.py:345
  159.9 1.2 fusion.78
  161.2 41.1 %collective-permute-done.11 = f32[16,1,768]{2,1,0:T(1,128)S(1)} collective-permute-done((f32[16,1,768]{2,1,0:T(1,128)S(1)}, f32[16,1,768]{2,1,0:T(1,128)S(1)}, u32[]{:S(2)}, u32[]{:S(2)}) %collective-permute-start.11) | collective-permute-done | bytes 49184 | tf_op jit(solution)/shard_map/ppermute | solution.py:308
  202.3 2.9 %collective-permute-start.17 = (f32[16,1,768]{2,1,0:T(1,128)S(1)}, f32[16,1,768]{2,1,0:T(1,128)S(1)}, u32[]{:S(2)}, u32[]{:S(2)}) collective-permute-start(f32[16,1,768]{2,1,0:T(1,128)S(1)} %get-tuple-element.33), channel_id=1, source_target_pairs={{4,0},{8,4},{12,8},{16,12},{20,16},{24,20},{28,24},{0,28},{5,1},{9... | collective-permute-start | bytes 147464 | tf_op jit(solution)/shard_map/ppermute | solution.py:308
  205.2 0.4 pad_maximum_fusion.2
  205.6 0.7 pad_maximum_fusion.15.rho_y
  206.3 0.4 pad_maximum_fusion.3
  206.8 0.5 copy-done.2
  207.5 0.5 fusion.8
  208.1 3.8 %collective-permute-start.13 = (f32[1,96,768]{2,1,0:T(8,128)S(1)}, f32[1,96,768]{2,1,0:T(8,128)S(1)}, u32[]{:S(2)}, u32[]{:S(2)}) collective-permute-start(f32[1,96,768]{2,1,0:T(8,128)S(1)} %get-tuple-element.57), channel_id=1, source_target_pairs={{1,0},{2,1},{3,2},{0,3},{5,4},{6,5},{7,6},{4,7},{9,8},{10,9},{11,1... | collective-permute-start | bytes 884744 | tf_op jit(solution)/shard_map/ppermute | solution.py:308
  212.0 0.5 fusion.31
  212.7 2.6 %collective-permute-start.15 = (f32[16,1,768]{2,1,0:T(1,128)S(1)}, f32[16,1,768]{2,1,0:T(1,128)S(1)}, u32[]{:S(2)}, u32[]{:S(2)}) collective-permute-start(f32[16,1,768]{2,1,0:T(1,128)S(1)} %get-tuple-element.69), channel_id=1, source_target_pairs={{4,0},{8,4},{12,8},{16,12},{20,16},{24,20},{28,24},{0,28},{5,1},{9... | collective-permute-start | bytes 147464 | tf_op jit(solution)/shard_map/ppermute | solution.py:308
  215.4 0.7 pad_maximum_fusion.20.rest_1_
  216.1 1.0 collective-permute-done.14
  217.1 0.7 pad_maximum_fusion.19.rim_y
  217.9 2.0 collective-permute-done.12
  219.8 2.9 %collective-permute-done.13 = f32[1,96,768]{2,1,0:T(8,128)S(1)} collective-permute-done((f32[1,96,768]{2,1,0:T(8,128)S(1)}, f32[1,96,768]{2,1,0:T(8,128)S(1)}, u32[]{:S(2)}, u32[]{:S(2)}) %collective-permute-start.13) | collective-permute-done | bytes 294944 | tf_op jit(solution)/shard_map/ppermute | solution.py:308
  222.7 0.9 pad_maximum_fusion.7.rim_z
  223.6 24.5 %shard_map.71 = f32[16,96,768]{2,1,0:T(8,128)} custom-call(f32[16,6]{1,0:T(8,128)} %stack.27.par, f32[16,96,768]{2,1,0:T(8,128)} %get-tuple-element.10.rho, f32[2,96,768]{2,1,0:T(8,128)} %copy-done.1, f32[16,2,768]{2,1,0:T(2,128)} %pad_maximum_fusion.15.rho_y, bf16[6,16,96,768]{3,2,1,0:T(8,128)(2,1)} %tensor.3, bf16[3,16,96,768]{3,2,1,0:T(8,128)(2,1)} %grad.3, ...), custom_call_target="tpu_custom_call" | custom-call | flops 94371840 | bytes 37748736 | tf_op jit(solution)/shard_map/pallas_call | solution.py:412
  248.1 10.5 %shard_map.72 = f32[16,96,768]{2,1,0:T(8,128)} custom-call(f32[16,6]{1,0:T(8,128)} %stack.27.par, f32[8,4,96,384]{3,2,1,0:T(8,128)} %all-to-all-done.1.in_ref), custom_call_target="tpu_custom_call" | custom-call | flops 3623878656 | bytes 9437184 | tf_op jit(solution)/shard_map/pallas_call | solution.py:456
  (93 shorter events, 1.8 us)
Async XLA Ops:
  2.0 50.2 %collective-permute-start = (f32[1,96,768]{2,1,0:T(8,128)S(1)}, f32[1,96,768]{2,1,0:T(8,128)}, u32[]{:S(2)}, u32[]{:S(2)}) collective-permute-start(f32[1,96,768]{2,1,0:T(8,128)S(1)} %get-tuple-element.53), channel_id=1, source_target_pairs={{0,1},{1,2},{2,3},{3,0},{4,5},{5,6},{6,7},{7,4},{8,9},{9,10},{10,1... | collective-permute-start | bytes 884744 | tf_op jit(solution)/shard_map/ppermute | solution.py:308
  5.0 47.2 %collective-permute-start.1 = (f32[1,96,768]{2,1,0:T(8,128)S(1)}, f32[1,96,768]{2,1,0:T(8,128)}, u32[]{:S(2)}, u32[]{:S(2)}) collective-permute-start(f32[1,96,768]{2,1,0:T(8,128)S(1)} %get-tuple-element.52), channel_id=1, source_target_pairs={{1,0},{2,1},{3,2},{0,3},{5,4},{6,5},{7,6},{4,7},{9,8},{10,9},{11,1... | collective-permute-start | bytes 884744 | tf_op jit(solution)/shard_map/ppermute | solution.py:308
  9.3 42.5 %collective-permute-start.2 = (f32[16,1,768]{2,1,0:T(1,128)S(1)}, f32[16,1,768]{2,1,0:T(1,128)S(1)}, u32[]{:S(2)}, u32[]{:S(2)}) collective-permute-start(f32[16,1,768]{2,1,0:T(1,128)S(1)} %get-tuple-element.46), channel_id=1, source_target_pairs={{0,4},{4,8},{8,12},{12,16},{16,20},{20,24},{24,28},{28,0},{1,5},{5... | collective-permute-start | bytes 147464 | tf_op jit(solution)/shard_map/ppermute | solution.py:308
  9.3 42.1 %collective-permute-start.3 = (f32[16,1,768]{2,1,0:T(1,128)S(1)}, f32[16,1,768]{2,1,0:T(1,128)S(1)}, u32[]{:S(2)}, u32[]{:S(2)}) collective-permute-start(f32[16,1,768]{2,1,0:T(1,128)S(1)} %get-tuple-element.45), channel_id=1, source_target_pairs={{4,0},{8,4},{12,8},{16,12},{20,16},{24,20},{28,24},{0,28},{5,1},{9... | collective-permute-start | bytes 147464 | tf_op jit(solution)/shard_map/ppermute | solution.py:308
  13.1 29.6 %copy-start.17 = (f32[16]{0:T(128)}, f32[16]{0:T(128)S(1)}, u32[]{:S(2)}) copy-start(f32[16]{0:T(128)S(1)} %get-tuple-element.87) | copy-start | bytes 196
  32.9 16.2 %slice-start = ((s8[4718592]{0:T(1024)(128)(4,1)}), s8[524288]{0:T(1024)(128)(4,1)S(1)}, s32[]{:S(2)}) async-start(s8[4718592]{0:T(1024)(128)(4,1)} %bitcast.65), calls=%async_computation.2 | async-start | bytes 1048576
  32.9 97.0 %all-to-all-start = ((f32[8,4,96,384]{3,2,1,0:T(8,128)}), f32[8,4,96,384]{3,2,1,0:T(8,128)}, u32[]{:S(2)}, u32[]{:S(2)}) async-start(f32[8,4,96,384]{3,2,1,0:T(8,128)} %shard_map.69), calls=%async_computation | async-start | bytes 9437184 | tf_op jit(solution)/shard_map/all_to_all | solution.py:473
  38.6 10.5 %slice-start.1 = ((s8[4718592]{0:T(1024)(128)(4,1)}), s8[4194304]{0:T(1024)(128)(4,1)S(1)}, s32[]{:S(2)}) async-start(s8[4718592]{0:T(1024)(128)(4,1)} %bitcast.65), calls=%async_computation.3 | async-start | bytes 8388608
  51.3 0.9 copy-start.22
  51.8 0.9 copy-start.9
  51.8 0.9 copy-start.10
  52.7 8.8 %copy-start.5 = (bf16[6,16,1,768]{3,2,1,0:T(2,128)(2,1)S(1)}, bf16[6,16,1,768]{3,2,1,0:T(2,128)(2,1)}, u32[]{:S(2)}) copy-start(bf16[6,16,1,768]{3,2,1,0:T(2,128)(2,1)} %get-tuple-element.24) | copy-start | bytes 442372
  52.7 8.8 %copy-start.6 = (bf16[6,16,1,768]{3,2,1,0:T(2,128)(2,1)S(1)}, bf16[6,16,1,768]{3,2,1,0:T(2,128)(2,1)}, u32[]{:S(2)}) copy-start(bf16[6,16,1,768]{3,2,1,0:T(2,128)(2,1)} %get-tuple-element.25) | copy-start | bytes 442372
  52.7 8.9 %copy-start.7 = (bf16[3,16,1,768]{3,2,1,0:T(2,128)(2,1)S(1)}, bf16[3,16,1,768]{3,2,1,0:T(2,128)(2,1)}, u32[]{:S(2)}) copy-start(bf16[3,16,1,768]{3,2,1,0:T(2,128)(2,1)} %get-tuple-element.28) | copy-start | bytes 221188
  52.7 8.9 %copy-start.8 = (bf16[3,16,1,768]{3,2,1,0:T(2,128)(2,1)S(1)}, bf16[3,16,1,768]{3,2,1,0:T(2,128)(2,1)}, u32[]{:S(2)}) copy-start(bf16[3,16,1,768]{3,2,1,0:T(2,128)(2,1)} %get-tuple-element.29) | copy-start | bytes 221188
  52.7 8.9 %copy-start.11 = (f32[16,2,767]{2,1,0:T(2,128)S(1)}, f32[16,2,767]{2,1,0:T(2,128)}, u32[]{:S(2)}) copy-start(f32[16,2,767]{2,1,0:T(2,128)} %get-tuple-element.76) | copy-start | bytes 294532
  52.7 8.9 %copy-start.12 = (f32[16,2,767]{2,1,0:T(2,128)S(1)}, f32[16,2,767]{2,1,0:T(2,128)}, u32[]{:S(2)}) copy-start(f32[16,2,767]{2,1,0:T(2,128)} %get-tuple-element.77) | copy-start | bytes 294532
  52.7 8.9 %copy-start.13 = (f32[15,2,768]{2,1,0:T(2,128)S(1)}, f32[15,2,768]{2,1,0:T(2,128)}, u32[]{:S(2)}) copy-start(f32[15,2,768]{2,1,0:T(2,128)} %get-tuple-element.80) | copy-start | bytes 276484
  52.7 8.9 %copy-start.14 = (f32[15,2,768]{2,1,0:T(2,128)S(1)}, f32[15,2,768]{2,1,0:T(2,128)}, u32[]{:S(2)}) copy-start(f32[15,2,768]{2,1,0:T(2,128)} %get-tuple-element.81) | copy-start | bytes 276484
  52.7 8.9 %copy-start.15 = (f32[16,1,768]{2,1,0:T(1,128)S(1)}, f32[16,1,768]{2,1,0:T(1,128)}, u32[]{:S(2)}) copy-start(f32[16,1,768]{2,1,0:T(1,128)} %get-tuple-element.44) | copy-start | bytes 147460
  52.8 8.9 %copy-start.16 = (f32[16,1,768]{2,1,0:T(1,128)S(1)}, f32[16,1,768]{2,1,0:T(1,128)}, u32[]{:S(2)}) copy-start(f32[16,1,768]{2,1,0:T(1,128)} %get-tuple-element.47) | copy-start | bytes 147460
  52.8 8.9 %copy-start.18 = (f32[16]{0:T(128)S(1)}, f32[16]{0:T(128)}, u32[]{:S(2)}) copy-start(f32[16]{0:T(128)} %copy-done.17) | copy-start | bytes 196
  52.8 8.9 %copy-start.20 = (f32[16]{0:T(128)S(1)}, f32[16]{0:T(128)}, u32[]{:S(2)}) copy-start(f32[16]{0:T(128)} %get-tuple-element.82) | copy-start | bytes 196
  55.6 37.9 %collective-permute-start.4 = (f32[1,96,768]{2,1,0:T(8,128)S(1)}, f32[1,96,768]{2,1,0:T(8,128)S(1)}, u32[]{:S(2)}, u32[]{:S(2)}) collective-permute-start(f32[1,96,768]{2,1,0:T(8,128)S(1)} %get-tuple-element.62), channel_id=1, source_target_pairs={{0,1},{1,2},{2,3},{3,0},{4,5},{5,6},{6,7},{7,4},{8,9},{9,10},{10,1... | collective-permute-start | bytes 884744 | tf_op jit(solution)/shard_map/ppermute | solution.py:308
  55.7 37.8 %collective-permute-start.5 = (f32[1,96,768]{2,1,0:T(8,128)S(1)}, f32[1,96,768]{2,1,0:T(8,128)S(1)}, u32[]{:S(2)}, u32[]{:S(2)}) collective-permute-start(f32[1,96,768]{2,1,0:T(8,128)S(1)} %get-tuple-element.63), channel_id=1, source_target_pairs={{1,0},{2,1},{3,2},{0,3},{5,4},{6,5},{7,6},{4,7},{9,8},{10,9},{11,1... | collective-permute-start | bytes 884744 | tf_op jit(solution)/shard_map/ppermute | solution.py:308
  61.5 32.9 %copy-start = (f32[2,96,768]{2,1,0:T(8,128)}, f32[2,96,768]{2,1,0:T(8,128)S(1)}, u32[]{:S(2)}) copy-start(f32[2,96,768]{2,1,0:T(8,128)S(1)} %constant_dynamic-update-slice_fusion.rho_z) | copy-start | bytes 1769476
  62.9 29.9 %collective-permute-start.6 = (f32[16,1,768]{2,1,0:T(1,128)S(1)}, f32[16,1,768]{2,1,0:T(1,128)S(1)}, u32[]{:S(2)}, u32[]{:S(2)}) collective-permute-start(f32[16,1,768]{2,1,0:T(1,128)S(1)} %get-tuple-element.74), channel_id=1, source_target_pairs={{0,4},{4,8},{8,12},{12,16},{16,20},{20,24},{24,28},{28,0},{1,5},{5... | collective-permute-start | bytes 147464 | tf_op jit(solution)/shard_map/ppermute | solution.py:308
  63.0 29.8 %collective-permute-start.7 = (f32[16,1,768]{2,1,0:T(1,128)S(1)}, f32[16,1,768]{2,1,0:T(1,128)S(1)}, u32[]{:S(2)}, u32[]{:S(2)}) collective-permute-start(f32[16,1,768]{2,1,0:T(1,128)S(1)} %get-tuple-element.75), channel_id=1, source_target_pairs={{4,0},{8,4},{12,8},{16,12},{20,16},{24,20},{28,24},{0,28},{5,1},{9... | collective-permute-start | bytes 147464 | tf_op jit(solution)/shard_map/ppermute | solution.py:308
  141.7 65.1 %collective-permute-start.8 = (f32[1,96,768]{2,1,0:T(8,128)S(1)}, f32[1,96,768]{2,1,0:T(8,128)S(1)}, u32[]{:S(2)}, u32[]{:S(2)}) collective-permute-start(f32[1,96,768]{2,1,0:T(8,128)S(1)} %get-tuple-element.43), channel_id=1, source_target_pairs={{0,1},{1,2},{2,3},{3,0},{4,5},{5,6},{6,7},{7,4},{8,9},{9,10},{10,1... | collective-permute-start | bytes 884744 | tf_op jit(solution)/shard_map/ppermute | solution.py:308
  141.7 65.0 %collective-permute-start.9 = (f32[1,96,768]{2,1,0:T(8,128)S(1)}, f32[1,96,768]{2,1,0:T(8,128)S(1)}, u32[]{:S(2)}, u32[]{:S(2)}) collective-permute-start(f32[1,96,768]{2,1,0:T(8,128)S(1)} %get-tuple-element.42), channel_id=1, source_target_pairs={{1,0},{2,1},{3,2},{0,3},{5,4},{6,5},{7,6},{4,7},{9,8},{10,9},{11,1... | collective-permute-start | bytes 884744 | tf_op jit(solution)/shard_map/ppermute | solution.py:308
  145.5 102.6 %all-to-all-start.1 = ((f32[8,4,96,384]{3,2,1,0:T(8,128)}), f32[8,4,96,384]{3,2,1,0:T(8,128)}, u32[]{:S(2)}, u32[]{:S(2)}) async-start(f32[8,4,96,384]{3,2,1,0:T(8,128)} %shard_map.68), calls=%async_computation.1 | async-start | bytes 9437184 | tf_op jit(solution)/shard_map/all_to_all | solution.py:473
  151.7 53.8 %collective-permute-start.10 = (f32[16,1,768]{2,1,0:T(1,128)S(1)}, f32[16,1,768]{2,1,0:T(1,128)S(1)}, u32[]{:S(2)}, u32[]{:S(2)}) collective-permute-start(f32[16,1,768]{2,1,0:T(1,128)S(1)} %get-tuple-element.37), channel_id=1, source_target_pairs={{0,4},{4,8},{8,12},{12,16},{16,20},{20,24},{24,28},{28,0},{1,5},{5... | collective-permute-start | bytes 147464 | tf_op jit(solution)/shard_map/ppermute | solution.py:308
  152.2 50.1 %collective-permute-start.11 = (f32[16,1,768]{2,1,0:T(1,128)S(1)}, f32[16,1,768]{2,1,0:T(1,128)S(1)}, u32[]{:S(2)}, u32[]{:S(2)}) collective-permute-start(f32[16,1,768]{2,1,0:T(1,128)S(1)} %get-tuple-element.36), channel_id=1, source_target_pairs={{4,0},{8,4},{12,8},{16,12},{20,16},{24,20},{28,24},{0,28},{5,1},{9... | collective-permute-start | bytes 147464 | tf_op jit(solution)/shard_map/ppermute | solution.py:308
  161.1 51.6 %collective-permute-start.16 = (f32[16,1,768]{2,1,0:T(1,128)S(1)}, f32[16,1,768]{2,1,0:T(1,128)S(1)}, u32[]{:S(2)}, u32[]{:S(2)}) collective-permute-start(f32[16,1,768]{2,1,0:T(1,128)S(1)} %get-tuple-element.32), channel_id=1, source_target_pairs={{0,4},{4,8},{8,12},{12,16},{16,20},{20,24},{24,28},{28,0},{1,5},{5... | collective-permute-start | bytes 147464 | tf_op jit(solution)/shard_map/ppermute | solution.py:308
  202.3 13.1 %collective-permute-start.17 = (f32[16,1,768]{2,1,0:T(1,128)S(1)}, f32[16,1,768]{2,1,0:T(1,128)S(1)}, u32[]{:S(2)}, u32[]{:S(2)}) collective-permute-start(f32[16,1,768]{2,1,0:T(1,128)S(1)} %get-tuple-element.33), channel_id=1, source_target_pairs={{4,0},{8,4},{12,8},{16,12},{20,16},{24,20},{28,24},{0,28},{5,1},{9... | collective-permute-start | bytes 147464 | tf_op jit(solution)/shard_map/ppermute | solution.py:308
  206.3 1.0 copy-start.2
  206.3 1.0 copy-start.3
  206.3 1.1 copy-start.4
  206.3 1.1 copy-start.23
  206.7 5.3 %copy-start.19 = (f32[16]{0:T(128)S(1)}, f32[16]{0:T(128)}, u32[]{:S(2)}) copy-start(f32[16]{0:T(128)} %copy-done.17) | copy-start | bytes 196
  206.8 5.3 %copy-start.21 = (f32[16]{0:T(128)S(1)}, f32[16]{0:T(128)}, u32[]{:S(2)}) copy-start(f32[16]{0:T(128)} %get-tuple-element.82) | copy-start | bytes 196
  208.0 11.8 %collective-permute-start.12 = (f32[1,96,768]{2,1,0:T(8,128)S(1)}, f32[1,96,768]{2,1,0:T(8,128)S(1)}, u32[]{:S(2)}, u32[]{:S(2)}) collective-permute-start(f32[1,96,768]{2,1,0:T(8,128)S(1)} %get-tuple-element.56), channel_id=1, source_target_pairs={{0,1},{1,2},{2,3},{3,0},{4,5},{5,6},{6,7},{7,4},{8,9},{9,10},{10,1... | collective-permute-start | bytes 884744 | tf_op jit(solution)/shard_map/ppermute | solution.py:308
  208.1 14.6 %collective-permute-start.13 = (f32[1,96,768]{2,1,0:T(8,128)S(1)}, f32[1,96,768]{2,1,0:T(8,128)S(1)}, u32[]{:S(2)}, u32[]{:S(2)}) collective-permute-start(f32[1,96,768]{2,1,0:T(8,128)S(1)} %get-tuple-element.57), channel_id=1, source_target_pairs={{1,0},{2,1},{3,2},{0,3},{5,4},{6,5},{7,6},{4,7},{9,8},{10,9},{11,1... | collective-permute-start | bytes 884744 | tf_op jit(solution)/shard_map/ppermute | solution.py:308
  212.0 11.7 %copy-start.1 = (f32[2,96,768]{2,1,0:T(8,128)}, f32[2,96,768]{2,1,0:T(8,128)S(1)}, u32[]{:S(2)}) copy-start(f32[2,96,768]{2,1,0:T(8,128)S(1)} %constant_dynamic-update-slice_fusion.2.rho_z) | copy-start | bytes 1769476
  212.7 4.5 %collective-permute-start.14 = (f32[16,1,768]{2,1,0:T(1,128)S(1)}, f32[16,1,768]{2,1,0:T(1,128)S(1)}, u32[]{:S(2)}, u32[]{:S(2)}) collective-permute-start(f32[16,1,768]{2,1,0:T(1,128)S(1)} %get-tuple-element.68), channel_id=1, source_target_pairs={{0,4},{4,8},{8,12},{12,16},{16,20},{20,24},{24,28},{28,0},{1,5},{5... | collective-permute-start | bytes 147464 | tf_op jit(solution)/shard_map/ppermute | solution.py:308
  212.7 4.4 %collective-permute-start.15 = (f32[16,1,768]{2,1,0:T(1,128)S(1)}, f32[16,1,768]{2,1,0:T(1,128)S(1)}, u32[]{:S(2)}, u32[]{:S(2)}) collective-permute-start(f32[16,1,768]{2,1,0:T(1,128)S(1)} %get-tuple-element.69), channel_id=1, source_target_pairs={{4,0},{8,4},{12,8},{16,12},{20,16},{24,20},{28,24},{0,28},{5,1},{9... | collective-permute-start | bytes 147464 | tf_op jit(solution)/shard_map/ppermute | solution.py:308

commit v2 on v1

--- a/solution.py
+++ b/solution.py
@@ -308,12 +308,6 @@
     return lax.ppermute(high_edge, axis, forward), lax.ppermute(low_edge, axis, backward)
 
 
-def rims(field):
-    z_low, z_high = exchange(field[:1], field[-1:], "ga")
-    y_low, y_high = exchange(field[:, :1], field[:, -1:], ("gx", "gy"))
-    return jnp.concatenate([z_low, z_high], 0), jnp.concatenate([y_low, y_high], 1)
-
-
 def rim_flux(target, centre, differences, tensor, grad, root, adjoint):
     scales = (root, root, 1.0)
     total = 0.0
@@ -336,7 +330,7 @@
     )
 
 
-def flux_rims(field, field_z, field_y, tensor, grad, root, adjoint):
+def flux_rims(field, field_z, field_y, field_z_y, outer_y, coupling_y, drift_y, tensor, grad, root, adjoint):
     def across_lanes(part):
         return jnp.roll(part, -1, 2) - jnp.roll(part, 1, 2)
 
@@ -354,24 +348,39 @@
         ends(root, 0),
         adjoint,
     )
-    row = ends(field, 1)
-    outer = ends(field_z, 1)
-    above = jnp.concatenate([field_y[:, :1], field[:, -2:-1]], 1)
-    below = jnp.concatenate([field[:, 1:2], field_y[:, 1:]], 1)
-    before = jnp.concatenate([outer[:1], row[:-1]], 0)
-    after = jnp.concatenate([row[1:], outer[1:]], 0)
-    flux_y = rim_flux(
-        1,
-        row,
-        (across_lanes(row), below - above, after - before),
-        ends(tensor, 2),
-        ends(grad, 2),
-        root,
-        adjoint,
-    )
     z_low, z_high = exchange(flux_z[:1], flux_z[1:], "ga")
-    y_low, y_high = exchange(flux_y[:, :1], flux_y[:, 1:], ("gx", "gy"))
-    return jnp.concatenate([z_low, z_high], 0), jnp.concatenate([y_low, y_high], 1)
+    sides = []
+    for side in range(2):
+        row = field_y[:, side : side + 1]
+        corner = field_z_y[:, side : side + 1]
+        before = jnp.concatenate([corner[:1], row[:-1]], 0)
+        after = jnp.concatenate([row[1:], corner[1:]], 0)
+        if side == 0:
+            along = field[:, :1] - outer_y[:, :1]
+        else:
+            along = outer_y[:, 1:] - field[:, -1:]
+        total = 0.0
+        for source, difference in enumerate((across_lanes(row), along, after - before)):
+            vector = 0.5 * difference
+            if not adjoint:
+                vector = vector + drift_y[side][:, source : source + 1] * row
+            total = total + coupling_y[side][:, source : source + 1] * vector
+        sides.append(total)
+    return jnp.concatenate([z_low, z_high], 0), jnp.concatenate(sides, 1)
+
+
+def edge_terms(tensor, grad, root, row):
+    scales = (root, root, 1.0)
+    terms = []
+    for source in range(3):
+        entry = lax.slice_in_dim(tensor[ENTRY[1][source]], row, row + 1, axis=1)
+        entry = entry.astype(jnp.float32)
+        if source == 1:
+            entry = entry + 1.0
+        terms.append(root * scales[source] * entry)
+    for source in range(3):
+        terms.append(lax.slice_in_dim(grad[source], row, row + 1, axis=1).astype(jnp.float32))
+    return terms
 
 
 def whole_block(array):
@@ -379,10 +388,17 @@
     return pl.BlockSpec(array.shape, lambda k: zeros)
 
 
-def stencil(adjoint, members, group, par, root, field, tensor, grad, extra=()):
+def stencil(
+    adjoint, members, group, par, root, field, field_y, outer_y, coupling_y, drift_y, tensor, grad, extra=()
+):
     planes, rows, lanes = field.shape
-    field_z, field_y = rims(field)
-    rim_z, rim_y = flux_rims(field, field_z, field_y, tensor, grad, root, adjoint)
+    taller = jnp.concatenate([ends(field, 0), ends(field_y, 0)], 1)
+    low, high = exchange(taller[:1], taller[1:], "ga")
+    field_z = jnp.concatenate([low[:, :rows], high[:, :rows]], 0)
+    field_z_y = jnp.concatenate([low[:, rows:], high[:, rows:]], 0)
+    rim_z, rim_y = flux_rims(
+        field, field_z, field_y, field_z_y, outer_y, coupling_y, drift_y, tensor, grad, root, adjoint
+    )
     stream = lambda k: (0, jnp.minimum(k, planes - 1), 0, 0)
     specs = [
         pl.BlockSpec(memory_space=pltpu.SMEM),
@@ -487,15 +503,53 @@
     step = jnp.exp(-theta * CHUNK)
     par = jnp.stack([plane_rate, root, theta, kappa, wrap, step], 1)
     root = root[:, None, None]
-    swept = traded(lines_solved(members, group, par, cotangent))
-    packed = stencil(False, members, group, par, root, density, tensor, grad_u)
+    low, high = exchange(
+        jnp.concatenate([density[:, :2]] + edge_terms(tensor, grad_u, root, 0), 1),
+        jnp.concatenate([density[:, -2:]] + edge_terms(tensor, grad_u, root, rows - 1), 1),
+        ("gx", "gy"),
+    )
+    swept = lines_solved(members, group, par, cotangent)
+    swept, low, high = lax.optimization_barrier((swept, low, high))
+    swept = traded(swept)
+    coupling_y = (low[:, 2:5], high[:, 2:5])
+    drift_y = (low[:, 5:8], high[:, 5:8])
+    packed = stencil(
+        False,
+        members,
+        group,
+        par,
+        root,
+        density,
+        jnp.concatenate([low[:, 1:2], high[:, :1]], 1),
+        jnp.concatenate([low[:, :1], high[:, 1:2]], 1),
+        coupling_y,
+        drift_y,
+        tensor,
+        grad_u,
+    )
     packed, swept = lax.optimization_barrier((packed, swept))
+    settled, returned = received_solved(True, par, swept)
+    low, high = exchange(
+        jnp.concatenate([settled[:, :2], returned[:, :1]], 1),
+        jnp.concatenate([settled[:, -2:], returned[:, -1:]], 1),
+        ("gx", "gy"),
+    )
+    packed, low, high = lax.optimization_barrier((packed, low, high))
     moved = traded(packed)
-    settled, returned = received_solved(True, par, swept)
-    low, high = exchange(returned[:, :1], returned[:, -1:], ("gx", "gy"))
-    returned_y = jnp.concatenate([low, high], 1)
     adjoint_density = stencil(
-        True, members, group, par, root, settled, tensor, grad_u, (returned, returned_y)
+        True,
+        members,
+        group,
+        par,
+        root,
+        settled,
+        jnp.concatenate([low[:, 1:2], high[:, :1]], 1),
+        jnp.concatenate([low[:, :1], high[:, 1:2]], 1),
+        coupling_y,
+        drift_y,
+        tensor,
+        grad_u,
+        (returned, jnp.concatenate([low[:, 2:], high[:, 2:]], 1)),
     )
     moved, adjoint_density = lax.optimization_barrier((moved, adjoint_density))
     (new_density,) = received_solved(False, par, moved)

time: 260 us -> 246 us (0.946)
  waiting for transfers between devices: 73.5 us -> 30.6 us
  local copies, waits for them, and re-layouts: 27 us -> 54.3 us
  other arithmetic: 18.1 us -> 31.9 us
  starting transfers between devices: 39.9 us -> 27.9 us
    ppermute x9 -> x6, waiting for transfers between devices: 44 us -> 11.4 us  [exchange(): lax.ppermute(low_edge, axis, backward)]
    ppermute x9 -> x6, starting transfers between devices: 26.6 us -> 14.8 us  [exchange(): lax.ppermute(low_edge, axis, backward)]
    slice x2, local copies, waits for them, and re-layouts: 5.58 us -> 17.3 us  [flux_rims(): field[:, 1:]]
    ppermute x9 -> x6, waiting for transfers between devices: 29.5 us -> 19.2 us  [exchange(): lax.ppermute(high_edge, axis, forward)]
    slice x5 -> x29, local copies, waits for them, and re-layouts: 5.05 us -> 14.6 us  [the longest x8 5.01 us: across_lanes(): return jnp.roll(part, -1, 2) - jnp.roll(part, 1, 2)]
    add x0 -> x2, other arithmetic: none -> 6.44 us  [flux_rims(): total = total + coupling_y[side][:, source:source + 1] * vector]
    another operation x7, local copies, waits for them, and re-layouts: 1.83 us -> 7.48 us  [local(): par = jnp.stack([plane_rate, root, theta, kappa, wrap, step], 1)]
    slice x6 -> x2, local copies, waits for them, and re-layouts: 7.43 us -> 2.14 us  [ends(): lax.slice_in_dim(array, 0, 1, axis=axis)]
  transfers between devices with their start and end apart: 20 -> 14, of which waited for: 5 -> 8; matrix products, arithmetic and copies ran while one was open for 16% -> 25% of each run, Pallas kernels for 30% -> 32%
where the time goes in v2:
time: 246 us; the launch traced here: 245 us
  Pallas kernels  98.8 us (40%)
  local copies, waits for them, and re-layouts  54.3 us (22%)
  other arithmetic  31.9 us (13%)
  waiting for transfers between devices  30.6 us (12%)
  starting transfers between devices  27.9 us (11%)
    pallas_call x2, Pallas kernels, stencil(): pl.pallas_call(functools.partial(stencil_kernel, adjoint, members), grid=...  59.9 us
    pallas_call x2, Pallas kernels, received_solved(): pl.pallas_call(functools.partial(received_kernel, keep), grid=(groups,),...  21 us
    ppermute x6, waiting for transfers between devices, exchange(): lax.ppermute(high_edge, axis, forward)  19.2 us
    pallas_call x1, Pallas kernels, lines_solved(): pl.pallas_call(functools.partial(lines_kernel, members), grid=(planes,),...  18 us
    slice x2, local copies, waits for them, and re-layouts, flux_rims(): field[:, 1:]  17.3 us
    ppermute x6, starting transfers between devices, exchange(): lax.ppermute(low_edge, axis, backward)  14.8 us
    ppermute x6, waiting for transfers between devices, exchange(): lax.ppermute(low_edge, axis, backward)  11.4 us
    all_to_all x2, starting transfers between devices, traded(): lax.all_to_all(block, ('gx', 'gy'), split_axis=0, concat_axis=0, tiled=True)  9.24 us
  transfers between devices with their start and end apart: 14, of which 8 were waited for; matrix products, arithmetic and copies ran while one was open for 25% of the time, Pallas kernels for 32%

profile of v2, /device:TPU:0, one launch (start us, length us, event | category | flops | bytes accessed | tf_op | source)
XLA Modules:
  0.0 244.7 jit_solution(13449785301860516340)
XLA Ops:
  0.6 1.4 fusion.93
  2.1 3.7 %slice_bitcast_fusion.3 = (bf16[16,96,768]{2,1,0:T(8,128)(2,1)S(1)}, bf16[16,96,768]{2,1,0:T(8,128)(2,1)S(1)}, bf16[16,96,768]{2,1,0:T(8,128)(2,1)S(1)}) fusion(bf16[6,16,96,768]{3,2,1,0:T(8,128)(2,1)} %tensor.3), kind=kLoop, calls=%fused_computation.7 | loop fusion | bytes 14155776 | tf_op jit(solution)/shard_map/squeeze | solution.py:376
  6.7 1.2 fusion.69
  8.3 1.2 concatenate.290
  9.6 3.3 %collective-permute-start.1 = (f32[16,8,768]{2,1,0:T(8,128)}, f32[16,8,768]{2,1,0:T(8,128)}, u32[]{:S(2)}, u32[]{:S(2)}) collective-permute-start(f32[16,8,768]{2,1,0:T(8,128)} %concatenate.290), channel_id=1, source_target_pairs={{4,0},{8,4},{12,8},{16,12},{20,16},{24,20},{28,24},{0,28},{5,1},{9... | collective-permute-start | bytes 1179656 | tf_op jit(solution)/shard_map/ppermute | solution.py:308
  12.9 1.2 concatenate.289
  14.1 2.2 fusion.68
  16.3 8.6 %fusion.67 = (f32[16,95,768]{2,1,0:T(8,128)}, f32[16,95,768]{2,1,0:T(8,128)}) fusion(f32[16,96,768]{2,1,0:T(8,128)} %rho.1), kind=kLoop, calls=%fused_computation.164 | loop fusion | bytes 18677760 | tf_op jit(solution)/shard_map/slice | solution.py:339
  25.7 0.7 fusion.32
  26.5 1.6 fusion.61
  28.0 2.1 fusion.62
  30.2 1.8 maximum_bitcast_fusion.2
  32.8 1.3 copy.14
  34.1 1.3 copy.16
  35.4 1.3 copy.18
  36.7 1.3 copy.13
  38.1 1.4 stack.27.par
  39.5 18.0 %shard_map.68 = f32[8,4,96,384]{3,2,1,0:T(8,128)} custom-call(f32[16,6]{1,0:T(8,128)} %stack.27.par, f32[16,96,768]{2,1,0:T(8,128)} %in_ref.1), custom_call_target="tpu_custom_call" | custom-call | flops 3623878656 | bytes 9437184 | tf_op jit(solution)/shard_map/pallas_call | solution.py:449
  57.5 1.7 slice.533
  59.1 1.6 slice.534
  60.8 4.6 %all-to-all-start = ((f32[8,4,96,384]{3,2,1,0:T(8,128)}), f32[8,4,96,384]{3,2,1,0:T(8,128)}, u32[]{:S(2)}, u32[]{:S(2)}) async-start(f32[8,4,96,384]{3,2,1,0:T(8,128)} %shard_map.68), calls=%async_computation | async-start | bytes 9437184 | tf_op jit(solution)/shard_map/all_to_all | solution.py:489
  66.2 3.7 %collective-permute-start.3 = (f32[1,98,768]{2,1,0:T(8,128)S(1)}, f32[1,98,768]{2,1,0:T(8,128)S(1)}, u32[]{:S(2)}, u32[]{:S(2)}) collective-permute-start(f32[1,98,768]{2,1,0:T(8,128)S(1)} %get-tuple-element.75), channel_id=1, source_target_pairs={{1,0},{2,1},{3,2},{0,3},{5,4},{6,5},{7,6},{4,7},{9,8},{10,9},{11,1... | collective-permute-start | bytes 903176 | tf_op jit(solution)/shard_map/ppermute | solution.py:308
  69.9 1.0 fusion.76
  70.8 1.0 fusion.79
  71.8 2.8 %pad_maximum_fusion = f32[16,96,768]{2,1,0:T(8,128)S(1)} fusion(f32[16,1,768]{2,1,0:T(1,128)} %slice.534, f32[16,95,768]{2,1,0:T(8,128)} %get-tuple-element.52), kind=kLoop, calls=%fused_computation | loop fusion | flops 1179648 | bytes 9437184 | tf_op jit(solution)/shard_map/concatenate | solution.py:339
  75.2 1.2 fusion.74
  76.4 1.1 fusion.77
  77.5 1.3 fusion.75
  79.5 1.3 fusion.78
  80.8 4.1 %collective-permute-done.2 = f32[1,98,768]{2,1,0:T(8,128)S(1)} collective-permute-done((f32[1,98,768]{2,1,0:T(8,128)S(1)}, f32[1,98,768]{2,1,0:T(8,128)S(1)}, u32[]{:S(2)}, u32[]{:S(2)}) %collective-permute-start.2) | collective-permute-done | bytes 301088 | tf_op jit(solution)/shard_map/ppermute | solution.py:308
  85.1 1.6 fusion.8
  86.7 1.7 collective-permute-start.4
  88.4 2.2 collective-permute-start.5
  90.6 3.4 %multiply_add_fusion = f32[16,1,768]{2,1,0:T(1,128)S(1)} fusion(f32[16,8,768]{2,1,0:T(8,128)} %collective-permute-done.1, f32[16,96,768]{2,1,0:T(8,128)} %rho.1, f32[16,1,767]{2,1,0:T(1,128)S(1)} %get-tuple-element.97, f32[16,1,1]{2,1,0:T(1,128)S(1)} %get-tuple-element.99, f32[16,1,1]{2,1,0:T(1,128)S(1)} %get-tuple-element.98, ...), kind=kLoop, calls=%fused_computation.145 | loop fusion | flops 258048 | bytes 688128 | tf_op jit(solution)/shard_map/add | solution.py:367
  94.0 3.1 %multiply_add_fusion.1 = f32[16,1,768]{2,1,0:T(1,128)S(1)} fusion(f32[16,8,768]{2,1,0:T(8,128)} %collective-permute-done, f32[16,96,768]{2,1,0:T(8,128)} %rho.1, f32[16,1,767]{2,1,0:T(1,128)S(1)} %get-tuple-element.91, f32[16,1,1]{2,1,0:T(1,128)S(1)} %get-tuple-element.93, f32[16,1,1]{2,1,0:T(1,128)S(1)} %get-tuple-element.92, ...), kind=kLoop, calls=%fused_computation.146 | loop fusion | flops 258048 | bytes 688128 | tf_op jit(solution)/shard_map/add | solution.py:367
  97.8 0.9 pad_maximum_fusion.6.rho_z
  98.7 4.4 %collective-permute-done.5 = f32[1,96,768]{2,1,0:T(8,128)S(1)} collective-permute-done((f32[1,96,768]{2,1,0:T(8,128)S(1)}, f32[1,96,768]{2,1,0:T(8,128)S(1)}, u32[]{:S(2)}, u32[]{:S(2)}) %collective-permute-start.5) | collective-permute-done | bytes 294944 | tf_op jit(solution)/shard_map/ppermute | solution.py:308
  103.0 0.9 pad_maximum_fusion.12.rim_z
  103.9 35.4 %shard_map.69 = f32[8,4,96,384]{3,2,1,0:T(8,128)} custom-call(f32[16,6]{1,0:T(8,128)} %stack.27.par, f32[16,96,768]{2,1,0:T(8,128)} %rho.1, f32[2,96,768]{2,1,0:T(8,128)} %pad_maximum_fusion.6.rho_z, f32[16,2,768]{2,1,0:T(2,128)} %pad_maximum_fusion.18.rho_y, bf16[6,16,96,768]{3,2,1,0:T(8,128)(2,1)} %tensor.3, bf16[3,16,96,768]{3,2,1,0:T(8,128)(2,1)} %grad.3, ...), custom_call_target="tpu_custom_call" | custom-call | flops 94371840 | bytes 37748736 | tf_op jit(solution)/shard_map/pallas_call | solution.py:428
  139.3 10.5 %shard_map.70 = (f32[16,96,768]{2,1,0:T(8,128)}, f32[16,96,768]{2,1,0:T(8,128)}) custom-call(f32[16,6]{1,0:T(8,128)} %stack.27.par, f32[8,4,96,384]{3,2,1,0:T(8,128)} %all-to-all-done.in_ref), custom_call_target="tpu_custom_call" | custom-call | flops 3623878656 | bytes 9437184 | tf_op jit(solution)/shard_map/pallas_call | solution.py:472
  149.8 1.2 fusion.65
  151.0 1.3 fusion.64
  152.3 8.7 %fusion.63 = (f32[16,95,768]{2,1,0:T(8,128)}, f32[16,95,768]{2,1,0:T(8,128)}) fusion(f32[16,96,768]{2,1,0:T(8,128)} %get-tuple-element.19.rho), kind=kLoop, calls=%fused_computation.160 | loop fusion | bytes 18677760 | tf_op jit(solution)/shard_map/slice | solution.py:339
  161.1 1.2 fusion.66
  162.3 1.7 collective-permute-start.7
  164.6 2.8 %collective-permute-done.7 = f32[16,3,768]{2,1,0:T(4,128)S(1)} collective-permute-done((f32[16,3,768]{2,1,0:T(4,128)S(1)}, f32[16,3,768]{2,1,0:T(4,128)S(1)}, u32[]{:S(2)}, u32[]{:S(2)}) %collective-permute-start.7) | collective-permute-done | bytes 147488 | tf_op jit(solution)/shard_map/ppermute | solution.py:308
  167.3 2.9 %collective-permute-done.6 = f32[16,3,768]{2,1,0:T(4,128)S(1)} collective-permute-done((f32[16,3,768]{2,1,0:T(4,128)S(1)}, f32[16,3,768]{2,1,0:T(4,128)S(1)}, u32[]{:S(2)}, u32[]{:S(2)}) %collective-permute-start.6) | collective-permute-done | bytes 147488 | tf_op jit(solution)/shard_map/ppermute | solution.py:308
  170.3 4.6 %all-to-all-start.1 = ((f32[8,4,96,384]{3,2,1,0:T(8,128)}), f32[8,4,96,384]{3,2,1,0:T(8,128)}, u32[]{:S(2)}, u32[]{:S(2)}) async-start(f32[8,4,96,384]{3,2,1,0:T(8,128)} %shard_map.69), calls=%async_computation.1 | async-start | bytes 9437184 | tf_op jit(solution)/shard_map/all_to_all | solution.py:489
  175.1 1.1 collective-permute-start.9
  176.3 0.9 collective-permute-start.8
  177.9 2.9 %pad_maximum_fusion.2 = f32[16,96,768]{2,1,0:T(8,128)S(1)} fusion(f32[16,1,768]{2,1,0:T(1,128)S(1)} %slice.606, f32[16,95,768]{2,1,0:T(8,128)} %get-tuple-element.42), kind=kLoop, calls=%fused_computation.2 | loop fusion | flops 1179648 | bytes 9437184 | tf_op jit(solution)/shard_map/concatenate | solution.py:339
  182.0 9.4 %collective-permute-done.8 = f32[1,98,768]{2,1,0:T(8,128)S(1)} collective-permute-done((f32[1,98,768]{2,1,0:T(8,128)S(1)}, f32[1,98,768]{2,1,0:T(8,128)S(1)}, u32[]{:S(2)}, u32[]{:S(2)}) %collective-permute-start.8) | collective-permute-done | bytes 301088 | tf_op jit(solution)/shard_map/ppermute | solution.py:308
  191.9 1.2 fusion.3
  193.2 1.2 collective-permute-start.10
  194.4 2.7 %collective-permute-start.11 = (f32[1,96,768]{2,1,0:T(8,128)S(1)}, f32[1,96,768]{2,1,0:T(8,128)S(1)}, u32[]{:S(2)}, u32[]{:S(2)}) collective-permute-start(f32[1,96,768]{2,1,0:T(8,128)S(1)} %get-tuple-element.77), channel_id=1, source_target_pairs={{1,0},{2,1},{3,2},{0,3},{5,4},{6,5},{7,6},{4,7},{9,8},{10,9},{11,1... | collective-permute-start | bytes 884744 | tf_op jit(solution)/shard_map/ppermute | solution.py:308
  197.0 1.8 fusion.84
  198.8 1.9 fusion.85
  200.8 0.7 pad_maximum_fusion.22.rest_1_
  201.5 0.7 pad_maximum_fusion.21.rim_y
  202.2 2.8 %collective-permute-done.10 = f32[1,96,768]{2,1,0:T(8,128)S(1)} collective-permute-done((f32[1,96,768]{2,1,0:T(8,128)S(1)}, f32[1,96,768]{2,1,0:T(8,128)S(1)}, u32[]{:S(2)}, u32[]{:S(2)}) %collective-permute-start.10) | collective-permute-done | bytes 294944 | tf_op jit(solution)/shard_map/ppermute | solution.py:308
  205.0 3.9 %collective-permute-done.11 = f32[1,96,768]{2,1,0:T(8,128)S(1)} collective-permute-done((f32[1,96,768]{2,1,0:T(8,128)S(1)}, f32[1,96,768]{2,1,0:T(8,128)S(1)}, u32[]{:S(2)}, u32[]{:S(2)}) %collective-permute-start.11) | collective-permute-done | bytes 294944 | tf_op jit(solution)/shard_map/ppermute | solution.py:308
  208.9 0.9 pad_maximum_fusion.13.rim_z
  209.8 24.5 %shard_map.71 = f32[16,96,768]{2,1,0:T(8,128)} custom-call(f32[16,6]{1,0:T(8,128)} %stack.27.par, f32[16,96,768]{2,1,0:T(8,128)} %get-tuple-element.19.rho, f32[2,96,768]{2,1,0:T(8,128)} %get-tuple-element.79.rho_z, f32[16,2,768]{2,1,0:T(2,128)} %pad_maximum_fusion.19.rho_y, bf16[6,16,96,768]{3,2,1,0:T(8,128)(2,1)} %tensor.3, bf16[3,16,96,768]{3,2,1,0:T(8,128)(2,1)} %grad.3, ...), custom_call_target="tpu_custom_call" | custom-call | flops 94371840 | bytes 37748736 | tf_op jit(solution)/shard_map/pallas_call | solution.py:428
  234.3 10.5 %shard_map.72 = f32[16,96,768]{2,1,0:T(8,128)} custom-call(f32[16,6]{1,0:T(8,128)} %stack.27.par, f32[8,4,96,384]{3,2,1,0:T(8,128)} %all-to-all-done.1.in_ref), custom_call_target="tpu_custom_call" | custom-call | flops 3623878656 | bytes 9437184 | tf_op jit(solution)/shard_map/pallas_call | solution.py:472
  (93 shorter events, 8.8 us)
Async XLA Ops:
  0.6 5.2 %slice-start = ((s8[7077888]{0:T(1024)(128)(4,1)}), s8[4194304]{0:T(1024)(128)(4,1)S(1)}, s32[]{:S(2)}) async-start(s8[7077888]{0:T(1024)(128)(4,1)} %bitcast.52), calls=%async_computation.2 | async-start | bytes 8388608
  2.1 28.1 %copy-start.12 = (f32[16]{0:T(128)}, f32[16]{0:T(128)S(1)}, u32[]{:S(2)}) copy-start(f32[16]{0:T(128)S(1)} %get-tuple-element.135) | copy-start | bytes 196
  2.1 4.1 %slice-start.1 = ((s8[7077888]{0:T(1024)(128)(4,1)}), s8[2883584]{0:T(1024)(128)(4,1)S(1)}, s32[]{:S(2)}) async-start(s8[7077888]{0:T(1024)(128)(4,1)} %bitcast.52), calls=%async_computation.3 | async-start | bytes 5767168
  9.6 47.9 %collective-permute-start.1 = (f32[16,8,768]{2,1,0:T(8,128)}, f32[16,8,768]{2,1,0:T(8,128)}, u32[]{:S(2)}, u32[]{:S(2)}) collective-permute-start(f32[16,8,768]{2,1,0:T(8,128)} %concatenate.290), channel_id=1, source_target_pairs={{4,0},{8,4},{12,8},{16,12},{20,16},{24,20},{28,24},{0,28},{5,1},{9... | collective-permute-start | bytes 1179656 | tf_op jit(solution)/shard_map/ppermute | solution.py:308
  14.1 43.3 %collective-permute-start = (f32[16,8,768]{2,1,0:T(8,128)}, f32[16,8,768]{2,1,0:T(8,128)}, u32[]{:S(2)}, u32[]{:S(2)}) collective-permute-start(f32[16,8,768]{2,1,0:T(8,128)} %concatenate.289), channel_id=1, source_target_pairs={{0,4},{4,8},{8,12},{12,16},{16,20},{20,24},{24,28},{28,0},{1,5},{5... | collective-permute-start | bytes 1179656 | tf_op jit(solution)/shard_map/ppermute | solution.py:308
  60.8 78.6 %all-to-all-start = ((f32[8,4,96,384]{3,2,1,0:T(8,128)}), f32[8,4,96,384]{3,2,1,0:T(8,128)}, u32[]{:S(2)}, u32[]{:S(2)}) async-start(f32[8,4,96,384]{3,2,1,0:T(8,128)} %shard_map.68), calls=%async_computation | async-start | bytes 9437184 | tf_op jit(solution)/shard_map/all_to_all | solution.py:489
  66.1 8.5 %slice-start.2 = ((s8[4718592]{0:T(1024)(128)(4,1)}), s8[4194304]{0:T(1024)(128)(4,1)S(1)}, s32[]{:S(2)}) async-start(s8[4718592]{0:T(1024)(128)(4,1)} %bitcast.54), calls=%async_computation.4 | async-start | bytes 8388608
  66.2 18.8 %collective-permute-start.3 = (f32[1,98,768]{2,1,0:T(8,128)S(1)}, f32[1,98,768]{2,1,0:T(8,128)S(1)}, u32[]{:S(2)}, u32[]{:S(2)}) collective-permute-start(f32[1,98,768]{2,1,0:T(8,128)S(1)} %get-tuple-element.75), channel_id=1, source_target_pairs={{1,0},{2,1},{3,2},{0,3},{5,4},{6,5},{7,6},{4,7},{9,8},{10,9},{11,1... | collective-permute-start | bytes 903176 | tf_op jit(solution)/shard_map/ppermute | solution.py:308
  69.9 15.1 %collective-permute-start.2 = (f32[1,98,768]{2,1,0:T(8,128)S(1)}, f32[1,98,768]{2,1,0:T(8,128)S(1)}, u32[]{:S(2)}, u32[]{:S(2)}) collective-permute-start(f32[1,98,768]{2,1,0:T(8,128)S(1)} %get-tuple-element.74), channel_id=1, source_target_pairs={{0,1},{1,2},{2,3},{3,0},{4,5},{5,6},{6,7},{7,4},{8,9},{9,10},{10,1... | collective-permute-start | bytes 903176 | tf_op jit(solution)/shard_map/ppermute | solution.py:308
  71.8 2.8 %slice-start.3 = ((s8[4718592]{0:T(1024)(128)(4,1)}), s8[524288]{0:T(1024)(128)(4,1)S(1)}, s32[]{:S(2)}) async-start(s8[4718592]{0:T(1024)(128)(4,1)} %bitcast.54), calls=%async_computation.5 | async-start | bytes 1048576
  71.8 2.8 %copy-start.7 = (f32[16,1,768]{2,1,0:T(1,128)S(1)}, f32[16,1,768]{2,1,0:T(1,128)}, u32[]{:S(2)}) copy-start(f32[16,1,768]{2,1,0:T(1,128)} %slice.533) | copy-start | bytes 147460
  74.6 4.2 %copy-start.8 = (f32[16,1,768]{2,1,0:T(1,128)S(1)}, f32[16,1,768]{2,1,0:T(1,128)}, u32[]{:S(2)}) copy-start(f32[16,1,768]{2,1,0:T(1,128)} %slice.534) | copy-start | bytes 147460
  74.7 10.4 %copy-start = (bf16[3,1,96,768]{3,2,1,0:T(8,128)(2,1)S(1)}, bf16[3,1,96,768]{3,2,1,0:T(8,128)(2,1)}, u32[]{:S(2)}) copy-start(bf16[3,1,96,768]{3,2,1,0:T(8,128)(2,1)} %get-tuple-element.37) | copy-start | bytes 1327108
  74.7 10.4 %copy-start.1 = (bf16[3,1,96,768]{3,2,1,0:T(8,128)(2,1)S(1)}, bf16[3,1,96,768]{3,2,1,0:T(8,128)(2,1)}, u32[]{:S(2)}) copy-start(bf16[3,1,96,768]{3,2,1,0:T(8,128)(2,1)} %get-tuple-element.38) | copy-start | bytes 1327108
  74.7 10.4 %copy-start.5 = (f32[1,96,768]{2,1,0:T(8,128)S(1)}, f32[1,96,768]{2,1,0:T(8,128)}, u32[]{:S(2)}) copy-start(f32[1,96,768]{2,1,0:T(8,128)} %get-tuple-element.54) | copy-start | bytes 884740
  74.7 10.4 %copy-start.6 = (f32[1,96,768]{2,1,0:T(8,128)S(1)}, f32[1,96,768]{2,1,0:T(8,128)}, u32[]{:S(2)}) copy-start(f32[1,96,768]{2,1,0:T(8,128)} %get-tuple-element.55) | copy-start | bytes 884740
  74.7 10.4 %copy-start.9 = (f32[2,96,1]{2,1,0:T(8,128)S(1)}, f32[2,96,1]{2,1,0:T(8,128)}, u32[]{:S(2)}) copy-start(f32[2,96,1]{2,1,0:T(8,128)} %get-tuple-element.84) | copy-start | bytes 2308
  74.7 10.4 %copy-start.10 = (f32[2,96,1]{2,1,0:T(8,128)S(1)}, f32[2,96,1]{2,1,0:T(8,128)}, u32[]{:S(2)}) copy-start(f32[2,96,1]{2,1,0:T(8,128)} %get-tuple-element.85) | copy-start | bytes 2308
  74.7 10.4 %copy-start.11 = (f32[2]{0:T(128)S(1)}, f32[2]{0:T(128)}, u32[]{:S(2)}) copy-start(f32[2]{0:T(128)} %maximum_bitcast_fusion.2) | copy-start | bytes 28
  86.7 11.9 %collective-permute-start.4 = (f32[1,96,768]{2,1,0:T(8,128)S(1)}, f32[1,96,768]{2,1,0:T(8,128)S(1)}, u32[]{:S(2)}, u32[]{:S(2)}) collective-permute-start(f32[1,96,768]{2,1,0:T(8,128)S(1)} %get-tuple-element.82), channel_id=1, source_target_pairs={{0,1},{1,2},{2,3},{3,0},{4,5},{5,6},{6,7},{7,4},{8,9},{9,10},{10,1... | collective-permute-start | bytes 884744 | tf_op jit(solution)/shard_map/ppermute | solution.py:308
  88.4 14.6 %collective-permute-start.5 = (f32[1,96,768]{2,1,0:T(8,128)S(1)}, f32[1,96,768]{2,1,0:T(8,128)S(1)}, u32[]{:S(2)}, u32[]{:S(2)}) collective-permute-start(f32[1,96,768]{2,1,0:T(8,128)S(1)} %get-tuple-element.83), channel_id=1, source_target_pairs={{1,0},{2,1},{3,2},{0,3},{5,4},{6,5},{7,6},{4,7},{9,8},{10,9},{11,1... | collective-permute-start | bytes 884744 | tf_op jit(solution)/shard_map/ppermute | solution.py:308
  162.3 5.0 %collective-permute-start.7 = (f32[16,3,768]{2,1,0:T(4,128)S(1)}, f32[16,3,768]{2,1,0:T(4,128)S(1)}, u32[]{:S(2)}, u32[]{:S(2)}) collective-permute-start(f32[16,3,768]{2,1,0:T(4,128)S(1)} %pad_maximum_fusion.17), channel_id=1, source_target_pairs={{4,0},{8,4},{12,8},{16,12},{20,16},{24,20},{28,24},{0,28},{5,1},{9... | collective-permute-start | bytes 442376 | tf_op jit(solution)/shard_map/ppermute | solution.py:308
  164.2 6.0 %collective-permute-start.6 = (f32[16,3,768]{2,1,0:T(4,128)S(1)}, f32[16,3,768]{2,1,0:T(4,128)S(1)}, u32[]{:S(2)}, u32[]{:S(2)}) collective-permute-start(f32[16,3,768]{2,1,0:T(4,128)S(1)} %pad_maximum_fusion.16), channel_id=1, source_target_pairs={{0,4},{4,8},{8,12},{12,16},{16,20},{20,24},{24,28},{28,0},{1,5},{5... | collective-permute-start | bytes 442376 | tf_op jit(solution)/shard_map/ppermute | solution.py:308
  170.3 63.9 %all-to-all-start.1 = ((f32[8,4,96,384]{3,2,1,0:T(8,128)}), f32[8,4,96,384]{3,2,1,0:T(8,128)}, u32[]{:S(2)}, u32[]{:S(2)}) async-start(f32[8,4,96,384]{3,2,1,0:T(8,128)} %shard_map.69), calls=%async_computation.1 | async-start | bytes 9437184 | tf_op jit(solution)/shard_map/all_to_all | solution.py:489
  175.1 16.7 %collective-permute-start.9 = (f32[1,98,768]{2,1,0:T(8,128)S(1)}, f32[1,98,768]{2,1,0:T(8,128)S(1)}, u32[]{:S(2)}, u32[]{:S(2)}) collective-permute-start(f32[1,98,768]{2,1,0:T(8,128)S(1)} %get-tuple-element.73), channel_id=1, source_target_pairs={{1,0},{2,1},{3,2},{0,3},{5,4},{6,5},{7,6},{4,7},{9,8},{10,9},{11,1... | collective-permute-start | bytes 903176 | tf_op jit(solution)/shard_map/ppermute | solution.py:308
  176.3 15.2 %collective-permute-start.8 = (f32[1,98,768]{2,1,0:T(8,128)S(1)}, f32[1,98,768]{2,1,0:T(8,128)S(1)}, u32[]{:S(2)}, u32[]{:S(2)}) collective-permute-start(f32[1,98,768]{2,1,0:T(8,128)S(1)} %get-tuple-element.72), channel_id=1, source_target_pairs={{0,1},{1,2},{2,3},{3,0},{4,5},{5,6},{6,7},{7,4},{8,9},{9,10},{10,1... | collective-permute-start | bytes 903176 | tf_op jit(solution)/shard_map/ppermute | solution.py:308
  177.5 4.0 %slice-start.4 = ((s8[4718592]{0:T(1024)(128)(4,1)}), s8[4194304]{0:T(1024)(128)(4,1)S(1)}, s32[]{:S(2)}) async-start(s8[4718592]{0:T(1024)(128)(4,1)} %bitcast.56), calls=%async_computation.6 | async-start | bytes 8388608
  177.9 3.7 %slice-start.5 = ((s8[4718592]{0:T(1024)(128)(4,1)}), s8[524288]{0:T(1024)(128)(4,1)S(1)}, s32[]{:S(2)}) async-start(s8[4718592]{0:T(1024)(128)(4,1)} %bitcast.56), calls=%async_computation.7 | async-start | bytes 1048576
  181.5 10.3 %copy-start.2 = (bf16[1,2,96,768]{3,2,1,0:T(8,128)(2,1)S(1)}, bf16[1,2,96,768]{3,2,1,0:T(8,128)(2,1)}, u32[]{:S(2)}) copy-start(bf16[1,2,96,768]{3,2,1,0:T(8,128)(2,1)} %get-tuple-element.27) | copy-start | bytes 884740
  181.5 10.3 %copy-start.3 = (bf16[2,96,768]{2,1,0:T(8,128)(2,1)S(1)}, bf16[2,96,768]{2,1,0:T(8,128)(2,1)}, u32[]{:S(2)}) copy-start(bf16[2,96,768]{2,1,0:T(8,128)(2,1)} %get-tuple-element.28) | copy-start | bytes 884740
  181.5 10.3 %copy-start.4 = (bf16[2,96,768]{2,1,0:T(8,128)(2,1)S(1)}, bf16[2,96,768]{2,1,0:T(8,128)(2,1)}, u32[]{:S(2)}) copy-start(bf16[2,96,768]{2,1,0:T(8,128)(2,1)} %get-tuple-element.29) | copy-start | bytes 884740
  193.2 11.8 %collective-permute-start.10 = (f32[1,96,768]{2,1,0:T(8,128)S(1)}, f32[1,96,768]{2,1,0:T(8,128)S(1)}, u32[]{:S(2)}, u32[]{:S(2)}) collective-permute-start(f32[1,96,768]{2,1,0:T(8,128)S(1)} %get-tuple-element.76), channel_id=1, source_target_pairs={{0,1},{1,2},{2,3},{3,0},{4,5},{5,6},{6,7},{7,4},{8,9},{9,10},{10,1... | collective-permute-start | bytes 884744 | tf_op jit(solution)/shard_map/ppermute | solution.py:308
  194.4 14.5 %collective-permute-start.11 = (f32[1,96,768]{2,1,0:T(8,128)S(1)}, f32[1,96,768]{2,1,0:T(8,128)S(1)}, u32[]{:S(2)}, u32[]{:S(2)}) collective-permute-start(f32[1,96,768]{2,1,0:T(8,128)S(1)} %get-tuple-element.77), channel_id=1, source_target_pairs={{1,0},{2,1},{3,2},{0,3},{5,4},{6,5},{7,6},{4,7},{9,8},{10,9},{11,1... | collective-permute-start | bytes 884744 | tf_op jit(solution)/shard_map/ppermute | solution.py:308

commit v3 on v2

--- a/solution.py
+++ b/solution.py
@@ -186,11 +186,12 @@
 
 
 def lines_kernel(members, par, in_ref, out_ref):
-    plane = pl.program_id(0)
-    rows = in_ref.shape[1]
-    group = out_ref.shape[3] // rows
-    results = solve_lanes(in_ref[0], par, plane)
-    pack_plane(results, out_ref, lax.rem(plane, group), members, rows)
+    group, rows, _ = in_ref.shape
+    for j in range(group):
+        results = solve_lanes(in_ref[j], par, pl.program_id(0) * group + j)
+        whole = jnp.concatenate(results, axis=1)
+        for d in range(members):
+            out_ref[d, 0, :, rows * j : rows * (j + 1)] = whole[:, rows * d : rows * (d + 1)]
 
 
 def received_kernel(keep, par, in_ref, *outs):
@@ -335,8 +336,9 @@
         return jnp.roll(part, -1, 2) - jnp.roll(part, 1, 2)
 
     plane = ends(field, 0)
-    above = jnp.concatenate([field_y[:, :1], field[:, :-1]], 1)[:: field.shape[0] - 1]
-    below = jnp.concatenate([field[:, 1:], field_y[:, 1:]], 1)[:: field.shape[0] - 1]
+    outer = ends(field_y, 0)
+    above = jnp.concatenate([outer[:, :1], plane[:, :-1]], 1)
+    below = jnp.concatenate([plane[:, 1:], outer[:, 1:]], 1)
     before = jnp.concatenate([field_z[:1], field[-2:-1]], 0)
     after = jnp.concatenate([field[1:2], field_z[1:]], 0)
     flux_z = rim_flux(
@@ -369,17 +371,22 @@
     return jnp.concatenate([z_low, z_high], 0), jnp.concatenate(sides, 1)
 
 
+def edge_row(array, member, row):
+    planes, lanes = array.shape[1], array.shape[3]
+    part = lax.slice(array, (member, 0, row, 0), (member + 1, planes, row + 1, lanes))
+    return part.reshape(planes, 1, lanes).astype(jnp.float32)
+
+
 def edge_terms(tensor, grad, root, row):
     scales = (root, root, 1.0)
     terms = []
     for source in range(3):
-        entry = lax.slice_in_dim(tensor[ENTRY[1][source]], row, row + 1, axis=1)
-        entry = entry.astype(jnp.float32)
+        entry = edge_row(tensor, ENTRY[1][source], row)
         if source == 1:
             entry = entry + 1.0
         terms.append(root * scales[source] * entry)
     for source in range(3):
-        terms.append(lax.slice_in_dim(grad[source], row, row + 1, axis=1).astype(jnp.float32))
+        terms.append(edge_row(grad, source, row))
     return terms
 
 
@@ -448,15 +455,15 @@
     planes, rows, lanes = field.shape
     return pl.pallas_call(
         functools.partial(lines_kernel, members),
-        grid=(planes,),
+        grid=(planes // group,),
         out_shape=jax.ShapeDtypeStruct(
             (members, planes // group, rows, group * rows), jnp.float32
         ),
         in_specs=[
             pl.BlockSpec(memory_space=pltpu.SMEM),
-            pl.BlockSpec((1, rows, lanes), lambda k: (k, 0, 0)),
+            pl.BlockSpec((group, rows, lanes), lambda k: (k, 0, 0)),
         ],
-        out_specs=pl.BlockSpec((members, 1, rows, group * rows), lambda k: (0, k // group, 0, 0)),
+        out_specs=pl.BlockSpec((members, 1, rows, group * rows), lambda k: (0, k, 0, 0)),
         compiler_params=pltpu.CompilerParams(vmem_limit_bytes=LIMIT),
         cost_estimate=pl.CostEstimate(
             flops=3072 * field.size, bytes_accessed=8 * field.size, transcendentals=0

time: 246 us -> 211 us (0.86)
  local copies, waits for them, and re-layouts: 54.3 us -> 25.2 us
  waiting for transfers between devices: 30.6 us -> 39.1 us
  other arithmetic: 31.9 us -> 23.7 us
  Pallas kernels: 98.8 us -> 91.7 us
    slice x2 -> x0, local copies, waits for them, and re-layouts: 17.3 us -> none  [flux_rims(): field[:, 1:]]
    ppermute x6, waiting for transfers between devices: 19.2 us -> 27.5 us  [exchange(): lax.ppermute(high_edge, axis, forward)]
    pallas_call x1, Pallas kernels: 18 us -> 10.8 us  [lines_solved(): pl.pallas_call(functools.partial(lines_kernel, members), grid=(planes //...]
    concatenate x4 -> x0, other arithmetic: 6.6 us -> none  [the longest x2 5.71 us: flux_rims(): jnp.concatenate([field[:, 1:], field_y[:, 1:]], 1)[::field.shape[0] - 1]]
    another operation x7, local copies, waits for them, and re-layouts: 7.48 us -> 1.17 us  [local(): par = jnp.stack([plane_rate, root, theta, kappa, wrap, step], 1)]
    squeeze x2 -> x0, local copies, waits for them, and re-layouts: 4.15 us -> none  [the longest x1 3.69 us: edge_terms(): entry = lax.slice_in_dim(tensor[ENTRY[1][source]], row, row + 1, axis=1)]
    slice x8 -> x6, local copies, waits for them, and re-layouts: 5.01 us -> 4.66 us  [across_lanes(): return jnp.roll(part, -1, 2) - jnp.roll(part, 1, 2)]
  transfers between devices with their start and end apart: 14 -> 14, of which waited for: 8 -> 9; matrix products, arithmetic and copies ran while one was open for 25% -> 18% of each run, Pallas kernels for 32% -> 34%
where the time goes in v3:
time: 211 us; the launch traced here: 209 us
  Pallas kernels  91.7 us (43%)
  waiting for transfers between devices  39.1 us (19%)
  starting transfers between devices  28.6 us (14%)
  local copies, waits for them, and re-layouts  25.2 us (12%)
  other arithmetic  23.7 us (11%)
    pallas_call x2, Pallas kernels, stencil(): pl.pallas_call(functools.partial(stencil_kernel, adjoint, members), grid=...  59.9 us
    ppermute x6, waiting for transfers between devices, exchange(): lax.ppermute(high_edge, axis, forward)  27.5 us
    pallas_call x2, Pallas kernels, received_solved(): pl.pallas_call(functools.partial(received_kernel, keep), grid=(groups,),...  21 us
    ppermute x6, starting transfers between devices, exchange(): lax.ppermute(low_edge, axis, backward)  15 us
    ppermute x6, waiting for transfers between devices, exchange(): lax.ppermute(low_edge, axis, backward)  11.7 us
    pallas_call x1, Pallas kernels, lines_solved(): pl.pallas_call(functools.partial(lines_kernel, members), grid=(planes //...  10.8 us
    all_to_all x2, starting transfers between devices, traded(): lax.all_to_all(block, ('gx', 'gy'), split_axis=0, concat_axis=0, tiled=True)  9.24 us
    add x2, other arithmetic, flux_rims(): total = total + coupling_y[side][:, source:source + 1] * vector  4.72 us
  transfers between devices with their start and end apart: 14, of which 9 were waited for; matrix products, arithmetic and copies ran while one was open for 18% of the time, Pallas kernels for 34%

profile of v3, /device:TPU:0, one launch (start us, length us, event | category | flops | bytes accessed | tf_op | source)
XLA Modules:
  0.0 209.3 jit_solution(13852033185208574338)
XLA Ops:
  0.6 0.7 fusion.93
  1.4 1.6 bitcast_convert_fusion
  3.0 1.2 fusion.69
  4.2 1.6 convert_multiply_fusion.5
  5.8 1.2 concatenate.291
  7.0 0.5 collective-permute-start
  7.5 1.2 concatenate.292
  8.7 2.9 %collective-permute-start.1 = (f32[16,8,768]{2,1,0:T(8,128)}, f32[16,8,768]{2,1,0:T(8,128)S(1)}, u32[]{:S(2)}, u32[]{:S(2)}) collective-permute-start(f32[16,8,768]{2,1,0:T(8,128)} %concatenate.292), channel_id=1, source_target_pairs={{4,0},{8,4},{12,8},{16,12},{20,16},{24,20},{28,24},{0,28},{5,1},{9... | collective-permute-start | bytes 1179656 | tf_op jit(solution)/shard_map/ppermute | solution.py:309
  11.6 2.1 %fusion.68 = (f32[1,96,768]{2,1,0:T(8,128)}, f32[1,96,768]{2,1,0:T(8,128)}, f32[1,96,768]{2,1,0:T(8,128)S(1)}, f32[1,96,768]{2,1,0:T(8,128)S(1)}) fusion(f32[16,96,768]{2,1,0:T(8,128)} %rho.1), kind=kLoop, calls=%fused_computation.171 | loop fusion | bytes 2359296 | tf_op jit(solution)/shard_map/slice | solution.py:342
  14.0 0.7 fusion.92
  14.7 1.4 maximum_bitcast_fusion.2
  16.6 0.7 stack.27.par
  17.2 10.8 %shard_map.68 = f32[8,4,96,384]{3,2,1,0:T(8,128)} custom-call(f32[16,6]{1,0:T(8,128)} %stack.27.par, f32[16,96,768]{2,1,0:T(8,128)} %in_ref.1), custom_call_target="tpu_custom_call" | custom-call | flops 3623878656 | bytes 9437184 | tf_op jit(solution)/shard_map/pallas_call | solution.py:456
  28.1 4.6 %all-to-all-start = ((f32[8,4,96,384]{3,2,1,0:T(8,128)}), f32[8,4,96,384]{3,2,1,0:T(8,128)}, u32[]{:S(2)}, u32[]{:S(2)}) async-start(f32[8,4,96,384]{3,2,1,0:T(8,128)} %shard_map.68), calls=%async_computation | async-start | bytes 9437184 | tf_op jit(solution)/shard_map/all_to_all | solution.py:496
  32.8 1.2 fusion.64
  34.0 1.6 fusion.63
  35.6 1.0 slice.507
  36.8 4.4 %collective-permute-start.3 = (f32[1,98,768]{2,1,0:T(8,128)S(1)}, f32[1,98,768]{2,1,0:T(8,128)S(1)}, u32[]{:S(2)}, u32[]{:S(2)}) collective-permute-start(f32[1,98,768]{2,1,0:T(8,128)S(1)} %get-tuple-element.69), channel_id=1, source_target_pairs={{1,0},{2,1},{3,2},{0,3},{5,4},{6,5},{7,6},{4,7},{9,8},{10,9},{11,1... | collective-permute-start | bytes 903176 | tf_op jit(solution)/shard_map/ppermute | solution.py:309
  41.3 0.7 pad_maximum_fusion.14.rho_y
  42.0 1.0 fusion.76
  43.0 1.2 fusion.74
  44.2 1.4 fusion.75
  45.6 10.7 %collective-permute-done.2 = f32[1,98,768]{2,1,0:T(8,128)S(1)} collective-permute-done((f32[1,98,768]{2,1,0:T(8,128)S(1)}, f32[1,98,768]{2,1,0:T(8,128)S(1)}, u32[]{:S(2)}, u32[]{:S(2)}) %collective-permute-start.2) | collective-permute-done | bytes 301088 | tf_op jit(solution)/shard_map/ppermute | solution.py:309
  56.4 1.7 fusion.8
  58.1 1.7 collective-permute-start.4
  59.8 2.2 %collective-permute-start.5 = (f32[1,96,768]{2,1,0:T(8,128)S(1)}, f32[1,96,768]{2,1,0:T(8,128)S(1)}, u32[]{:S(2)}, u32[]{:S(2)}) collective-permute-start(f32[1,96,768]{2,1,0:T(8,128)S(1)} %get-tuple-element.77), channel_id=1, source_target_pairs={{1,0},{2,1},{3,2},{0,3},{5,4},{6,5},{7,6},{4,7},{9,8},{10,9},{11,1... | collective-permute-start | bytes 884744 | tf_op jit(solution)/shard_map/ppermute | solution.py:309
  62.0 1.5 multiply_add_fusion
  63.6 3.2 %multiply_add_fusion.1 = f32[16,1,768]{2,1,0:T(1,128)S(1)} fusion(f32[16,8,768]{2,1,0:T(8,128)} %collective-permute-done, f32[16,96,768]{2,1,0:T(8,128)} %rho.1, f32[16,1,767]{2,1,0:T(1,128)S(1)} %get-tuple-element.87, f32[16,1,1]{2,1,0:T(1,128)S(1)} %get-tuple-element.89, f32[16,1,1]{2,1,0:T(1,128)S(1)} %get-tuple-element.88, ...), kind=kLoop, calls=%fused_computation.148 | loop fusion | flops 258048 | bytes 688128 | tf_op jit(solution)/shard_map/add | solution.py:369
  66.8 0.7 pad_maximum_fusion.16.rim_y
  67.5 0.9 pad_maximum_fusion.2.rho_z
  68.3 1.6 collective-permute-done.4
  69.9 4.5 %collective-permute-done.5 = f32[1,96,768]{2,1,0:T(8,128)S(1)} collective-permute-done((f32[1,96,768]{2,1,0:T(8,128)S(1)}, f32[1,96,768]{2,1,0:T(8,128)S(1)}, u32[]{:S(2)}, u32[]{:S(2)}) %collective-permute-start.5) | collective-permute-done | bytes 294944 | tf_op jit(solution)/shard_map/ppermute | solution.py:309
  74.4 0.9 pad_maximum_fusion.8.rim_z
  75.3 35.4 %shard_map.69 = f32[8,4,96,384]{3,2,1,0:T(8,128)} custom-call(f32[16,6]{1,0:T(8,128)} %stack.27.par, f32[16,96,768]{2,1,0:T(8,128)} %rho.1, f32[2,96,768]{2,1,0:T(8,128)} %pad_maximum_fusion.2.rho_z, f32[16,2,768]{2,1,0:T(2,128)} %pad_maximum_fusion.14.rho_y, bf16[6,16,96,768]{3,2,1,0:T(8,128)(2,1)} %tensor.3, bf16[3,16,96,768]{3,2,1,0:T(8,128)(2,1)} %grad.3, ...), custom_call_target="tpu_custom_call" | custom-call | flops 94371840 | bytes 37748736 | tf_op jit(solution)/shard_map/pallas_call | solution.py:435
  110.7 10.5 %shard_map.70 = (f32[16,96,768]{2,1,0:T(8,128)}, f32[16,96,768]{2,1,0:T(8,128)}) custom-call(f32[16,6]{1,0:T(8,128)} %stack.27.par, f32[8,4,96,384]{3,2,1,0:T(8,128)} %all-to-all-done.in_ref), custom_call_target="tpu_custom_call" | custom-call | flops 3623878656 | bytes 9437184 | tf_op jit(solution)/shard_map/pallas_call | solution.py:479
  121.2 1.2 fusion.66
  122.4 2.2 %fusion.65 = (f32[1,96,768]{2,1,0:T(8,128)}, f32[1,96,768]{2,1,0:T(8,128)}, f32[1,96,768]{2,1,0:T(8,128)S(1)}, f32[1,96,768]{2,1,0:T(8,128)S(1)}) fusion(f32[16,96,768]{2,1,0:T(8,128)} %get-tuple-element.19.rho), kind=kLoop, calls=%fused_computation.168 | loop fusion | bytes 2359296 | tf_op jit(solution)/shard_map/slice | solution.py:342
  124.6 1.2 fusion.67
  125.9 1.7 collective-permute-start.7
  128.0 2.8 %collective-permute-done.7 = f32[16,3,768]{2,1,0:T(4,128)S(1)} collective-permute-done((f32[16,3,768]{2,1,0:T(4,128)S(1)}, f32[16,3,768]{2,1,0:T(4,128)S(1)}, u32[]{:S(2)}, u32[]{:S(2)}) %collective-permute-start.7) | collective-permute-done | bytes 147488 | tf_op jit(solution)/shard_map/ppermute | solution.py:309
  130.8 2.9 %collective-permute-done.6 = f32[16,3,768]{2,1,0:T(4,128)S(1)} collective-permute-done((f32[16,3,768]{2,1,0:T(4,128)S(1)}, f32[16,3,768]{2,1,0:T(4,128)S(1)}, u32[]{:S(2)}, u32[]{:S(2)}) %collective-permute-start.6) | collective-permute-done | bytes 147488 | tf_op jit(solution)/shard_map/ppermute | solution.py:309
  133.7 0.7 copy-done.7
  134.3 4.6 %all-to-all-start.1 = ((f32[8,4,96,384]{3,2,1,0:T(8,128)}), f32[8,4,96,384]{3,2,1,0:T(8,128)}, u32[]{:S(2)}, u32[]{:S(2)}) async-start(f32[8,4,96,384]{3,2,1,0:T(8,128)} %shard_map.69), calls=%async_computation.1 | async-start | bytes 9437184 | tf_op jit(solution)/shard_map/all_to_all | solution.py:496
  139.1 1.1 slice.579
  140.4 1.1 collective-permute-start.9
  141.5 1.0 collective-permute-start.8
  142.5 0.7 pad_maximum_fusion.15.rho_y
  143.2 0.9 fusion.87
  144.1 1.1 fusion.88
  145.3 1.2 fusion.86
  146.7 10.0 %collective-permute-done.8 = f32[1,98,768]{2,1,0:T(8,128)S(1)} collective-permute-done((f32[1,98,768]{2,1,0:T(8,128)S(1)}, f32[1,98,768]{2,1,0:T(8,128)S(1)}, u32[]{:S(2)}, u32[]{:S(2)}) %collective-permute-start.8) | collective-permute-done | bytes 301088 | tf_op jit(solution)/shard_map/ppermute | solution.py:309
  157.1 0.5 fusion.3
  157.7 1.2 collective-permute-start.10
  158.9 2.7 %collective-permute-start.11 = (f32[1,96,768]{2,1,0:T(8,128)S(1)}, f32[1,96,768]{2,1,0:T(8,128)S(1)}, u32[]{:S(2)}, u32[]{:S(2)}) collective-permute-start(f32[1,96,768]{2,1,0:T(8,128)S(1)} %get-tuple-element.71), channel_id=1, source_target_pairs={{1,0},{2,1},{3,2},{0,3},{5,4},{6,5},{7,6},{4,7},{9,8},{10,9},{11,1... | collective-permute-start | bytes 884744 | tf_op jit(solution)/shard_map/ppermute | solution.py:309
  161.6 1.9 fusion.84
  163.5 1.4 fusion.85
  164.9 0.7 pad_maximum_fusion.18.rest_1_
  165.6 0.7 pad_maximum_fusion.17.rim_y
  166.4 0.9 pad_maximum_fusion.5.rho_z
  167.3 2.3 %collective-permute-done.10 = f32[1,96,768]{2,1,0:T(8,128)S(1)} collective-permute-done((f32[1,96,768]{2,1,0:T(8,128)S(1)}, f32[1,96,768]{2,1,0:T(8,128)S(1)}, u32[]{:S(2)}, u32[]{:S(2)}) %collective-permute-start.10) | collective-permute-done | bytes 294944 | tf_op jit(solution)/shard_map/ppermute | solution.py:309
  169.6 3.9 %collective-permute-done.11 = f32[1,96,768]{2,1,0:T(8,128)S(1)} collective-permute-done((f32[1,96,768]{2,1,0:T(8,128)S(1)}, f32[1,96,768]{2,1,0:T(8,128)S(1)}, u32[]{:S(2)}, u32[]{:S(2)}) %collective-permute-start.11) | collective-permute-done | bytes 294944 | tf_op jit(solution)/shard_map/ppermute | solution.py:309
  173.5 0.9 pad_maximum_fusion.9.rim_z
  174.3 24.5 %shard_map.71 = f32[16,96,768]{2,1,0:T(8,128)} custom-call(f32[16,6]{1,0:T(8,128)} %stack.27.par, f32[16,96,768]{2,1,0:T(8,128)} %get-tuple-element.19.rho, f32[2,96,768]{2,1,0:T(8,128)} %pad_maximum_fusion.5.rho_z, f32[16,2,768]{2,1,0:T(2,128)} %pad_maximum_fusion.15.rho_y, bf16[6,16,96,768]{3,2,1,0:T(8,128)(2,1)} %tensor.3, bf16[3,16,96,768]{3,2,1,0:T(8,128)(2,1)} %grad.3, ...), custom_call_target="tpu_custom_call" | custom-call | flops 94371840 | bytes 37748736 | tf_op jit(solution)/shard_map/pallas_call | solution.py:435
  198.8 10.5 %shard_map.72 = f32[16,96,768]{2,1,0:T(8,128)} custom-call(f32[16,6]{1,0:T(8,128)} %stack.27.par, f32[8,4,96,384]{3,2,1,0:T(8,128)} %all-to-all-done.1.in_ref), custom_call_target="tpu_custom_call" | custom-call | flops 3623878656 | bytes 9437184 | tf_op jit(solution)/shard_map/pallas_call | solution.py:479
  (65 shorter events, 2.7 us)
Async XLA Ops:
  0.6 15.8 %copy-start.9 = (f32[16]{0:T(128)S(1)}, f32[16]{0:T(128)}, u32[]{:S(2)}) copy-start(f32[16]{0:T(128)} %param.8) | copy-start | bytes 196
  7.0 21.0 %collective-permute-start = (f32[16,8,768]{2,1,0:T(8,128)}, f32[16,8,768]{2,1,0:T(8,128)}, u32[]{:S(2)}, u32[]{:S(2)}) collective-permute-start(f32[16,8,768]{2,1,0:T(8,128)} %concatenate.291), channel_id=1, source_target_pairs={{0,4},{4,8},{8,12},{12,16},{16,20},{20,24},{24,28},{28,0},{1,5},{5... | collective-permute-start | bytes 1179656 | tf_op jit(solution)/shard_map/ppermute | solution.py:309
  8.7 19.4 %collective-permute-start.1 = (f32[16,8,768]{2,1,0:T(8,128)}, f32[16,8,768]{2,1,0:T(8,128)S(1)}, u32[]{:S(2)}, u32[]{:S(2)}) collective-permute-start(f32[16,8,768]{2,1,0:T(8,128)} %concatenate.292), channel_id=1, source_target_pairs={{4,0},{8,4},{12,8},{16,12},{20,16},{24,20},{28,24},{0,28},{5,1},{9... | collective-permute-start | bytes 1179656 | tf_op jit(solution)/shard_map/ppermute | solution.py:309
  28.1 82.7 %all-to-all-start = ((f32[8,4,96,384]{3,2,1,0:T(8,128)}), f32[8,4,96,384]{3,2,1,0:T(8,128)}, u32[]{:S(2)}, u32[]{:S(2)}) async-start(f32[8,4,96,384]{3,2,1,0:T(8,128)} %shard_map.68), calls=%async_computation | async-start | bytes 9437184 | tf_op jit(solution)/shard_map/all_to_all | solution.py:496
  34.0 22.4 %copy-start.3 = (f32[1,96,768]{2,1,0:T(8,128)S(1)}, f32[1,96,768]{2,1,0:T(8,128)}, u32[]{:S(2)}) copy-start(f32[1,96,768]{2,1,0:T(8,128)} %get-tuple-element.60) | copy-start | bytes 884740
  34.0 22.4 %copy-start.4 = (f32[1,96,768]{2,1,0:T(8,128)S(1)}, f32[1,96,768]{2,1,0:T(8,128)}, u32[]{:S(2)}) copy-start(f32[1,96,768]{2,1,0:T(8,128)} %get-tuple-element.61) | copy-start | bytes 884740
  36.8 19.5 %collective-permute-start.3 = (f32[1,98,768]{2,1,0:T(8,128)S(1)}, f32[1,98,768]{2,1,0:T(8,128)S(1)}, u32[]{:S(2)}, u32[]{:S(2)}) collective-permute-start(f32[1,98,768]{2,1,0:T(8,128)S(1)} %get-tuple-element.69), channel_id=1, source_target_pairs={{1,0},{2,1},{3,2},{0,3},{5,4},{6,5},{7,6},{4,7},{9,8},{10,9},{11,1... | collective-permute-start | bytes 903176 | tf_op jit(solution)/shard_map/ppermute | solution.py:309
  41.3 15.1 %collective-permute-start.2 = (f32[1,98,768]{2,1,0:T(8,128)S(1)}, f32[1,98,768]{2,1,0:T(8,128)S(1)}, u32[]{:S(2)}, u32[]{:S(2)}) collective-permute-start(f32[1,98,768]{2,1,0:T(8,128)S(1)} %get-tuple-element.68), channel_id=1, source_target_pairs={{0,1},{1,2},{2,3},{3,0},{4,5},{5,6},{6,7},{7,4},{8,9},{9,10},{10,1... | collective-permute-start | bytes 903176 | tf_op jit(solution)/shard_map/ppermute | solution.py:309
  58.1 11.8 %collective-permute-start.4 = (f32[1,96,768]{2,1,0:T(8,128)S(1)}, f32[1,96,768]{2,1,0:T(8,128)S(1)}, u32[]{:S(2)}, u32[]{:S(2)}) collective-permute-start(f32[1,96,768]{2,1,0:T(8,128)S(1)} %get-tuple-element.76), channel_id=1, source_target_pairs={{0,1},{1,2},{2,3},{3,0},{4,5},{5,6},{6,7},{7,4},{8,9},{9,10},{10,1... | collective-permute-start | bytes 884744 | tf_op jit(solution)/shard_map/ppermute | solution.py:309
  59.8 14.6 %collective-permute-start.5 = (f32[1,96,768]{2,1,0:T(8,128)S(1)}, f32[1,96,768]{2,1,0:T(8,128)S(1)}, u32[]{:S(2)}, u32[]{:S(2)}) collective-permute-start(f32[1,96,768]{2,1,0:T(8,128)S(1)} %get-tuple-element.77), channel_id=1, source_target_pairs={{1,0},{2,1},{3,2},{0,3},{5,4},{6,5},{7,6},{4,7},{9,8},{10,9},{11,1... | collective-permute-start | bytes 884744 | tf_op jit(solution)/shard_map/ppermute | solution.py:309
  125.9 4.9 %collective-permute-start.7 = (f32[16,3,768]{2,1,0:T(4,128)S(1)}, f32[16,3,768]{2,1,0:T(4,128)S(1)}, u32[]{:S(2)}, u32[]{:S(2)}) collective-permute-start(f32[16,3,768]{2,1,0:T(4,128)S(1)} %pad_maximum_fusion.13), channel_id=1, source_target_pairs={{4,0},{8,4},{12,8},{16,12},{20,16},{24,20},{28,24},{0,28},{5,1},{9... | collective-permute-start | bytes 442376 | tf_op jit(solution)/shard_map/ppermute | solution.py:309
  127.6 6.0 %collective-permute-start.6 = (f32[16,3,768]{2,1,0:T(4,128)S(1)}, f32[16,3,768]{2,1,0:T(4,128)S(1)}, u32[]{:S(2)}, u32[]{:S(2)}) collective-permute-start(f32[16,3,768]{2,1,0:T(4,128)S(1)} %pad_maximum_fusion.12), channel_id=1, source_target_pairs={{0,4},{4,8},{8,12},{12,16},{16,20},{20,24},{24,28},{28,0},{1,5},{5... | collective-permute-start | bytes 442376 | tf_op jit(solution)/shard_map/ppermute | solution.py:309
  133.7 0.7 copy-start.7
  134.3 64.5 %all-to-all-start.1 = ((f32[8,4,96,384]{3,2,1,0:T(8,128)}), f32[8,4,96,384]{3,2,1,0:T(8,128)}, u32[]{:S(2)}, u32[]{:S(2)}) async-start(f32[8,4,96,384]{3,2,1,0:T(8,128)} %shard_map.69), calls=%async_computation.1 | async-start | bytes 9437184 | tf_op jit(solution)/shard_map/all_to_all | solution.py:496
  139.0 18.1 %copy-start = (bf16[1,2,96,768]{3,2,1,0:T(8,128)(2,1)S(1)}, bf16[1,2,96,768]{3,2,1,0:T(8,128)(2,1)}, u32[]{:S(2)}) copy-start(bf16[1,2,96,768]{3,2,1,0:T(8,128)(2,1)} %get-tuple-element.27) | copy-start | bytes 884740
  139.0 18.1 %copy-start.1 = (bf16[2,96,768]{2,1,0:T(8,128)(2,1)S(1)}, bf16[2,96,768]{2,1,0:T(8,128)(2,1)}, u32[]{:S(2)}) copy-start(bf16[2,96,768]{2,1,0:T(8,128)(2,1)} %get-tuple-element.28) | copy-start | bytes 884740
  139.0 18.1 %copy-start.2 = (bf16[2,96,768]{2,1,0:T(8,128)(2,1)S(1)}, bf16[2,96,768]{2,1,0:T(8,128)(2,1)}, u32[]{:S(2)}) copy-start(bf16[2,96,768]{2,1,0:T(8,128)(2,1)} %get-tuple-element.29) | copy-start | bytes 884740
  139.0 18.1 %copy-start.5 = (f32[1,96,768]{2,1,0:T(8,128)S(1)}, f32[1,96,768]{2,1,0:T(8,128)}, u32[]{:S(2)}) copy-start(f32[1,96,768]{2,1,0:T(8,128)} %get-tuple-element.52) | copy-start | bytes 884740
  139.0 18.1 %copy-start.6 = (f32[1,96,768]{2,1,0:T(8,128)S(1)}, f32[1,96,768]{2,1,0:T(8,128)}, u32[]{:S(2)}) copy-start(f32[1,96,768]{2,1,0:T(8,128)} %get-tuple-element.53) | copy-start | bytes 884740
  140.3 21.3 %copy-start.8 = (f32[16,3,768]{2,1,0:T(4,128)S(1)}, f32[16,3,768]{2,1,0:T(4,128)}, u32[]{:S(2)}) copy-start(f32[16,3,768]{2,1,0:T(4,128)} %copy-done.7) | copy-start | bytes 442372
  140.4 16.7 %collective-permute-start.9 = (f32[1,98,768]{2,1,0:T(8,128)S(1)}, f32[1,98,768]{2,1,0:T(8,128)S(1)}, u32[]{:S(2)}, u32[]{:S(2)}) collective-permute-start(f32[1,98,768]{2,1,0:T(8,128)S(1)} %get-tuple-element.67), channel_id=1, source_target_pairs={{1,0},{2,1},{3,2},{0,3},{5,4},{6,5},{7,6},{4,7},{9,8},{10,9},{11,1... | collective-permute-start | bytes 903176 | tf_op jit(solution)/shard_map/ppermute | solution.py:309
  141.5 15.2 %collective-permute-start.8 = (f32[1,98,768]{2,1,0:T(8,128)S(1)}, f32[1,98,768]{2,1,0:T(8,128)S(1)}, u32[]{:S(2)}, u32[]{:S(2)}) collective-permute-start(f32[1,98,768]{2,1,0:T(8,128)S(1)} %get-tuple-element.66), channel_id=1, source_target_pairs={{0,1},{1,2},{2,3},{3,0},{4,5},{5,6},{6,7},{7,4},{8,9},{9,10},{10,1... | collective-permute-start | bytes 903176 | tf_op jit(solution)/shard_map/ppermute | solution.py:309
  157.7 11.8 %collective-permute-start.10 = (f32[1,96,768]{2,1,0:T(8,128)S(1)}, f32[1,96,768]{2,1,0:T(8,128)S(1)}, u32[]{:S(2)}, u32[]{:S(2)}) collective-permute-start(f32[1,96,768]{2,1,0:T(8,128)S(1)} %get-tuple-element.70), channel_id=1, source_target_pairs={{0,1},{1,2},{2,3},{3,0},{4,5},{5,6},{6,7},{7,4},{8,9},{9,10},{10,1... | collective-permute-start | bytes 884744 | tf_op jit(solution)/shard_map/ppermute | solution.py:309
  158.9 14.6 %collective-permute-start.11 = (f32[1,96,768]{2,1,0:T(8,128)S(1)}, f32[1,96,768]{2,1,0:T(8,128)S(1)}, u32[]{:S(2)}, u32[]{:S(2)}) collective-permute-start(f32[1,96,768]{2,1,0:T(8,128)S(1)} %get-tuple-element.71), channel_id=1, source_target_pairs={{1,0},{2,1},{3,2},{0,3},{5,4},{6,5},{7,6},{4,7},{9,8},{10,9},{11,1... | collective-permute-start | bytes 884744 | tf_op jit(solution)/shard_map/ppermute | solution.py:309

commit v4 on v3

--- a/solution.py
+++ b/solution.py
@@ -396,13 +396,11 @@
 
 
 def stencil(
-    adjoint, members, group, par, root, field, field_y, outer_y, coupling_y, drift_y, tensor, grad, extra=()
+    adjoint, members, group, par, root, field, field_z, field_y, outer_y, coupling_y, drift_y, tensor, grad, extra=()
 ):
     planes, rows, lanes = field.shape
-    taller = jnp.concatenate([ends(field, 0), ends(field_y, 0)], 1)
-    low, high = exchange(taller[:1], taller[1:], "ga")
-    field_z = jnp.concatenate([low[:, :rows], high[:, :rows]], 0)
-    field_z_y = jnp.concatenate([low[:, rows:], high[:, rows:]], 0)
+    low, high = exchange(field_y[:1], field_y[-1:], "ga")
+    field_z_y = jnp.concatenate([low, high], 0)
     rim_z, rim_y = flux_rims(
         field, field_z, field_y, field_z_y, outer_y, coupling_y, drift_y, tensor, grad, root, adjoint
     )
@@ -516,7 +514,8 @@
         ("gx", "gy"),
     )
     swept = lines_solved(members, group, par, cotangent)
-    swept, low, high = lax.optimization_barrier((swept, low, high))
+    z_low, z_high = exchange(density[:1], density[-1:], "ga")
+    swept, low, high, z_low, z_high = lax.optimization_barrier((swept, low, high, z_low, z_high))
     swept = traded(swept)
     coupling_y = (low[:, 2:5], high[:, 2:5])
     drift_y = (low[:, 5:8], high[:, 5:8])
@@ -527,6 +526,7 @@
         par,
         root,
         density,
+        jnp.concatenate([z_low, z_high], 0),
         jnp.concatenate([low[:, 1:2], high[:, :1]], 1),
         jnp.concatenate([low[:, :1], high[:, 1:2]], 1),
         coupling_y,
@@ -541,7 +541,8 @@
         jnp.concatenate([settled[:, -2:], returned[:, -1:]], 1),
         ("gx", "gy"),
     )
-    packed, low, high = lax.optimization_barrier((packed, low, high))
+    z_low, z_high = exchange(settled[:1], settled[-1:], "ga")
+    packed, low, high, z_low, z_high = lax.optimization_barrier((packed, low, high, z_low, z_high))
     moved = traded(packed)
     adjoint_density = stencil(
         True,
@@ -550,6 +551,7 @@
         par,
         root,
         settled,
+        jnp.concatenate([z_low, z_high], 0),
         jnp.concatenate([low[:, 1:2], high[:, :1]], 1),
         jnp.concatenate([low[:, :1], high[:, 1:2]], 1),
         coupling_y,

time: 211 us -> 194 us (0.919)
  waiting for transfers between devices: 39.1 us -> 28.7 us
  local copies, waits for them, and re-layouts: 25.2 us -> 15.8 us
  starting transfers between devices: 28.6 us -> 35 us
  other arithmetic: 23.7 us -> 20.5 us
    ppermute x6 -> x8, waiting for transfers between devices: 27.5 us -> 10.8 us  [exchange(): lax.ppermute(high_edge, axis, forward)]
    ppermute x6 -> x8, starting transfers between devices: 15 us -> 20 us  [exchange(): lax.ppermute(low_edge, axis, backward)]
    all_to_all x2, waiting for transfers between devices: 0.01 us -> 4.4 us  [traded(): lax.all_to_all(block, ('gx', 'gy'), split_axis=0, concat_axis=0, tiled=True)]
    slice x6, local copies, waits for them, and re-layouts: 4.66 us -> 0.89 us  [across_lanes(): return jnp.roll(part, -1, 2) - jnp.roll(part, 1, 2)]
    slice x5, local copies, waits for them, and re-layouts: 2.4 us -> 0.23 us  [flux_rims(): after = jnp.concatenate([row[1:], corner[1:]], 0)]
    ppermute x6 -> x8, waiting for transfers between devices: 11.7 us -> 13.6 us  [exchange(): lax.ppermute(low_edge, axis, backward)]
    ppermute x6 -> x8, starting transfers between devices: 4.35 us -> 5.77 us  [exchange(): lax.ppermute(high_edge, axis, forward)]
  transfers between devices with their start and end apart: 14 -> 18, of which waited for: 9 -> 8; matrix products, arithmetic and copies ran while one was open for 18% -> 14% of each run, Pallas kernels for 34% -> 37%
where the time goes in v4:
time: 194 us; the launch traced here: 193 us
  Pallas kernels  91.7 us (47%)
  starting transfers between devices  35 us (18%)
  waiting for transfers between devices  28.7 us (15%)
  other arithmetic  20.5 us (11%)
  local copies, waits for them, and re-layouts  15.8 us (8%)
    pallas_call x2, Pallas kernels, stencil(): pl.pallas_call(functools.partial(stencil_kernel, adjoint, members), grid=...  59.9 us
    pallas_call x2, Pallas kernels, received_solved(): pl.pallas_call(functools.partial(received_kernel, keep), grid=(groups,),...  21 us
    ppermute x8, starting transfers between devices, exchange(): lax.ppermute(low_edge, axis, backward)  20 us
    ppermute x8, waiting for transfers between devices, exchange(): lax.ppermute(low_edge, axis, backward)  13.6 us
    pallas_call x1, Pallas kernels, lines_solved(): pl.pallas_call(functools.partial(lines_kernel, members), grid=(planes //...  10.8 us
    ppermute x8, waiting for transfers between devices, exchange(): lax.ppermute(high_edge, axis, forward)  10.8 us
    all_to_all x2, starting transfers between devices, traded(): lax.all_to_all(block, ('gx', 'gy'), split_axis=0, concat_axis=0, tiled=True)  9.24 us
    ppermute x8, starting transfers between devices, exchange(): lax.ppermute(high_edge, axis, forward)  5.77 us
  transfers between devices with their start and end apart: 18, of which 8 were waited for; matrix products, arithmetic and copies ran while one was open for 14% of the time, Pallas kernels for 37%

profile of v4, /device:TPU:0, one launch (start us, length us, event | category | flops | bytes accessed | tf_op | source)
XLA Modules:
  0.0 192.6 jit_solution(257145512100089019)
XLA Ops:
  0.6 0.7 fusion.91
  1.4 1.6 bitcast_convert_fusion
  3.0 1.2 fusion.69
  4.2 1.6 convert_multiply_fusion.5
  5.8 0.6 concatenate.280
  6.4 0.5 collective-permute-start
  6.9 0.6 concatenate.281
  7.5 3.0 %collective-permute-start.1 = (f32[16,8,768]{2,1,0:T(8,128)S(1)}, f32[16,8,768]{2,1,0:T(8,128)S(1)}, u32[]{:S(2)}, u32[]{:S(2)}) collective-permute-start(f32[16,8,768]{2,1,0:T(8,128)S(1)} %concatenate.281), channel_id=1, source_target_pairs={{4,0},{8,4},{12,8},{16,12},{20,16},{24,20},{28,24},{0,28},{5,1},{9... | collective-permute-start | bytes 1179656 | tf_op jit(solution)/shard_map/ppermute | solution.py:309
  10.4 1.3 fusion.68
  11.7 2.4 %collective-permute-start.2 = (f32[1,96,768]{2,1,0:T(8,128)S(1)}, f32[1,96,768]{2,1,0:T(8,128)S(1)}, u32[]{:S(2)}, u32[]{:S(2)}) collective-permute-start(f32[1,96,768]{2,1,0:T(8,128)S(1)} %get-tuple-element.71), channel_id=1, source_target_pairs={{0,1},{1,2},{2,3},{3,0},{4,5},{5,6},{6,7},{7,4},{8,9},{9,10},{10,1... | collective-permute-start | bytes 884744 | tf_op jit(solution)/shard_map/ppermute | solution.py:309
  14.1 2.1 %collective-permute-start.3 = (f32[1,96,768]{2,1,0:T(8,128)S(1)}, f32[1,96,768]{2,1,0:T(8,128)S(1)}, u32[]{:S(2)}, u32[]{:S(2)}) collective-permute-start(f32[1,96,768]{2,1,0:T(8,128)S(1)} %get-tuple-element.70), channel_id=1, source_target_pairs={{1,0},{2,1},{3,2},{0,3},{5,4},{6,5},{7,6},{4,7},{9,8},{10,9},{11,1... | collective-permute-start | bytes 884744 | tf_op jit(solution)/shard_map/ppermute | solution.py:309
  16.2 0.6 fusion.90
  17.3 0.7 stack.27.par
  18.0 10.8 %shard_map.68 = f32[8,4,96,384]{3,2,1,0:T(8,128)} custom-call(f32[16,6]{1,0:T(8,128)} %stack.27.par, f32[16,96,768]{2,1,0:T(8,128)} %in_ref.1), custom_call_target="tpu_custom_call" | custom-call | flops 3623878656 | bytes 9437184 | tf_op jit(solution)/shard_map/pallas_call | solution.py:454
  28.8 4.6 %all-to-all-start = ((f32[8,4,96,384]{3,2,1,0:T(8,128)}), f32[8,4,96,384]{3,2,1,0:T(8,128)}, u32[]{:S(2)}, u32[]{:S(2)}) async-start(f32[8,4,96,384]{3,2,1,0:T(8,128)} %shard_map.68), calls=%async_computation | async-start | bytes 9437184 | tf_op jit(solution)/shard_map/all_to_all | solution.py:494
  33.5 1.3 maximum_bitcast_fusion.2
  35.0 0.2 fusion.13
  35.2 1.2 fusion.64
  36.4 1.6 fusion.63
  38.1 2.0 %collective-permute-start.6 = (f32[1,2,768]{2,1,0:T(2,128)S(1)}, f32[1,2,768]{2,1,0:T(2,128)S(1)}, u32[]{:S(2)}, u32[]{:S(2)}) collective-permute-start(f32[1,2,768]{2,1,0:T(2,128)S(1)} %get-tuple-element.118), channel_id=1, source_target_pairs={{1,0},{2,1},{3,2},{0,3},{5,4},{6,5},{7,6},{4,7},{9,8},{10,9},{11,1... | collective-permute-start | bytes 18440 | tf_op jit(solution)/shard_map/ppermute | solution.py:309
  40.2 0.9 pad_maximum_fusion.2.rho_z
  41.2 0.7 fusion.8
  42.0 0.3 fusion.73
  42.3 0.7 pad_maximum_fusion.14.rho_y
  43.1 0.4 collective-permute-start.4
  43.4 3.5 %collective-permute-start.5 = (f32[1,96,768]{2,1,0:T(8,128)S(1)}, f32[1,96,768]{2,1,0:T(8,128)S(1)}, u32[]{:S(2)}, u32[]{:S(2)}) collective-permute-start(f32[1,96,768]{2,1,0:T(8,128)S(1)} %get-tuple-element.81), channel_id=1, source_target_pairs={{1,0},{2,1},{3,2},{0,3},{5,4},{6,5},{7,6},{4,7},{9,8},{10,9},{11,1... | collective-permute-start | bytes 884744 | tf_op jit(solution)/shard_map/ppermute | solution.py:309
  46.9 1.5 multiply_add_fusion
  48.5 1.5 multiply_add_fusion.1
  50.0 0.7 pad_maximum_fusion.16.rim_y
  50.7 4.1 %collective-permute-done.4 = f32[1,96,768]{2,1,0:T(8,128)S(1)} collective-permute-done((f32[1,96,768]{2,1,0:T(8,128)S(1)}, f32[1,96,768]{2,1,0:T(8,128)S(1)}, u32[]{:S(2)}, u32[]{:S(2)}) %collective-permute-start.4) | collective-permute-done | bytes 294944 | tf_op jit(solution)/shard_map/ppermute | solution.py:309
  54.8 3.5 %collective-permute-done.5 = f32[1,96,768]{2,1,0:T(8,128)S(1)} collective-permute-done((f32[1,96,768]{2,1,0:T(8,128)S(1)}, f32[1,96,768]{2,1,0:T(8,128)S(1)}, u32[]{:S(2)}, u32[]{:S(2)}) %collective-permute-start.5) | collective-permute-done | bytes 294944 | tf_op jit(solution)/shard_map/ppermute | solution.py:309
  58.3 0.9 pad_maximum_fusion.8.rim_z
  59.2 35.4 %shard_map.69 = f32[8,4,96,384]{3,2,1,0:T(8,128)} custom-call(f32[16,6]{1,0:T(8,128)} %stack.27.par, f32[16,96,768]{2,1,0:T(8,128)} %rho.1, f32[2,96,768]{2,1,0:T(8,128)} %pad_maximum_fusion.2.rho_z, f32[16,2,768]{2,1,0:T(2,128)} %pad_maximum_fusion.14.rho_y, bf16[6,16,96,768]{3,2,1,0:T(8,128)(2,1)} %tensor.3, bf16[3,16,96,768]{3,2,1,0:T(8,128)(2,1)} %grad.3, ...), custom_call_target="tpu_custom_call" | custom-call | flops 94371840 | bytes 37748736 | tf_op jit(solution)/shard_map/pallas_call | solution.py:433
  94.6 10.5 %shard_map.70 = (f32[16,96,768]{2,1,0:T(8,128)}, f32[16,96,768]{2,1,0:T(8,128)}) custom-call(f32[16,6]{1,0:T(8,128)} %stack.27.par, f32[8,4,96,384]{3,2,1,0:T(8,128)} %all-to-all-done.in_ref), custom_call_target="tpu_custom_call" | custom-call | flops 3623878656 | bytes 9437184 | tf_op jit(solution)/shard_map/pallas_call | solution.py:477
  105.1 1.3 fusion.65
  106.4 1.2 fusion.66
  107.6 2.4 %collective-permute-start.10 = (f32[1,96,768]{2,1,0:T(8,128)S(1)}, f32[1,96,768]{2,1,0:T(8,128)S(1)}, u32[]{:S(2)}, u32[]{:S(2)}) collective-permute-start(f32[1,96,768]{2,1,0:T(8,128)S(1)} %get-tuple-element.63), channel_id=1, source_target_pairs={{0,1},{1,2},{2,3},{3,0},{4,5},{5,6},{6,7},{7,4},{8,9},{9,10},{10,1... | collective-permute-start | bytes 884744 | tf_op jit(solution)/shard_map/ppermute | solution.py:309
  110.0 1.5 collective-permute-start.11
  111.5 1.2 fusion.67
  112.8 0.6 collective-permute-start.9
  113.6 3.0 %collective-permute-done.9 = f32[16,3,768]{2,1,0:T(4,128)S(1)} collective-permute-done((f32[16,3,768]{2,1,0:T(4,128)S(1)}, f32[16,3,768]{2,1,0:T(4,128)S(1)}, u32[]{:S(2)}, u32[]{:S(2)}) %collective-permute-start.9) | collective-permute-done | bytes 147488 | tf_op jit(solution)/shard_map/ppermute | solution.py:309
  116.6 3.1 %collective-permute-done.8 = f32[16,3,768]{2,1,0:T(4,128)S(1)} collective-permute-done((f32[16,3,768]{2,1,0:T(4,128)S(1)}, f32[16,3,768]{2,1,0:T(4,128)S(1)}, u32[]{:S(2)}, u32[]{:S(2)}) %collective-permute-start.8) | collective-permute-done | bytes 147488 | tf_op jit(solution)/shard_map/ppermute | solution.py:309
  119.7 0.7 copy-done.2
  120.3 3.4 %collective-permute-done.11 = f32[1,96,768]{2,1,0:T(8,128)S(1)} collective-permute-done((f32[1,96,768]{2,1,0:T(8,128)S(1)}, f32[1,96,768]{2,1,0:T(8,128)S(1)}, u32[]{:S(2)}, u32[]{:S(2)}) %collective-permute-start.11) | collective-permute-done | bytes 294944 | tf_op jit(solution)/shard_map/ppermute | solution.py:309
  123.7 4.6 %all-to-all-start.1 = ((f32[8,4,96,384]{3,2,1,0:T(8,128)}), f32[8,4,96,384]{3,2,1,0:T(8,128)}, u32[]{:S(2)}, u32[]{:S(2)}) async-start(f32[8,4,96,384]{3,2,1,0:T(8,128)} %shard_map.69), calls=%async_computation.1 | async-start | bytes 9437184 | tf_op jit(solution)/shard_map/all_to_all | solution.py:494
  128.5 0.2 fusion.11
  128.8 1.0 slice.539
  129.7 1.0 slice.540
  130.7 3.5 %collective-permute-start.14 = (f32[1,2,768]{2,1,0:T(2,128)S(1)}, f32[1,2,768]{2,1,0:T(2,128)S(1)}, u32[]{:S(2)}, u32[]{:S(2)}) collective-permute-start(f32[1,2,768]{2,1,0:T(2,128)S(1)} %get-tuple-element.116), channel_id=1, source_target_pairs={{1,0},{2,1},{3,2},{0,3},{5,4},{6,5},{7,6},{4,7},{9,8},{10,9},{11,1... | collective-permute-start | bytes 18440 | tf_op jit(solution)/shard_map/ppermute | solution.py:309
  134.3 0.9 pad_maximum_fusion.5.rho_z
  135.4 0.2 fusion.80
  135.8 0.5 fusion.3
  136.4 0.7 pad_maximum_fusion.15.rho_y
  137.1 3.8 %collective-permute-start.13 = (f32[1,96,768]{2,1,0:T(8,128)S(1)}, f32[1,96,768]{2,1,0:T(8,128)S(1)}, u32[]{:S(2)}, u32[]{:S(2)}) collective-permute-start(f32[1,96,768]{2,1,0:T(8,128)S(1)} %get-tuple-element.75), channel_id=1, source_target_pairs={{1,0},{2,1},{3,2},{0,3},{5,4},{6,5},{7,6},{4,7},{9,8},{10,9},{11,1... | collective-permute-start | bytes 884744 | tf_op jit(solution)/shard_map/ppermute | solution.py:309
  141.0 1.4 fusion.78
  142.4 1.4 fusion.79
  143.8 0.7 pad_maximum_fusion.18.rest_1_
  144.5 0.7 pad_maximum_fusion.17.rim_y
  145.2 3.6 %collective-permute-done.12 = f32[1,96,768]{2,1,0:T(8,128)S(1)} collective-permute-done((f32[1,96,768]{2,1,0:T(8,128)S(1)}, f32[1,96,768]{2,1,0:T(8,128)S(1)}, u32[]{:S(2)}, u32[]{:S(2)}) %collective-permute-start.12) | collective-permute-done | bytes 294944 | tf_op jit(solution)/shard_map/ppermute | solution.py:309
  148.8 3.6 %collective-permute-done.13 = f32[1,96,768]{2,1,0:T(8,128)S(1)} collective-permute-done((f32[1,96,768]{2,1,0:T(8,128)S(1)}, f32[1,96,768]{2,1,0:T(8,128)S(1)}, u32[]{:S(2)}, u32[]{:S(2)}) %collective-permute-start.13) | collective-permute-done | bytes 294944 | tf_op jit(solution)/shard_map/ppermute | solution.py:309
  152.4 0.8 pad_maximum_fusion.9.rim_z
  153.3 24.5 %shard_map.71 = f32[16,96,768]{2,1,0:T(8,128)} custom-call(f32[16,6]{1,0:T(8,128)} %stack.27.par, f32[16,96,768]{2,1,0:T(8,128)} %get-tuple-element.25.rho, f32[2,96,768]{2,1,0:T(8,128)} %pad_maximum_fusion.5.rho_z, f32[16,2,768]{2,1,0:T(2,128)} %pad_maximum_fusion.15.rho_y, bf16[6,16,96,768]{3,2,1,0:T(8,128)(2,1)} %tensor.3, bf16[3,16,96,768]{3,2,1,0:T(8,128)(2,1)} %grad.3, ...), custom_call_target="tpu_custom_call" | custom-call | flops 94371840 | bytes 37748736 | tf_op jit(solution)/shard_map/pallas_call | solution.py:433
  177.8 4.4 %all-to-all-done.1.in_ref = f32[8,4,96,384]{3,2,1,0:T(8,128)} async-done(((f32[8,4,96,384]{3,2,1,0:T(8,128)}), f32[8,4,96,384]{3,2,1,0:T(8,128)}, u32[]{:S(2)}, u32[]{:S(2)}) %all-to-all-start.1) | async-done | bytes 4718624 | tf_op jit(solution)/shard_map/all_to_all | solution.py:494
  182.2 10.5 %shard_map.72 = f32[16,96,768]{2,1,0:T(8,128)} custom-call(f32[16,6]{1,0:T(8,128)} %stack.27.par, f32[8,4,96,384]{3,2,1,0:T(8,128)} %all-to-all-done.1.in_ref), custom_call_target="tpu_custom_call" | custom-call | flops 3623878656 | bytes 9437184 | tf_op jit(solution)/shard_map/pallas_call | solution.py:477
  (55 shorter events, 2.1 us)
Async XLA Ops:
  0.6 16.6 %copy-start.4 = (f32[16]{0:T(128)S(1)}, f32[16]{0:T(128)}, u32[]{:S(2)}) copy-start(f32[16]{0:T(128)} %param.8) | copy-start | bytes 196
  6.4 22.4 %collective-permute-start = (f32[16,8,768]{2,1,0:T(8,128)S(1)}, f32[16,8,768]{2,1,0:T(8,128)S(1)}, u32[]{:S(2)}, u32[]{:S(2)}) collective-permute-start(f32[16,8,768]{2,1,0:T(8,128)S(1)} %concatenate.280), channel_id=1, source_target_pairs={{0,4},{4,8},{8,12},{12,16},{16,20},{20,24},{24,28},{28,0},{1,5},{5... | collective-permute-start | bytes 1179656 | tf_op jit(solution)/shard_map/ppermute | solution.py:309
  7.5 21.3 %collective-permute-start.1 = (f32[16,8,768]{2,1,0:T(8,128)S(1)}, f32[16,8,768]{2,1,0:T(8,128)S(1)}, u32[]{:S(2)}, u32[]{:S(2)}) collective-permute-start(f32[16,8,768]{2,1,0:T(8,128)S(1)} %concatenate.281), channel_id=1, source_target_pairs={{4,0},{8,4},{12,8},{16,12},{20,16},{24,20},{28,24},{0,28},{5,1},{9... | collective-permute-start | bytes 1179656 | tf_op jit(solution)/shard_map/ppermute | solution.py:309
  11.7 17.1 %collective-permute-start.2 = (f32[1,96,768]{2,1,0:T(8,128)S(1)}, f32[1,96,768]{2,1,0:T(8,128)S(1)}, u32[]{:S(2)}, u32[]{:S(2)}) collective-permute-start(f32[1,96,768]{2,1,0:T(8,128)S(1)} %get-tuple-element.71), channel_id=1, source_target_pairs={{0,1},{1,2},{2,3},{3,0},{4,5},{5,6},{6,7},{7,4},{8,9},{9,10},{10,1... | collective-permute-start | bytes 884744 | tf_op jit(solution)/shard_map/ppermute | solution.py:309
  14.1 14.7 %collective-permute-start.3 = (f32[1,96,768]{2,1,0:T(8,128)S(1)}, f32[1,96,768]{2,1,0:T(8,128)S(1)}, u32[]{:S(2)}, u32[]{:S(2)}) collective-permute-start(f32[1,96,768]{2,1,0:T(8,128)S(1)} %get-tuple-element.70), channel_id=1, source_target_pairs={{1,0},{2,1},{3,2},{0,3},{5,4},{6,5},{7,6},{4,7},{9,8},{10,9},{11,1... | collective-permute-start | bytes 884744 | tf_op jit(solution)/shard_map/ppermute | solution.py:309
  28.8 65.8 %all-to-all-start = ((f32[8,4,96,384]{3,2,1,0:T(8,128)}), f32[8,4,96,384]{3,2,1,0:T(8,128)}, u32[]{:S(2)}, u32[]{:S(2)}) async-start(f32[8,4,96,384]{3,2,1,0:T(8,128)} %shard_map.68), calls=%async_computation | async-start | bytes 9437184 | tf_op jit(solution)/shard_map/all_to_all | solution.py:494
  38.1 8.8 %collective-permute-start.6 = (f32[1,2,768]{2,1,0:T(2,128)S(1)}, f32[1,2,768]{2,1,0:T(2,128)S(1)}, u32[]{:S(2)}, u32[]{:S(2)}) collective-permute-start(f32[1,2,768]{2,1,0:T(2,128)S(1)} %get-tuple-element.118), channel_id=1, source_target_pairs={{1,0},{2,1},{3,2},{0,3},{5,4},{6,5},{7,6},{4,7},{9,8},{10,9},{11,1... | collective-permute-start | bytes 18440 | tf_op jit(solution)/shard_map/ppermute | solution.py:309
  40.1 6.8 %collective-permute-start.7 = (f32[1,2,768]{2,1,0:T(2,128)S(1)}, f32[1,2,768]{2,1,0:T(2,128)S(1)}, u32[]{:S(2)}, u32[]{:S(2)}) collective-permute-start(f32[1,2,768]{2,1,0:T(2,128)S(1)} %get-tuple-element.119), channel_id=1, source_target_pairs={{0,1},{1,2},{2,3},{3,0},{4,5},{5,6},{6,7},{7,4},{8,9},{9,10},{10,1... | collective-permute-start | bytes 18440 | tf_op jit(solution)/shard_map/ppermute | solution.py:309
  43.1 11.7 %collective-permute-start.4 = (f32[1,96,768]{2,1,0:T(8,128)S(1)}, f32[1,96,768]{2,1,0:T(8,128)S(1)}, u32[]{:S(2)}, u32[]{:S(2)}) collective-permute-start(f32[1,96,768]{2,1,0:T(8,128)S(1)} %get-tuple-element.80), channel_id=1, source_target_pairs={{0,1},{1,2},{2,3},{3,0},{4,5},{5,6},{6,7},{7,4},{8,9},{9,10},{10,1... | collective-permute-start | bytes 884744 | tf_op jit(solution)/shard_map/ppermute | solution.py:309
  43.4 14.9 %collective-permute-start.5 = (f32[1,96,768]{2,1,0:T(8,128)S(1)}, f32[1,96,768]{2,1,0:T(8,128)S(1)}, u32[]{:S(2)}, u32[]{:S(2)}) collective-permute-start(f32[1,96,768]{2,1,0:T(8,128)S(1)} %get-tuple-element.81), channel_id=1, source_target_pairs={{1,0},{2,1},{3,2},{0,3},{5,4},{6,5},{7,6},{4,7},{9,8},{10,9},{11,1... | collective-permute-start | bytes 884744 | tf_op jit(solution)/shard_map/ppermute | solution.py:309
  107.6 12.1 %collective-permute-start.10 = (f32[1,96,768]{2,1,0:T(8,128)S(1)}, f32[1,96,768]{2,1,0:T(8,128)S(1)}, u32[]{:S(2)}, u32[]{:S(2)}) collective-permute-start(f32[1,96,768]{2,1,0:T(8,128)S(1)} %get-tuple-element.63), channel_id=1, source_target_pairs={{0,1},{1,2},{2,3},{3,0},{4,5},{5,6},{6,7},{7,4},{8,9},{9,10},{10,1... | collective-permute-start | bytes 884744 | tf_op jit(solution)/shard_map/ppermute | solution.py:309
  110.0 13.7 %collective-permute-start.11 = (f32[1,96,768]{2,1,0:T(8,128)S(1)}, f32[1,96,768]{2,1,0:T(8,128)S(1)}, u32[]{:S(2)}, u32[]{:S(2)}) collective-permute-start(f32[1,96,768]{2,1,0:T(8,128)S(1)} %get-tuple-element.62), channel_id=1, source_target_pairs={{1,0},{2,1},{3,2},{0,3},{5,4},{6,5},{7,6},{4,7},{9,8},{10,9},{11,1... | collective-permute-start | bytes 884744 | tf_op jit(solution)/shard_map/ppermute | solution.py:309
  112.8 3.8 %collective-permute-start.9 = (f32[16,3,768]{2,1,0:T(4,128)S(1)}, f32[16,3,768]{2,1,0:T(4,128)S(1)}, u32[]{:S(2)}, u32[]{:S(2)}) collective-permute-start(f32[16,3,768]{2,1,0:T(4,128)S(1)} %pad_maximum_fusion.13), channel_id=1, source_target_pairs={{4,0},{8,4},{12,8},{16,12},{20,16},{24,20},{28,24},{0,28},{5,1},{9... | collective-permute-start | bytes 442376 | tf_op jit(solution)/shard_map/ppermute | solution.py:309
  113.5 6.2 %collective-permute-start.8 = (f32[16,3,768]{2,1,0:T(4,128)S(1)}, f32[16,3,768]{2,1,0:T(4,128)S(1)}, u32[]{:S(2)}, u32[]{:S(2)}) collective-permute-start(f32[16,3,768]{2,1,0:T(4,128)S(1)} %pad_maximum_fusion.12), channel_id=1, source_target_pairs={{0,4},{4,8},{8,12},{12,16},{16,20},{20,24},{24,28},{28,0},{1,5},{5... | collective-permute-start | bytes 442376 | tf_op jit(solution)/shard_map/ppermute | solution.py:309
  116.6 3.1 %copy-start = (f32[16,3,768]{2,1,0:T(4,128)}, f32[16,3,768]{2,1,0:T(4,128)S(1)}, u32[]{:S(2)}) copy-start(f32[16,3,768]{2,1,0:T(4,128)S(1)} %collective-permute-done.9) | copy-start | bytes 442372
  119.7 0.7 copy-start.2
  123.7 58.4 %all-to-all-start.1 = ((f32[8,4,96,384]{3,2,1,0:T(8,128)}), f32[8,4,96,384]{3,2,1,0:T(8,128)}, u32[]{:S(2)}, u32[]{:S(2)}) async-start(f32[8,4,96,384]{3,2,1,0:T(8,128)} %shard_map.69), calls=%async_computation.1 | async-start | bytes 9437184 | tf_op jit(solution)/shard_map/all_to_all | solution.py:494
  128.4 6.8 %copy-start.3 = (f32[16,3,768]{2,1,0:T(4,128)S(1)}, f32[16,3,768]{2,1,0:T(4,128)}, u32[]{:S(2)}) copy-start(f32[16,3,768]{2,1,0:T(4,128)} %copy-done.2) | copy-start | bytes 442372
  128.4 6.8 %copy-start.1 = (f32[16,3,768]{2,1,0:T(4,128)S(1)}, f32[16,3,768]{2,1,0:T(4,128)}, u32[]{:S(2)}) copy-start(f32[16,3,768]{2,1,0:T(4,128)} %copy-done) | copy-start | bytes 442372
  130.7 10.2 %collective-permute-start.14 = (f32[1,2,768]{2,1,0:T(2,128)S(1)}, f32[1,2,768]{2,1,0:T(2,128)S(1)}, u32[]{:S(2)}, u32[]{:S(2)}) collective-permute-start(f32[1,2,768]{2,1,0:T(2,128)S(1)} %get-tuple-element.116), channel_id=1, source_target_pairs={{1,0},{2,1},{3,2},{0,3},{5,4},{6,5},{7,6},{4,7},{9,8},{10,9},{11,1... | collective-permute-start | bytes 18440 | tf_op jit(solution)/shard_map/ppermute | solution.py:309
  134.2 6.7 %collective-permute-start.15 = (f32[1,2,768]{2,1,0:T(2,128)S(1)}, f32[1,2,768]{2,1,0:T(2,128)S(1)}, u32[]{:S(2)}, u32[]{:S(2)}) collective-permute-start(f32[1,2,768]{2,1,0:T(2,128)S(1)} %get-tuple-element.117), channel_id=1, source_target_pairs={{0,1},{1,2},{2,3},{3,0},{4,5},{5,6},{6,7},{7,4},{8,9},{9,10},{10,1... | collective-permute-start | bytes 18440 | tf_op jit(solution)/shard_map/ppermute | solution.py:309
  137.1 11.7 %collective-permute-start.12 = (f32[1,96,768]{2,1,0:T(8,128)S(1)}, f32[1,96,768]{2,1,0:T(8,128)S(1)}, u32[]{:S(2)}, u32[]{:S(2)}) collective-permute-start(f32[1,96,768]{2,1,0:T(8,128)S(1)} %get-tuple-element.74), channel_id=1, source_target_pairs={{0,1},{1,2},{2,3},{3,0},{4,5},{5,6},{6,7},{7,4},{8,9},{9,10},{10,1... | collective-permute-start | bytes 884744 | tf_op jit(solution)/shard_map/ppermute | solution.py:309
  137.1 15.3 %collective-permute-start.13 = (f32[1,96,768]{2,1,0:T(8,128)S(1)}, f32[1,96,768]{2,1,0:T(8,128)S(1)}, u32[]{:S(2)}, u32[]{:S(2)}) collective-permute-start(f32[1,96,768]{2,1,0:T(8,128)S(1)} %get-tuple-element.75), channel_id=1, source_target_pairs={{1,0},{2,1},{3,2},{0,3},{5,4},{6,5},{7,6},{4,7},{9,8},{10,9},{11,1... | collective-permute-start | bytes 884744 | tf_op jit(solution)/shard_map/ppermute | solution.py:309
